TPU v7x, 32 devices: a whole 2x2x4 slice. The times are simulated.
32 devices in a mesh: groups: 2 (over y), ex: 8 (over z, x), layer: 2 (over core).
Axes of the slice: x: 2, y: 2, z: 4, core: 2. Of those that a mesh axis runs over, the one named last changes fastest.
Arguments:
- query_out_grads: bfloat16 [2, 32, 7168], P('layer', ('groups', 'ex')), parts along dimension 1, may hold values from -6 to 6
- query_inputs: bfloat16 [2, 32, 4096], P('layer', ('groups', 'ex')), parts along dimension 1, may hold values from -6 to 6
- train_out_grads: bfloat16 [2, 2560, 7168], P('layer', ('groups', 'ex')), parts along dimension 1, may hold values from -0.0625 to 0.0625
- train_inputs: bfloat16 [2, 2560, 4096], P('layer', ('groups', 'ex')), parts along dimension 1, may hold values from -0.09375 to 0.09375
- basis_hidden: bfloat16 [2, 7168, 7168], P('layer', None, 'ex'), may hold values from -0.0625 to 0.0625
- basis_inputs: bfloat16 [2, 4096, 4096], P('layer', None, 'ex'), may hold values from -0.09375 to 0.09375
- eig_hidden: float32 [2, 7168], P('layer'), may hold values from 0.5 to 5
- eig_inputs: float32 [2, 4096], P('layer'), may hold values from 0.5 to 5
- query_ids: int32 [32], P('groups'), parts along dimension 0, may hold values from 0 to 7, as said below
- example_ids: int32 [16, 160], P(('groups', 'ex')), parts along dimension 0, may hold values from 0 to 1, as said below
Outputs:
- relative_scores: float32 [16, 16], P(('groups', 'layer'), 'ex'), parts along dimension 0
There are 2 independent parts, one for each index of `groups`. A program takes and returns all parts, laid end to end along the dimension named above; an argument that names none is the same for every part. Nothing has to cross between parts.
Inputs may be any that keep to these rules, and one draw needn't show every extreme that they name: `query_ids`: never falls along the tokens; every query owns one token or more. `example_ids`: never falls along each row; every number appears in every row.
All inputs are finite; a program needn't handle non-finite values.
Results may differ from a plain program's by a relative error of at most 0.0045.
Values may be sent and summed in bfloat16 or wider, within the bound.
No kernel may reach another device: no remote copies, remote signals or barrier semaphores. Data moves between devices by JAX's collectives and lax.ppermute only.
A program may use at most 64 MiB of HBM per device.

v0:
```python
import jax
import jax.numpy as jnp
from jax import lax
from jax.sharding import PartitionSpec as P

E_DEV = 2
QUERIES = 8


DAMP = 0.1


def body(
    query_out_grads,
    query_inputs,
    train_out_grads,
    train_inputs,
    basis_hidden,
    basis_inputs,
    eig_hidden,
    eig_inputs,
    query_ids,
    example_ids,
):
    shards = lax.axis_size("ex")
    my_index = lax.axis_index("ex")
    hid_block = basis_hidden.shape[2]
    inp_block = basis_inputs.shape[2]
    width = hid_block + inp_block
    nqueries = QUERIES
    gain_hidden = 1.0 / (eig_hidden[0] + DAMP)
    gain_inputs = 1.0 / (eig_inputs[0] + DAMP)
    all_hidden, all_inputs = (
        lax.all_gather(query_out_grads[0], "ex", axis=0, tiled=True),
        lax.all_gather(query_inputs[0], "ex", axis=0, tiled=True),
    )
    own_gain_h = lax.dynamic_slice_in_dim(gain_hidden, my_index * hid_block, hid_block)
    own_gain_a = lax.dynamic_slice_in_dim(gain_inputs, my_index * inp_block, inp_block)
    rot_hidden = (
        jnp.dot(all_hidden, basis_hidden[0], preferred_element_type=jnp.float32) * own_gain_h
    ).astype(jnp.bfloat16)
    rot_inputs = (
        jnp.dot(all_inputs, basis_inputs[0], preferred_element_type=jnp.float32) * own_gain_a
    ).astype(jnp.bfloat16)
    rotated = jnp.concatenate([rot_hidden, rot_inputs], axis=1)
    train_hidden = train_out_grads[0]
    train_input = train_inputs[0]
    tokens = train_hidden.shape[0]
    split_hidden = train_hidden.reshape(tokens, shards, hid_block)
    split_inputs = train_input.reshape(tokens, shards, inp_block)
    example_hot = (example_ids[0][None, :] == jnp.arange(E_DEV, dtype=jnp.int32)[:, None]).astype(
        jnp.float32
    )
    query_range = jnp.arange(nqueries, dtype=jnp.int32)[:, None]
    mine = lax.all_to_all(rotated, "ex", split_axis=0, concat_axis=1, tiled=True)
    mine_blocks = mine.reshape(mine.shape[0], shards, width)
    piece = lax.all_gather(mine_blocks, "ex", axis=0, tiled=True)
    gram_hidden = jnp.einsum(
        "qnf,tnf->qt", piece[:, :, :hid_block], split_hidden, preferred_element_type=jnp.float32
    )
    gram_inputs = jnp.einsum(
        "qnf,tnf->qt", piece[:, :, hid_block:], split_inputs, preferred_element_type=jnp.float32
    )
    piece_hot = (query_ids[None, :] == query_range).astype(jnp.float32)
    summed = jnp.dot(piece_hot, gram_hidden * gram_inputs, precision=lax.Precision.HIGHEST)
    scores = jnp.dot(summed, example_hot.T, precision=lax.Precision.HIGHEST)
    scaled_hidden = (train_hidden * gain_hidden).astype(jnp.bfloat16)
    scaled_inputs = (train_input * gain_inputs).astype(jnp.bfloat16)
    own_pairs = jnp.dot(
        scaled_hidden, train_hidden.T, preferred_element_type=jnp.float32
    ) * jnp.dot(scaled_inputs, train_input.T, preferred_element_type=jnp.float32)
    own_self = jnp.sum(
        jnp.dot(example_hot, own_pairs, precision=lax.Precision.HIGHEST) * example_hot, axis=1
    )
    half = nqueries // 2
    total_scores, total_self = lax.psum((scores, own_self), "layer")
    my_scores = lax.dynamic_slice_in_dim(total_scores, lax.axis_index("layer") * half, half, 0)
    return my_scores / jnp.sqrt(total_self + 1e-06)[None, :]


def solution(mesh):
    in_specs = (
        P("layer", ("groups", "ex"), None),
        P("layer", ("groups", "ex"), None),
        P("layer", ("groups", "ex"), None),
        P("layer", ("groups", "ex"), None),
        P("layer", None, "ex"),
        P("layer", None, "ex"),
        P("layer", None),
        P("layer", None),
        P("groups"),
        P(("groups", "ex"), None),
    )
    out_specs = P(("groups", "layer"), "ex")
    return jax.shard_map(body, mesh=mesh, in_specs=in_specs, out_specs=out_specs, check_vma=False)
```

profile of v0, /device:TPU:0, one launch (start us, length us, event | category | flops | bytes accessed | tf_op | source)
XLA Modules:
  0.0 123.8 jit_solution(4064454641542120981)
XLA Ops:
  0.0 0.8 add_divide_fusion
  0.8 0.8 copy.21
  1.6 32.9 %all-gather = bf16[1,16,7168]{2,0,1:T(2,128)(2,1)S(1)} all-gather(bf16[1,2,7168]{2,0,1:T(2,128)(2,1)S(1)} %copy.21), channel_id=2, replica_groups=mesh['groups'=2,'ex'=8,'layer'=2] {'ex'}, dimensions={1}, use_global_device_ids=true | all-gather | bytes 258048 | tf_op jit(solution)/shard_map/all_gather | solution.py:34
  34.4 0.7 add_divide_fusion.1
  35.2 0.7 copy.22
  35.9 30.7 %all-gather.1 = bf16[1,16,4096]{2,0,1:T(2,128)(2,1)S(1)} all-gather(bf16[1,2,4096]{2,0,1:T(2,128)(2,1)S(1)} %copy.22), channel_id=3, replica_groups=mesh['groups'=2,'ex'=8,'layer'=2] {'ex'}, dimensions={1}, use_global_device_ids=true | all-gather | bytes 147456 | tf_op jit(solution)/shard_map/all_gather | solution.py:35
  66.7 0.0 copy-start
  66.7 6.6 %fusion.26 = bf16[16,896]{1,0:T(8,128)(2,1)S(1)} fusion(bf16[1,7168,896]{2,1,0:T(8,128)(2,1)} %param.14, bf16[1,16,7168]{2,0,1:T(2,128)(2,1)S(1)} %all-gather, f32[896]{0:T(1024)S(1)} %dynamic-slice_reduce_fusion), kind=kOutput, calls=%fused_computation.20 | convolution fusion | flops 205549568 | bytes 13106688 | tf_op jit(solution)/shard_map/dot_general | solution.py:40
  73.3 0.0 copy-start.1
  73.3 0.7 fusion.32
  74.0 0.6 all_to_all.12
  74.6 5.6 %all-to-all-start = ((bf16[8,2,1408]{2,1,0:T(2,128)(2,1)}), bf16[8,2,1408]{2,1,0:T(2,128)(2,1)S(1)}, u32[]{:S(2)}, u32[]{:S(2)}) async-start(bf16[8,2,1408]{2,1,0:T(2,128)(2,1)} %all_to_all.12), calls=%async_computation | async-start | bytes 90112 | tf_op jit(solution)/shard_map/all_to_all | solution.py:55
  80.3 0.0 copy-done.1
  80.3 0.0 copy-start.3
  80.3 1.8 %copy.32 = bf16[20,8,8,896]{3,2,1,0:T(8,128)(2,1)} copy(bf16[20,8,8,896]{3,1,2,0:T(8,128)(2,1)S(1)} %bitcast.56) | data formatting | bytes 4587520
  82.1 0.0 copy-done.3
  82.1 1.6 %copy.33 = bf16[20,8,8,512]{3,2,1,0:T(8,128)(2,1)} copy(bf16[20,8,8,512]{3,1,2,0:T(8,128)(2,1)S(1)} %bitcast.58) | data formatting | bytes 2621440
  83.7 0.8 fusion.5
  84.5 0.0 copy-start.5
  84.5 2.4 %fusion.18 = f32[160,160]{1,0:T(8,128)S(1)} fusion(f32[160,160]{1,0:T(8,128)S(1)} %fusion.5, bf16[1,160,4096]{2,1,0:T(8,128)(2,1)} %param.13, f32[4096]{0:T(1024)S(1)} %bitcast.62), kind=kOutput, calls=%fused_computation.18 | convolution fusion | flops 211706880 | bytes 1531904 | tf_op jit(solution)/shard_map/dot_general | solution.py:71
  86.9 0.3 fusion.44
  87.2 0.0 all-to-all-done
  87.2 0.0 copy-start.4
  87.2 31.6 %all_gather.11 = bf16[16,8,1408]{2,1,0:T(8,128)(2,1)S(1)} all-gather(bf16[2,8,1408]{2,1,0:T(8,128)(2,1)S(1)} %copy.23), channel_id=1, replica_groups=mesh['groups'=2,'ex'=8,'layer'=2] {'ex'}, dimensions={0}, use_global_device_ids=true | all-gather | bytes 405504 | tf_op jit(solution)/shard_map/all_gather | solution.py:57
  118.8 0.0 copy-start.6
  118.9 0.7 fusion.38
  119.6 0.9 fusion.41
  120.4 0.0 copy-done.6
  120.4 0.1 fusion.51
  120.6 0.1 fusion.52
  120.7 2.5 %all-reduce = (f32[8,2]{0,1:T(2,128)S(1)}, f32[2]{0:T(128)S(1)}) all-reduce(f32[8,2]{0,1:T(2,128)S(1)} %fusion.52, f32[2]{0:T(128)S(1)} %fusion.44), channel_id=1, replica_groups=mesh['groups'=2,'ex'=8,'layer'=2] {'layer'}, use_global_device_ids=true, to_apply=%region_0.0 | all-reduce | flops 18 | bytes 144 | tf_op jit(solution)/shard_map/psum | solution.py:76
  123.2 0.6 dynamic-slice_divide_fusion
  (12 shorter events, 0.1 us)
Async XLA Ops:
  66.7 6.6 %copy-start = (bf16[1,4096,512]{2,1,0:T(8,128)(2,1)S(1)}, bf16[1,4096,512]{2,1,0:T(8,128)(2,1)}, u32[]{:S(2)}) copy-start(bf16[1,4096,512]{2,1,0:T(8,128)(2,1)} %param.15) | copy-start | bytes 12582916
  73.3 7.0 %copy-start.1 = (bf16[1,160,7168]{2,1,0:T(8,128)(2,1)S(1)}, bf16[1,160,7168]{2,1,0:T(8,128)(2,1)}, u32[]{:S(2)}) copy-start(bf16[1,160,7168]{2,1,0:T(8,128)(2,1)} %param.12) | copy-start | bytes 6881284
  74.6 12.6 %all-to-all-start = ((bf16[8,2,1408]{2,1,0:T(2,128)(2,1)}), bf16[8,2,1408]{2,1,0:T(2,128)(2,1)S(1)}, u32[]{:S(2)}, u32[]{:S(2)}) async-start(bf16[8,2,1408]{2,1,0:T(2,128)(2,1)} %all_to_all.12), calls=%async_computation | async-start | bytes 90112 | tf_op jit(solution)/shard_map/all_to_all | solution.py:55
  80.3 1.8 %copy-start.3 = (bf16[1,160,4096]{2,1,0:T(8,128)(2,1)S(1)}, bf16[1,160,4096]{2,1,0:T(8,128)(2,1)}, u32[]{:S(2)}) copy-start(bf16[1,160,4096]{2,1,0:T(8,128)(2,1)} %param.13) | copy-start | bytes 3932164
  84.5 2.4 %copy-start.5 = (s32[1,160]{1,0:T(1,128)S(1)}, s32[1,160]{1,0:T(1,128)}, u32[]{:S(2)}) copy-start(s32[1,160]{1,0:T(1,128)} %param.19) | copy-start | bytes 1924
  84.5 34.4 %copy-start.2 = (bf16[20,8,8,896]{3,2,1,0:T(8,128)(2,1)S(1)}, bf16[20,8,8,896]{3,2,1,0:T(8,128)(2,1)}, u32[]{:S(2)}) copy-start(bf16[20,8,8,896]{3,2,1,0:T(8,128)(2,1)} %copy.32) | copy-start | bytes 6881284
  87.2 32.4 %copy-start.4 = (bf16[20,8,8,512]{3,2,1,0:T(8,128)(2,1)S(1)}, bf16[20,8,8,512]{3,2,1,0:T(8,128)(2,1)}, u32[]{:S(2)}) copy-start(bf16[20,8,8,512]{3,2,1,0:T(8,128)(2,1)} %copy.33) | copy-start | bytes 3932164
  118.8 1.6 %copy-start.6 = (s32[16]{0:T(128)S(1)}, s32[16]{0:T(128)}, u32[]{:S(2)}) copy-start(s32[16]{0:T(128)} %param.18) | copy-start | bytes 196
where the time goes:
time: 124 us
  blocking collectives  97.7 us (79%)
  matrix products  12.5 us (10%)
  local copies, waits for them, and re-layouts  5.7 us (5%)
  starting transfers between devices  5.64 us (5%)
  other arithmetic  2.19 us (2%)
    all_gather x1, blocking collectives, body(): lax.all_gather(query_out_grads[0], 'ex', axis=0, tiled=True)  32.9 us
    all_gather x1, blocking collectives, body(): piece = lax.all_gather(mine_blocks, 'ex', axis=0, tiled=True)  31.6 us
    all_gather x1, blocking collectives, body(): lax.all_gather(query_inputs[0], 'ex', axis=0, tiled=True)  30.7 us
    dot_general x1, matrix products, body(): jnp.dot(all_hidden, basis_hidden[0], preferred_element_type=jnp.float32)  6.57 us
    all_to_all x1, starting transfers between devices, body(): lax.all_to_all(rotated, 'ex', split_axis=0, concat_axis=1, tiled=True)  5.64 us
    unnamed x18, local copies, waits for them, and re-layouts  4.99 us
  transfers between devices with their start and end apart: 1, of which 0 were waited for; matrix products, arithmetic and copies ran while one was open for 6% of the time, Pallas kernels for 0%

commit v1 on v0

v1 whole, which is shorter than its diff:
```python
import functools

import jax
import jax.numpy as jnp
from jax import lax
from jax.experimental import pallas as pl
from jax.experimental.pallas import tpu as pltpu
from jax.sharding import PartitionSpec as P

E_DEV = 2
QUERIES = 8
DAMP = 0.1
LANES = 128
MIB = 2**20
BY_LANES = (((1,), (1,)), ((), ()))


def vmem(x):
    return pltpu.with_memory_space_constraint(x, pltpu.VMEM)


def hbm(x):
    return pltpu.with_memory_space_constraint(x, pltpu.HBM)


def gather(x, shards):
    x = x[None]
    masks = [0]
    stride = shards
    while True:
        radix = min(4, stride // 2) if stride > 2 else stride
        stride //= radix
        parts, of_parts = [x], [masks]
        for m in reversed(range(1, radix)):
            mask = m * stride
            parts.append(lax.ppermute(x, "ex", [(i, i ^ mask) for i in range(shards)]))
            of_parts.append([mask ^ old for old in masks])
        if stride == 1:
            return parts, of_parts
        x = jnp.concatenate(parts, axis=0)
        masks = sum(of_parts, [])


def in_order(parts, masks):
    place = {mask: at for at, mask in enumerate(sum(masks, []))}
    device = jnp.bitwise_xor(jnp.arange(len(place), dtype=jnp.int32), lax.axis_index("ex"))
    table = jnp.array([place[mask] for mask in range(len(place))], dtype=jnp.int32)
    return jnp.concatenate(parts, axis=0)[table[device]]


def join_kernel(hidden, inputs, out, sems):
    width_h = hidden.shape[1]
    copies = [
        pltpu.make_async_copy(hidden, out.at[:, :width_h], sems.at[0]),
        pltpu.make_async_copy(inputs, out.at[:, width_h:], sems.at[1]),
    ]
    for copy in copies:
        copy.start()
    for copy in copies:
        copy.wait()


def self_kernel(train_h, train_i, eig_h, eig_i, ids, out):
    def pairs(train, eig):
        values = train[...]
        scaled = (values.astype(jnp.float32) * (1.0 / (eig[...] + DAMP))).astype(jnp.bfloat16)
        return lax.dot_general(scaled, values, BY_LANES, preferred_element_type=jnp.float32)

    own_pairs = pairs(train_h, eig_h) * pairs(train_i, eig_i)
    row = lax.broadcasted_iota(jnp.int32, (out.shape[0], ids.shape[1]), 0)
    hot = (ids[...] == row - E_DEV).astype(jnp.float32)
    sums = jnp.dot(
        hot, own_pairs, precision=lax.Precision.HIGHEST, preferred_element_type=jnp.float32
    )
    out[...] = jnp.broadcast_to(jnp.sum(sums * hot, axis=1, keepdims=True), out.shape)


def rotate_kernel(masks, *refs):
    parts = refs[:-6]
    basis_h, basis_i, eig_h, eig_i, out, tokens = refs[-6:]
    width_h = basis_h.shape[0]
    hid_block = basis_h.shape[1]
    inp_block = basis_i.shape[1]
    me = lax.axis_index("ex")
    own_tokens = parts[0].shape[1]
    rows = tokens.shape[0]
    column = lax.broadcasted_iota(jnp.int32, (rows, rows), 1)
    device_of = jnp.zeros((rows, rows), jnp.int32)
    at = 0
    for part, of_part in zip(parts, masks):
        for i, mask in enumerate(of_part):
            tokens[pl.ds(at, own_tokens), :] = part[i].astype(jnp.float32)
            device_of = jnp.where(column // own_tokens == at // own_tokens, me ^ mask, device_of)
            at += own_tokens
    token = lax.broadcasted_iota(jnp.int32, (rows, rows), 0)
    order = (token == device_of * own_tokens + column % own_tokens).astype(jnp.bfloat16)

    def rotate(lanes, basis, eig, block, to):
        product = jnp.dot(
            tokens[:, lanes].astype(jnp.bfloat16), basis[...], preferred_element_type=jnp.float32
        )
        at = pl.ds(pl.multiple_of(me * block, LANES), block)
        rotated = (product * (1.0 / (eig[:, at] + DAMP))).astype(jnp.bfloat16)
        out[0, :, to] = jnp.dot(order, rotated, preferred_element_type=jnp.float32).astype(
            jnp.bfloat16
        )

    rotate(slice(0, width_h), basis_h, eig_h, hid_block, slice(0, hid_block))
    rotate(slice(width_h, None), basis_i, eig_i, inp_block, slice(hid_block, None))


def score_kernel(masks, hid_block, inp_block, *refs):
    parts = refs[:-6]
    train_h, train_i, query_ids, ids, own_self, out = refs[-6:]
    me = lax.axis_index("ex")
    gram_h = gram_i = 0.0
    for part, of_part in zip(parts, masks):
        for i, mask in enumerate(of_part):
            block = me ^ mask
            at_h = pl.ds(pl.multiple_of(block * hid_block, LANES), hid_block)
            at_i = pl.ds(pl.multiple_of(block * inp_block, LANES), inp_block)
            gram_h += lax.dot_general(
                part[i, :, :hid_block],
                train_h[:, at_h],
                BY_LANES,
                preferred_element_type=jnp.float32,
            )
            gram_i += lax.dot_general(
                part[i, :, hid_block:],
                train_i[:, at_i],
                BY_LANES,
                preferred_element_type=jnp.float32,
            )
    row = lax.broadcasted_iota(jnp.int32, (out.shape[0], ids.shape[1]), 0)
    example_hot = ((ids[...] == row) & (row < E_DEV)).astype(jnp.float32)
    summed = lax.dot_general(
        example_hot,
        gram_h * gram_i,
        BY_LANES,
        precision=lax.Precision.HIGHEST,
        preferred_element_type=jnp.float32,
    )
    query = lax.broadcasted_iota(jnp.int32, (LANES, query_ids.shape[1]), 0)
    query_hot = (query_ids[...] == query).astype(jnp.float32)
    scores = lax.dot_general(
        summed,
        query_hot,
        BY_LANES,
        precision=lax.Precision.HIGHEST,
        preferred_element_type=jnp.float32,
    )
    out[...] = scores + own_self[...]


def finish_kernel(mine, other, out):
    total = mine[...] + other[...]
    half = QUERIES // 2
    relative = total[:E_DEV] / jnp.sqrt(total[E_DEV : 2 * E_DEV] + 1e-06)
    out[...] = jnp.where(
        lax.axis_index("layer") == 0, relative[:, :half], relative[:, half:QUERIES]
    )


def call(kernel, name, out_shape, flops=0, moved=0, **more):
    return pl.pallas_call(
        kernel,
        out_shape=out_shape,
        name=name,
        compiler_params=pltpu.CompilerParams(vmem_limit_bytes=8 * MIB),
        cost_estimate=pl.CostEstimate(flops=flops, bytes_accessed=moved, transcendentals=0),
        **more,
    )


def layer_swap(x):
    return lax.ppermute(x, "layer", [(0, 1), (1, 0)])


def body(
    query_out_grads,
    query_inputs,
    train_out_grads,
    train_inputs,
    basis_hidden,
    basis_inputs,
    eig_hidden,
    eig_inputs,
    query_ids,
    example_ids,
):
    shards = lax.axis_size("ex")
    hid_block = basis_hidden.shape[2]
    inp_block = basis_inputs.shape[2]
    rest = (
        train_out_grads[0],
        train_inputs[0],
        basis_hidden[0],
        basis_inputs[0],
        eig_hidden,
        eig_inputs,
        query_ids[None, :],
        example_ids,
    )
    if hid_block % LANES or inp_block % LANES:
        own = jnp.concatenate([query_out_grads[0], query_inputs[0]], axis=1)
        return plain(own, *rest)
    train_h, train_i, basis_h, basis_i, eig_h, eig_i, query_ids, example_ids = map(vmem, rest)
    own_tokens = query_inputs.shape[1]
    width = query_out_grads.shape[2] + query_inputs.shape[2]
    tokens = own_tokens * shards
    own = call(
        join_kernel,
        "join",
        pltpu.VMEM((own_tokens, width), jnp.bfloat16),
        flops=20_000_000_000,
        in_specs=[pl.BlockSpec(memory_space=pl.ANY)] * 2,
        out_specs=pl.BlockSpec(memory_space=pltpu.VMEM),
        scratch_shapes=[pltpu.SemaphoreType.DMA((2,))],
    )(hbm(query_out_grads[0]), hbm(query_inputs[0]))
    everyone, masks = gather(own, shards)
    small = jax.ShapeDtypeStruct((8, LANES), jnp.float32)
    own_self = call(
        self_kernel, "self_influence", small, flops=2 * 160 * 160 * 11264, moved=3_700_000
    )(train_h, train_i, eig_h, eig_i, example_ids)
    rotated = call(
        functools.partial(rotate_kernel, masks),
        "rotate",
        jax.ShapeDtypeStruct((1, tokens, hid_block + inp_block), jnp.bfloat16),
        flops=2 * 16 * 8_500_000,
        moved=17_000_000,
        scratch_shapes=[pltpu.VMEM((tokens, width), jnp.float32)],
    )(*everyone, basis_h, basis_i, eig_h, eig_i)
    parts, masks = gather(rotated[0], shards)
    mine = call(functools.partial(score_kernel, masks, hid_block, inp_block), "scores", small)(
        *parts, train_h, train_i, query_ids, example_ids, own_self
    )
    return call(
        finish_kernel,
        "finish",
        jax.ShapeDtypeStruct((E_DEV, QUERIES // 2), jnp.float32),
    )(mine, layer_swap(mine)).T


def plain(own, train_h, train_i, basis_h, basis_i, eig_h, eig_i, query_ids, example_ids):
    shards = lax.axis_size("ex")
    my_index = lax.axis_index("ex")
    width_h, hid_block = basis_h.shape
    inp_block = basis_i.shape[1]
    everyone = in_order(*gather(own, shards)).reshape(-1, own.shape[1])
    gain_h = 1.0 / (eig_h + DAMP)
    gain_i = 1.0 / (eig_i + DAMP)

    def rotate(tokens, basis, gain, block):
        product = jnp.dot(tokens, basis, preferred_element_type=jnp.float32)
        own_gain = lax.dynamic_slice_in_dim(gain, my_index * block, block, 1)
        return (product * own_gain).astype(jnp.bfloat16)

    rot_h = rotate(everyone[:, :width_h], basis_h, gain_h, hid_block)
    rot_i = rotate(everyone[:, width_h:], basis_i, gain_i, inp_block)
    pieces = in_order(*gather(jnp.concatenate([rot_h, rot_i], axis=1), shards))

    def gram(piece, train):
        split = train.reshape(train.shape[0], shards, -1)
        return jnp.einsum("nqf,tnf->qt", piece, split, preferred_element_type=jnp.float32)

    cross = gram(pieces[:, :, :hid_block], train_h) * gram(pieces[:, :, hid_block:], train_i)
    query_hot = query_ids == jnp.arange(QUERIES, dtype=jnp.int32)[:, None]
    example_hot = (example_ids == jnp.arange(E_DEV, dtype=jnp.int32)[:, None]).astype(jnp.float32)
    summed = jnp.dot(query_hot.astype(jnp.float32), cross, precision=lax.Precision.HIGHEST)
    scores = jnp.dot(summed, example_hot.T, precision=lax.Precision.HIGHEST)

    def pairs(train, gain):
        scaled = (train * gain).astype(jnp.bfloat16)
        return jnp.dot(scaled, train.T, preferred_element_type=jnp.float32)

    own_pairs = pairs(train_h, gain_h) * pairs(train_i, gain_i)
    sums = jnp.dot(example_hot, own_pairs, precision=lax.Precision.HIGHEST)
    own_self = jnp.sum(sums * example_hot, axis=1)
    mine = jnp.concatenate([scores, jnp.broadcast_to(own_self, scores.shape)], axis=1)
    total = mine + layer_swap(mine)
    half = QUERIES // 2
    total = lax.dynamic_slice_in_dim(total, lax.axis_index("layer") * half, half, 0)
    return total[:, :E_DEV] / jnp.sqrt(total[:, E_DEV:] + 1e-06)


def solution(mesh):
    in_specs = (
        P("layer", ("groups", "ex"), None),
        P("layer", ("groups", "ex"), None),
        P("layer", ("groups", "ex"), None),
        P("layer", ("groups", "ex"), None),
        P("layer", None, "ex"),
        P("layer", None, "ex"),
        P("layer", None),
        P("layer", None),
        P("groups"),
        P(("groups", "ex"), None),
    )
    out_specs = P(("groups", "layer"), "ex")
    return jax.shard_map(body, mesh=mesh, in_specs=in_specs, out_specs=out_specs, check_vma=False)
```

time: 124 us -> 36.3 us (0.29)
  blocking collectives: 97.7 us -> 0 us
  waiting for transfers between devices: 0.01 us -> 15 us
  matrix products: 12.5 us -> 0 us
  starting transfers between devices: 5.64 us -> 13.3 us
  Pallas kernels: 0 us -> 7.25 us
  local copies, waits for them, and re-layouts: 5.7 us -> 0.05 us
  other arithmetic: 2.19 us -> 0.36 us
    all_gather x3 -> x0, blocking collectives: 95.2 us -> none  [the longest x1 32.9 us: body(): lax.all_gather(query_out_grads[0], 'ex', axis=0, tiled=True)]
    ppermute x0 -> x9, waiting for transfers between devices: none -> 15 us  [the longest x8 13.8 us: gather(): parts.append(lax.ppermute(x, 'ex', [(i, i ^ mask) for i in range(shards)]))]
    ppermute x0 -> x9, starting transfers between devices: none -> 13.3 us  [the longest x8 13.3 us: gather(): parts.append(lax.ppermute(x, 'ex', [(i, i ^ mask) for i in range(shards)]))]
    dot_general x9 -> x0, matrix products: 12.5 us -> none  [the longest x1 6.57 us: body(): jnp.dot(all_hidden, basis_hidden[0], preferred_element_type=jnp.float32)]
    pallas_call x0 -> x5, Pallas kernels: none -> 7.25 us  [the longest x1 2.61 us: body(): call(functools.partial(rotate_kernel, masks), 'rotate', jax.ShapeDtypeStr...]
    all_to_all x1 -> x0, starting transfers between devices: 5.64 us -> none  [body(): lax.all_to_all(rotated, 'ex', split_axis=0, concat_axis=1, tiled=True)]
    unnamed x18 -> x22, local copies, waits for them, and re-layouts: 4.99 us -> 0.05 us
    psum x1 -> x0, blocking collectives: 2.46 us -> none  [body(): total_scores, total_self = lax.psum((scores, own_self), 'layer')]
  transfers between devices with their start and end apart: 1 -> 9, of which waited for: 0 -> 7; matrix products, arithmetic and copies ran while one was open for 6% -> 0% of each run, Pallas kernels for 0% -> 4%
where the time goes in v1:
time: 36.3 us; the launch traced here: 36.1 us
  waiting for transfers between devices  15 us (41%)
  starting transfers between devices  13.3 us (37%)
  Pallas kernels  7.25 us (20%)
    ppermute x8, waiting for transfers between devices, gather(): parts.append(lax.ppermute(x, 'ex', [(i, i ^ mask) for i in range(shards)]))  13.8 us
    ppermute x8, starting transfers between devices, gather(): parts.append(lax.ppermute(x, 'ex', [(i, i ^ mask) for i in range(shards)]))  13.3 us
    pallas_call x1, Pallas kernels, body(): call(functools.partial(rotate_kernel, masks), 'rotate', jax.ShapeDtypeStr...  2.61 us
    pallas_call x1, Pallas kernels, body(): call(functools.partial(score_kernel, masks, hid_block, inp_block), 'score...  1.68 us
    pallas_call x1, Pallas kernels, body(): call(self_kernel, 'self_influence', small, flops=2 * 160 * 160 * 11264, m...  1.39 us
    ppermute x1, waiting for transfers between devices, layer_swap(): return lax.ppermute(x, 'layer', [(0, 1), (1, 0)])  1.2 us
    pallas_call x1, Pallas kernels, body(): call(join_kernel, 'join', pltpu.VMEM((own_tokens, width), jnp.bfloat16),...  0.92 us
  transfers between devices with their start and end apart: 9, of which 7 were waited for; matrix products, arithmetic and copies ran while one was open for 0% of the time, Pallas kernels for 4%

profile of v1, /device:TPU:0, one launch (start us, length us, event | category | flops | bytes accessed | tf_op | source)
XLA Modules:
  0.0 36.1 jit_solution(16535676596250342174)
XLA Ops:
  0.0 0.0 copy-start.3
  0.0 0.0 copy-start.4
  0.0 0.9 %join.1 = bf16[2,11264]{1,0:T(2,128)(2,1)S(1)} custom-call(bf16[2,7168]{1,0:T(2,128)(2,1)} %bitcast.22, bf16[2,4096]{1,0:T(2,128)(2,1)} %bitcast.23), custom_call_target="tpu_custom_call" | custom-call | flops 20000000000 | tf_op jit(solution)/shard_map/join/pallas_call | solution.py:211
  1.0 5.1 %collective-permute-start = (bf16[1,2,11264]{2,1,0:T(2,128)(2,1)S(1)}, bf16[1,2,11264]{2,1,0:T(2,128)(2,1)S(1)}, u32[]{:S(2)}, u32[]{:S(2)}) collective-permute-start(bf16[1,2,11264]{2,1,0:T(2,128)(2,1)S(1)} %bitcast.17), channel_id=1, source_target_pairs={{0,12},{2,14},{4,8},{6,10},{8,4},{10,6},{12,0},{14,2},{1,13},{3,15... | collective-permute-start | bytes 135176 | tf_op jit(solution)/shard_map/ppermute | solution.py:36
  6.1 0.0 collective-permute-start.1
  6.1 0.6 %collective-permute-start.2 = (bf16[1,2,11264]{2,1,0:T(2,128)(2,1)S(1)}, bf16[1,2,11264]{2,1,0:T(2,128)(2,1)S(1)}, u32[]{:S(2)}, u32[]{:S(2)}) collective-permute-start(bf16[1,2,11264]{2,1,0:T(2,128)(2,1)S(1)} %bitcast.19), channel_id=1, source_target_pairs={{0,4},{2,6},{4,0},{6,2},{8,12},{10,14},{12,8},{14,10},{1,5},{3,7},... | collective-permute-start | bytes 135176 | tf_op jit(solution)/shard_map/ppermute | solution.py:36
  6.7 1.4 %collective-permute-done = bf16[1,2,11264]{2,1,0:T(2,128)(2,1)S(1)} collective-permute-done((bf16[1,2,11264]{2,1,0:T(2,128)(2,1)S(1)}, bf16[1,2,11264]{2,1,0:T(2,128)(2,1)S(1)}, u32[]{:S(2)}, u32[]{:S(2)}) %collective-permute-start) | collective-permute-done | bytes 45088 | tf_op jit(solution)/shard_map/ppermute | solution.py:36
  8.2 2.9 %collective-permute-done.1 = bf16[1,2,11264]{2,1,0:T(2,128)(2,1)S(1)} collective-permute-done((bf16[1,2,11264]{2,1,0:T(2,128)(2,1)S(1)}, bf16[1,2,11264]{2,1,0:T(2,128)(2,1)S(1)}, u32[]{:S(2)}, u32[]{:S(2)}) %collective-permute-start.1) | collective-permute-done | bytes 45088 | tf_op jit(solution)/shard_map/ppermute | solution.py:36
  11.0 0.0 collective-permute-done.2
  11.0 0.3 pad_maximum_fusion.refs_0_
  11.4 1.6 %collective-permute-start.3 = (bf16[4,2,11264]{2,1,0:T(2,128)(2,1)S(1)}, bf16[4,2,11264]{2,1,0:T(2,128)(2,1)S(1)}, u32[]{:S(2)}, u32[]{:S(2)}) collective-permute-start(bf16[4,2,11264]{2,1,0:T(2,128)(2,1)S(1)} %pad_maximum_fusion.refs_0_), channel_id=1, source_target_pairs={{0,2},{2,0},{4,6},{6,4},{8,10},{10,8},{12,14},{14,12},{1,3},{3,1},... | collective-permute-start | bytes 540680 | tf_op jit(solution)/shard_map/ppermute | solution.py:36
  12.9 4.0 %collective-permute-done.3.refs_1_ = bf16[4,2,11264]{2,1,0:T(2,128)(2,1)S(1)} collective-permute-done((bf16[4,2,11264]{2,1,0:T(2,128)(2,1)S(1)}, bf16[4,2,11264]{2,1,0:T(2,128)(2,1)S(1)}, u32[]{:S(2)}, u32[]{:S(2)}) %collective-permute-start.3) | collective-permute-done | bytes 180256 | tf_op jit(solution)/shard_map/ppermute | solution.py:36
  16.9 0.0 slice-done.1
  17.0 0.0 copy-start
  17.0 0.0 copy-start.1
  17.0 0.0 copy-start.5
  17.0 0.0 copy-start.6
  17.0 2.6 %rotate.1 = bf16[1,16,1408]{2,1,0:T(8,128)(2,1)S(1)} custom-call(bf16[4,2,11264]{2,1,0:T(2,128)(2,1)S(1)} %pad_maximum_fusion.refs_0_, bf16[4,2,11264]{2,1,0:T(2,128)(2,1)S(1)} %collective-permute-done.3.refs_1_, bf16[7168,896]{1,0:T(8,128)(2,1)S(1)} %bitcast.11, bf16[4096,512]{1,0:T(8,128)(2,1)S(1)} %bitcast.16, f32[1,7168]{1,0:T(1,128)S(1)} %copy-done.3, ...), custom_call_target="tpu_custom_call" | custom-call | flops 272000000 | bytes 17000000 | tf_op jit(solution)/shard_map/rotate/pallas_call | solution.py:225
  19.7 1.9 %collective-permute-start.4 = (bf16[1,16,1408]{2,1,0:T(8,128)(2,1)S(1)}, bf16[1,16,1408]{2,1,0:T(8,128)(2,1)S(1)}, u32[]{:S(2)}, u32[]{:S(2)}) collective-permute-start(bf16[1,16,1408]{2,1,0:T(8,128)(2,1)S(1)} %rotate.1), channel_id=1, source_target_pairs={{0,12},{2,14},{4,8},{6,10},{8,4},{10,6},{12,0},{14,2},{1,13},{3,15... | collective-permute-start | bytes 135176 | tf_op jit(solution)/shard_map/ppermute | solution.py:36
  21.5 0.2 collective-permute-start.5
  21.8 2.3 %collective-permute-start.6 = (bf16[1,16,1408]{2,1,0:T(8,128)(2,1)S(1)}, bf16[1,16,1408]{2,1,0:T(8,128)(2,1)S(1)}, u32[]{:S(2)}, u32[]{:S(2)}) collective-permute-start(bf16[1,16,1408]{2,1,0:T(8,128)(2,1)S(1)} %rotate.1), channel_id=1, source_target_pairs={{0,4},{2,6},{4,0},{6,2},{8,12},{10,14},{12,8},{14,10},{1,5},{3,7},... | collective-permute-start | bytes 135176 | tf_op jit(solution)/shard_map/ppermute | solution.py:36
  24.1 1.5 %collective-permute-done.4 = bf16[1,16,1408]{2,1,0:T(8,128)(2,1)S(1)} collective-permute-done((bf16[1,16,1408]{2,1,0:T(8,128)(2,1)S(1)}, bf16[1,16,1408]{2,1,0:T(8,128)(2,1)S(1)}, u32[]{:S(2)}, u32[]{:S(2)}) %collective-permute-start.4) | collective-permute-done | bytes 45088 | tf_op jit(solution)/shard_map/ppermute | solution.py:36
  25.5 1.4 %collective-permute-done.5 = bf16[1,16,1408]{2,1,0:T(8,128)(2,1)S(1)} collective-permute-done((bf16[1,16,1408]{2,1,0:T(8,128)(2,1)S(1)}, bf16[1,16,1408]{2,1,0:T(8,128)(2,1)S(1)}, u32[]{:S(2)}, u32[]{:S(2)}) %collective-permute-start.5) | collective-permute-done | bytes 45088 | tf_op jit(solution)/shard_map/ppermute | solution.py:36
  26.9 0.0 collective-permute-done.6
  27.0 1.6 %collective-permute-start.7 = (bf16[4,16,1408]{2,1,0:T(8,128)(2,1)S(1)}, bf16[4,16,1408]{2,1,0:T(8,128)(2,1)S(1)}, u32[]{:S(2)}, u32[]{:S(2)}) collective-permute-start(bf16[4,16,1408]{2,1,0:T(8,128)(2,1)S(1)} %pad_maximum_fusion.1.refs_0_), channel_id=1, source_target_pairs={{0,2},{2,0},{4,6},{6,4},{8,10},{10,8},{12,14},{14,12},{1,3},{3,1},... | collective-permute-start | bytes 540680 | tf_op jit(solution)/shard_map/ppermute | solution.py:36
  28.5 1.4 %self_influence.1.refs_6_ = f32[8,128]{1,0:T(8,128)S(1)} custom-call(bf16[160,7168]{1,0:T(8,128)(2,1)S(1)} %bitcast.12, bf16[160,4096]{1,0:T(8,128)(2,1)S(1)} %bitcast.14, f32[1,7168]{1,0:T(1,128)S(1)} %copy-done.3, f32[1,4096]{1,0:T(1,128)S(1)} %copy-done.4, s32[1,160]{1,0:T(1,128)S(1)} %copy-done.5), custom_call_target="tpu_custom_call" | custom-call | flops 576716800 | bytes 3700000 | tf_op jit(solution)/shard_map/self_influence/pallas_call | solution.py:222
  29.9 2.6 %collective-permute-done.7.refs_1_ = bf16[4,16,1408]{2,1,0:T(8,128)(2,1)S(1)} collective-permute-done((bf16[4,16,1408]{2,1,0:T(8,128)(2,1)S(1)}, bf16[4,16,1408]{2,1,0:T(8,128)(2,1)S(1)}, u32[]{:S(2)}, u32[]{:S(2)}) %collective-permute-start.7) | collective-permute-done | bytes 180256 | tf_op jit(solution)/shard_map/ppermute | solution.py:36
  32.5 0.0 copy-done.6
  32.5 1.7 %scores.1.mine = f32[8,128]{1,0:T(8,128)S(1)} custom-call(bf16[4,16,1408]{2,1,0:T(8,128)(2,1)S(1)} %pad_maximum_fusion.1.refs_0_, bf16[4,16,1408]{2,1,0:T(8,128)(2,1)S(1)} %collective-permute-done.7.refs_1_, bf16[160,7168]{1,0:T(8,128)(2,1)S(1)} %bitcast.13, bf16[160,4096]{1,0:T(8,128)(2,1)S(1)} %bitcast.15, s32[1,16]{1,0:T(1,128)S(1)} %bitcast.21, ...), custom_call_target="tpu_custom_call" | custom-call | tf_op jit(solution)/shard_map/scores/pallas_call | solution.py:234
  34.2 0.0 collective-permute-start.8
  34.2 1.2 %collective-permute-done.8.other = f32[8,128]{1,0:T(8,128)S(1)} collective-permute-done((f32[8,128]{1,0:T(8,128)S(1)}, f32[8,128]{1,0:T(8,128)S(1)}, u32[]{:S(2)}, u32[]{:S(2)}) %collective-permute-start.8) | collective-permute-done | bytes 4128 | tf_op jit(solution)/shard_map/ppermute | solution.py:176
  35.4 0.6 %finish.1 = f32[2,4]{1,0:T(2,128)} custom-call(f32[8,128]{1,0:T(8,128)S(1)} %scores.1.mine, f32[8,128]{1,0:T(8,128)S(1)} %collective-permute-done.8.other), custom_call_target="tpu_custom_call" | custom-call | tf_op jit(solution)/shard_map/finish/pallas_call | solution.py:237
  (16 shorter events, 0.1 us)
Async XLA Ops:
  0.0 16.9 %slice-start = ((s8[12845056]{0:T(1024)(128)(4,1)}), s8[4194304]{0:T(1024)(128)(4,1)S(1)}, s32[]{:S(2)}) async-start(s8[12845056]{0:T(1024)(128)(4,1)} %bitcast.9), calls=%async_computation | async-start | bytes 8388608
  0.0 16.9 %slice-start.1 = ((s8[12845056]{0:T(1024)(128)(4,1)}), s8[4194304]{0:T(1024)(128)(4,1)S(1)}, s32[]{:S(2)}) async-start(s8[12845056]{0:T(1024)(128)(4,1)} %bitcast.9), calls=%async_computation.1 | async-start | bytes 8388608
  0.0 16.9 %slice-start.2 = ((s8[12845056]{0:T(1024)(128)(4,1)}), s8[4194304]{0:T(1024)(128)(4,1)S(1)}, s32[]{:S(2)}) async-start(s8[12845056]{0:T(1024)(128)(4,1)} %bitcast.9), calls=%async_computation.2 | async-start | bytes 8388608
  0.0 16.9 %slice-start.3 = ((s8[12845056]{0:T(1024)(128)(4,1)}), s8[262144]{0:T(1024)(128)(4,1)S(1)}, s32[]{:S(2)}) async-start(s8[12845056]{0:T(1024)(128)(4,1)} %bitcast.9), calls=%async_computation.3 | async-start | bytes 524288
  0.0 16.9 %copy-start.2 = (bf16[1,4096,512]{2,1,0:T(8,128)(2,1)S(1)}, bf16[1,4096,512]{2,1,0:T(8,128)(2,1)}, u32[]{:S(2)}) copy-start(bf16[1,4096,512]{2,1,0:T(8,128)(2,1)} %param.15) | copy-start | bytes 12582916
  0.0 16.9 %copy-start.3 = (f32[1,7168]{1,0:T(1,128)S(1)}, f32[1,7168]{1,0:T(1,128)}, u32[]{:S(2)}) copy-start(f32[1,7168]{1,0:T(1,128)} %eig_h.1) | copy-start | bytes 86020
  0.0 16.9 %copy-start.4 = (f32[1,4096]{1,0:T(1,128)S(1)}, f32[1,4096]{1,0:T(1,128)}, u32[]{:S(2)}) copy-start(f32[1,4096]{1,0:T(1,128)} %eig_i.1) | copy-start | bytes 49156
  1.0 7.2 %collective-permute-start = (bf16[1,2,11264]{2,1,0:T(2,128)(2,1)S(1)}, bf16[1,2,11264]{2,1,0:T(2,128)(2,1)S(1)}, u32[]{:S(2)}, u32[]{:S(2)}) collective-permute-start(bf16[1,2,11264]{2,1,0:T(2,128)(2,1)S(1)} %bitcast.17), channel_id=1, source_target_pairs={{0,12},{2,14},{4,8},{6,10},{8,4},{10,6},{12,0},{14,2},{1,13},{3,15... | collective-permute-start | bytes 135176 | tf_op jit(solution)/shard_map/ppermute | solution.py:36
  6.1 4.9 %collective-permute-start.1 = (bf16[1,2,11264]{2,1,0:T(2,128)(2,1)S(1)}, bf16[1,2,11264]{2,1,0:T(2,128)(2,1)S(1)}, u32[]{:S(2)}, u32[]{:S(2)}) collective-permute-start(bf16[1,2,11264]{2,1,0:T(2,128)(2,1)S(1)} %bitcast.18), channel_id=1, source_target_pairs={{0,8},{2,10},{4,12},{6,14},{8,0},{10,2},{12,4},{14,6},{1,9},{3,11}... | collective-permute-start | bytes 135176 | tf_op jit(solution)/shard_map/ppermute | solution.py:36
  6.1 4.9 %collective-permute-start.2 = (bf16[1,2,11264]{2,1,0:T(2,128)(2,1)S(1)}, bf16[1,2,11264]{2,1,0:T(2,128)(2,1)S(1)}, u32[]{:S(2)}, u32[]{:S(2)}) collective-permute-start(bf16[1,2,11264]{2,1,0:T(2,128)(2,1)S(1)} %bitcast.19), channel_id=1, source_target_pairs={{0,4},{2,6},{4,0},{6,2},{8,12},{10,14},{12,8},{14,10},{1,5},{3,7},... | collective-permute-start | bytes 135176 | tf_op jit(solution)/shard_map/ppermute | solution.py:36
  11.4 5.6 %collective-permute-start.3 = (bf16[4,2,11264]{2,1,0:T(2,128)(2,1)S(1)}, bf16[4,2,11264]{2,1,0:T(2,128)(2,1)S(1)}, u32[]{:S(2)}, u32[]{:S(2)}) collective-permute-start(bf16[4,2,11264]{2,1,0:T(2,128)(2,1)S(1)} %pad_maximum_fusion.refs_0_), channel_id=1, source_target_pairs={{0,2},{2,0},{4,6},{6,4},{8,10},{10,8},{12,14},{14,12},{1,3},{3,1},... | collective-permute-start | bytes 540680 | tf_op jit(solution)/shard_map/ppermute | solution.py:36
  17.0 11.5 %copy-start = (bf16[1,160,7168]{2,1,0:T(8,128)(2,1)S(1)}, bf16[1,160,7168]{2,1,0:T(8,128)(2,1)}, u32[]{:S(2)}) copy-start(bf16[1,160,7168]{2,1,0:T(8,128)(2,1)} %param.12) | copy-start | bytes 6881284
  17.0 11.5 %copy-start.1 = (bf16[1,160,4096]{2,1,0:T(8,128)(2,1)S(1)}, bf16[1,160,4096]{2,1,0:T(8,128)(2,1)}, u32[]{:S(2)}) copy-start(bf16[1,160,4096]{2,1,0:T(8,128)(2,1)} %param.13) | copy-start | bytes 3932164
  17.0 11.5 %copy-start.5 = (s32[1,160]{1,0:T(1,128)S(1)}, s32[1,160]{1,0:T(1,128)}, u32[]{:S(2)}) copy-start(s32[1,160]{1,0:T(1,128)} %refs_5_.3) | copy-start | bytes 1924
  17.0 15.5 %copy-start.6 = (s32[16]{0:T(128)S(1)}, s32[16]{0:T(128)}, u32[]{:S(2)}) copy-start(s32[16]{0:T(128)} %param.18) | copy-start | bytes 196
  19.7 5.9 %collective-permute-start.4 = (bf16[1,16,1408]{2,1,0:T(8,128)(2,1)S(1)}, bf16[1,16,1408]{2,1,0:T(8,128)(2,1)S(1)}, u32[]{:S(2)}, u32[]{:S(2)}) collective-permute-start(bf16[1,16,1408]{2,1,0:T(8,128)(2,1)S(1)} %rotate.1), channel_id=1, source_target_pairs={{0,12},{2,14},{4,8},{6,10},{8,4},{10,6},{12,0},{14,2},{1,13},{3,15... | collective-permute-start | bytes 135176 | tf_op jit(solution)/shard_map/ppermute | solution.py:36
  21.5 5.4 %collective-permute-start.5 = (bf16[1,16,1408]{2,1,0:T(8,128)(2,1)S(1)}, bf16[1,16,1408]{2,1,0:T(8,128)(2,1)S(1)}, u32[]{:S(2)}, u32[]{:S(2)}) collective-permute-start(bf16[1,16,1408]{2,1,0:T(8,128)(2,1)S(1)} %rotate.1), channel_id=1, source_target_pairs={{0,8},{2,10},{4,12},{6,14},{8,0},{10,2},{12,4},{14,6},{1,9},{3,11}... | collective-permute-start | bytes 135176 | tf_op jit(solution)/shard_map/ppermute | solution.py:36
  21.8 5.2 %collective-permute-start.6 = (bf16[1,16,1408]{2,1,0:T(8,128)(2,1)S(1)}, bf16[1,16,1408]{2,1,0:T(8,128)(2,1)S(1)}, u32[]{:S(2)}, u32[]{:S(2)}) collective-permute-start(bf16[1,16,1408]{2,1,0:T(8,128)(2,1)S(1)} %rotate.1), channel_id=1, source_target_pairs={{0,4},{2,6},{4,0},{6,2},{8,12},{10,14},{12,8},{14,10},{1,5},{3,7},... | collective-permute-start | bytes 135176 | tf_op jit(solution)/shard_map/ppermute | solution.py:36
  27.0 5.6 %collective-permute-start.7 = (bf16[4,16,1408]{2,1,0:T(8,128)(2,1)S(1)}, bf16[4,16,1408]{2,1,0:T(8,128)(2,1)S(1)}, u32[]{:S(2)}, u32[]{:S(2)}) collective-permute-start(bf16[4,16,1408]{2,1,0:T(8,128)(2,1)S(1)} %pad_maximum_fusion.1.refs_0_), channel_id=1, source_target_pairs={{0,2},{2,0},{4,6},{6,4},{8,10},{10,8},{12,14},{14,12},{1,3},{3,1},... | collective-permute-start | bytes 540680 | tf_op jit(solution)/shard_map/ppermute | solution.py:36
  34.2 1.2 %collective-permute-start.8 = (f32[8,128]{1,0:T(8,128)S(1)}, f32[8,128]{1,0:T(8,128)S(1)}, u32[]{:S(2)}, u32[]{:S(2)}) collective-permute-start(f32[8,128]{1,0:T(8,128)S(1)} %scores.1.mine), channel_id=1, source_target_pairs={{0,1},{1,0},{2,3},{3,2},{4,5},{5,4},{6,7},{7,6},{8,9},{9,8},{10,11... | collective-permute-start | bytes 12296 | tf_op jit(solution)/shard_map/ppermute | solution.py:176

commit v2 on v1

--- a/solution.py
+++ b/solution.py
@@ -12,6 +12,8 @@
 DAMP = 0.1
 LANES = 128
 MIB = 2**20
+X, Z, FAR = 1, 2, 4
+PLAN = [(Z, (0,)), (FAR, (0,)), (X ^ FAR, (0, Z)), (X, (0, Z)), (Z, (FAR,))]
 BY_LANES = (((1,), (1,)), ((), ()))
 
 
@@ -23,22 +25,31 @@
     return pltpu.with_memory_space_constraint(x, pltpu.HBM)
 
 
+def steps(shards):
+    if shards == 8:
+        return PLAN
+    plan, known, stride = [], [0], shards
+    while stride > 1:
+        radix = min(4, stride)
+        stride //= radix
+        plan += [(m * stride, tuple(known)) for m in range(1, radix)]
+        known = [k ^ (m * stride) for m in range(radix) for k in known]
+    return plan
+
+
 def gather(x, shards):
     x = x[None]
-    masks = [0]
-    stride = shards
-    while True:
-        radix = min(4, stride // 2) if stride > 2 else stride
-        stride //= radix
-        parts, of_parts = [x], [masks]
-        for m in reversed(range(1, radix)):
-            mask = m * stride
-            parts.append(lax.ppermute(x, "ex", [(i, i ^ mask) for i in range(shards)]))
-            of_parts.append([mask ^ old for old in masks])
-        if stride == 1:
-            return parts, of_parts
-        x = jnp.concatenate(parts, axis=0)
-        masks = sum(of_parts, [])
+    parts, masks = [x], [[0]]
+    blocks, joined = {0: x}, {(0,): x}
+    for mask, sent in steps(shards):
+        if sent not in joined:
+            joined[sent] = jnp.concatenate([blocks[s] for s in sent], axis=0)
+        part = lax.ppermute(joined[sent], "ex", [(i, i ^ mask) for i in range(shards)])
+        parts.append(part)
+        masks.append([mask ^ s for s in sent])
+        for i, s in enumerate(sent):
+            blocks[mask ^ s] = part[i : i + 1]
+    return parts, masks
 
 
 def in_order(parts, masks):
@@ -76,8 +87,8 @@
 
 
 def rotate_kernel(masks, *refs):
-    parts = refs[:-6]
-    basis_h, basis_i, eig_h, eig_i, out, tokens = refs[-6:]
+    parts = refs[:-7]
+    basis_h, basis_i, eig_h, eig_i, _, out, tokens = refs[-7:]
     width_h = basis_h.shape[0]
     hid_block = basis_h.shape[1]
     inp_block = basis_i.shape[1]
@@ -109,47 +120,52 @@
     rotate(slice(width_h, None), basis_i, eig_i, inp_block, slice(hid_block, None))
 
 
-def score_kernel(masks, hid_block, inp_block, *refs):
-    parts = refs[:-6]
-    train_h, train_i, query_ids, ids, own_self, out = refs[-6:]
+def add_grams(grams, masks, parts, train_h, train_i):
     me = lax.axis_index("ex")
-    gram_h = gram_i = 0.0
+    trains = (train_h, train_i)
+    ends = [train.shape[1] // lax.axis_size("ex") for train in trains]
+    lanes = (slice(0, ends[0]), slice(ends[0], None))
     for part, of_part in zip(parts, masks):
         for i, mask in enumerate(of_part):
             block = me ^ mask
-            at_h = pl.ds(pl.multiple_of(block * hid_block, LANES), hid_block)
-            at_i = pl.ds(pl.multiple_of(block * inp_block, LANES), inp_block)
-            gram_h += lax.dot_general(
-                part[i, :, :hid_block],
-                train_h[:, at_h],
-                BY_LANES,
-                preferred_element_type=jnp.float32,
-            )
-            gram_i += lax.dot_general(
-                part[i, :, hid_block:],
-                train_i[:, at_i],
-                BY_LANES,
-                preferred_element_type=jnp.float32,
-            )
-    row = lax.broadcasted_iota(jnp.int32, (out.shape[0], ids.shape[1]), 0)
-    example_hot = ((ids[...] == row) & (row < E_DEV)).astype(jnp.float32)
-    summed = lax.dot_general(
-        example_hot,
-        gram_h * gram_i,
-        BY_LANES,
-        precision=lax.Precision.HIGHEST,
-        preferred_element_type=jnp.float32,
-    )
-    query = lax.broadcasted_iota(jnp.int32, (LANES, query_ids.shape[1]), 0)
-    query_hot = (query_ids[...] == query).astype(jnp.float32)
-    scores = lax.dot_general(
-        summed,
-        query_hot,
-        BY_LANES,
-        precision=lax.Precision.HIGHEST,
-        preferred_element_type=jnp.float32,
-    )
-    out[...] = scores + own_self[...]
+            grams = [
+                gram
+                + lax.dot_general(
+                    part[i, :, at],
+                    train[:, pl.ds(pl.multiple_of(block * size, LANES), size)],
+                    BY_LANES,
+                    preferred_element_type=jnp.float32,
+                )
+                for gram, train, size, at in zip(grams, trains, ends, lanes)
+            ]
+    return grams
+
+
+def early_kernel(masks, *refs):
+    parts = refs[:-5]
+    train_h, train_i, query_ids, grams, query_hot = refs[-5:]
+    grams[0], grams[1] = add_grams((0.0, 0.0), masks, parts, train_h, train_i)
+    tokens = query_ids.shape[1]
+    row = lax.broadcasted_iota(jnp.int32, (tokens, tokens), 0)
+    column = lax.broadcasted_iota(jnp.int32, (tokens, tokens), 1)
+    own_id = jnp.where(row == column, jnp.broadcast_to(query_ids[...], (tokens, tokens)), 0)
+    own_id = jnp.sum(own_id.astype(jnp.float32), axis=1, keepdims=True)
+    query = lax.broadcasted_iota(jnp.int32, query_hot.shape, 1).astype(jnp.float32)
+    query_hot[...] = (own_id == query).astype(jnp.float32)
+
+
+def late_kernel(masks, *refs):
+    parts = refs[:-7]
+    train_h, train_i, grams, query_hot, ids, own_self, out = refs[-7:]
+    gram_h, gram_i = add_grams((grams[0], grams[1]), masks, parts, train_h, train_i)
+    cross = gram_h * gram_i
+    row = lax.broadcasted_iota(jnp.int32, out.shape, 0)
+    scores = own_self[...]
+    for e in range(E_DEV):
+        of_token = jnp.sum(jnp.where(ids[...] == e, cross, 0.0), axis=1, keepdims=True)
+        of_query = jnp.sum(of_token * query_hot[...], axis=0, keepdims=True)
+        scores = jnp.where(row == e, of_query, scores)
+    out[...] = scores
 
 
 def finish_kernel(mine, other, out):
@@ -229,10 +245,20 @@
         flops=2 * 16 * 8_500_000,
         moved=17_000_000,
         scratch_shapes=[pltpu.VMEM((tokens, width), jnp.float32)],
-    )(*everyone, basis_h, basis_i, eig_h, eig_i)
+    )(*everyone, basis_h, basis_i, eig_h, eig_i, own_self)
     parts, masks = gather(rotated[0], shards)
-    mine = call(functools.partial(score_kernel, masks, hid_block, inp_block), "scores", small)(
-        *parts, train_h, train_i, query_ids, example_ids, own_self
+    first = 3
+    grams, query_hot = call(
+        functools.partial(early_kernel, masks[:first]),
+        "early_grams",
+        (
+            jax.ShapeDtypeStruct((2, tokens, train_h.shape[0]), jnp.float32),
+            jax.ShapeDtypeStruct((tokens, LANES), jnp.float32),
+        ),
+        flops=500_000_000,
+    )(*parts[:first], train_h, train_i, query_ids)
+    mine = call(functools.partial(late_kernel, masks[first:]), "scores", small)(
+        *parts[first:], train_h, train_i, grams, query_hot, example_ids, own_self
     )
     return call(
         finish_kernel,

time: 36.3 us -> 33 us (0.909)
  waiting for transfers between devices: 15 us -> 7.05 us
  starting transfers between devices: 13.3 us -> 18.5 us
    ppermute x8 -> x10, waiting for transfers between devices: 13.8 us -> 5.89 us  [gather(): lax.ppermute(joined[sent], 'ex', [(i, i ^ mask) for i in range(shards)])]
    ppermute x8 -> x10, starting transfers between devices: 13.3 us -> 18.5 us  [gather(): lax.ppermute(joined[sent], 'ex', [(i, i ^ mask) for i in range(shards)])]
    pallas_call x1 -> x2, Pallas kernels: 1.68 us -> 1.32 us  [the longest x1 0.84 us: body(): call(functools.partial(late_kernel, masks[first:]), 'scores', small)]
  transfers between devices with their start and end apart: 9 -> 11, of which waited for: 7 -> 5; matrix products, arithmetic and copies ran while one was open for 0% -> 0% of each run, Pallas kernels for 4% -> 6%
where the time goes in v2:
time: 33 us; the launch traced here: 32.8 us
  starting transfers between devices  18.5 us (56%)
  waiting for transfers between devices  7.05 us (21%)
  Pallas kernels  6.91 us (21%)
    ppermute x10, starting transfers between devices, gather(): lax.ppermute(joined[sent], 'ex', [(i, i ^ mask) for i in range(shards)])  18.5 us
    ppermute x10, waiting for transfers between devices, gather(): lax.ppermute(joined[sent], 'ex', [(i, i ^ mask) for i in range(shards)])  5.89 us
    pallas_call x1, Pallas kernels, body(): call(functools.partial(rotate_kernel, masks), 'rotate', jax.ShapeDtypeStr...  2.61 us
    pallas_call x1, Pallas kernels, body(): call(self_kernel, 'self_influence', small, flops=2 * 160 * 160 * 11264, m...  1.41 us
    ppermute x1, waiting for transfers between devices, layer_swap(): return lax.ppermute(x, 'layer', [(0, 1), (1, 0)])  1.16 us
    pallas_call x1, Pallas kernels, body(): call(join_kernel, 'join', pltpu.VMEM((own_tokens, width), jnp.bfloat16),...  0.92 us
    pallas_call x1, Pallas kernels, body(): call(functools.partial(late_kernel, masks[first:]), 'scores', small)  0.84 us
  transfers between devices with their start and end apart: 11, of which 5 were waited for; matrix products, arithmetic and copies ran while one was open for 0% of the time, Pallas kernels for 6%

profile of v2, /device:TPU:0, one launch (start us, length us, event | category | flops | bytes accessed | tf_op | source)
XLA Modules:
  0.0 32.8 jit_solution(2494027006996351312)
XLA Ops:
  0.0 0.0 slice-start.1
  0.0 0.0 slice-start.2
  0.0 0.0 slice-start.3
  0.1 0.9 %join.1 = bf16[2,11264]{1,0:T(2,128)(2,1)S(1)} custom-call(bf16[2,7168]{1,0:T(2,128)(2,1)} %bitcast.24, bf16[2,4096]{1,0:T(2,128)(2,1)} %bitcast.25), custom_call_target="tpu_custom_call" | custom-call | flops 20000000000 | tf_op jit(solution)/shard_map/join/pallas_call | solution.py:227
  1.0 3.1 %collective-permute-start = (bf16[1,2,11264]{2,1,0:T(2,128)(2,1)S(1)}, bf16[1,2,11264]{2,1,0:T(2,128)(2,1)S(1)}, u32[]{:S(2)}, u32[]{:S(2)}) collective-permute-start(bf16[1,2,11264]{2,1,0:T(2,128)(2,1)S(1)} %bitcast.19), channel_id=1, source_target_pairs={{0,4},{2,6},{4,0},{6,2},{8,12},{10,14},{12,8},{14,10},{1,5},{3,7},... | collective-permute-start | bytes 135176 | tf_op jit(solution)/shard_map/ppermute | solution.py:47
  4.1 2.6 %collective-permute-start.1 = (bf16[1,2,11264]{2,1,0:T(2,128)(2,1)S(1)}, bf16[1,2,11264]{2,1,0:T(2,128)(2,1)S(1)}, u32[]{:S(2)}, u32[]{:S(2)}) collective-permute-start(bf16[1,2,11264]{2,1,0:T(2,128)(2,1)S(1)} %bitcast.20), channel_id=1, source_target_pairs={{0,8},{2,10},{4,12},{6,14},{8,0},{10,2},{12,4},{14,6},{1,9},{3,11}... | collective-permute-start | bytes 135176 | tf_op jit(solution)/shard_map/ppermute | solution.py:47
  6.7 0.0 collective-permute-done.refs_1_
  6.7 0.1 pad_maximum_fusion
  6.8 3.5 %collective-permute-start.2 = (bf16[2,2,11264]{2,1,0:T(2,128)(2,1)S(1)}, bf16[2,2,11264]{2,1,0:T(2,128)(2,1)S(1)}, u32[]{:S(2)}, u32[]{:S(2)}) collective-permute-start(bf16[2,2,11264]{2,1,0:T(2,128)(2,1)S(1)} %pad_maximum_fusion), channel_id=1, source_target_pairs={{0,10},{2,8},{4,14},{6,12},{8,2},{10,0},{12,6},{14,4},{1,11},{3,9}... | collective-permute-start | bytes 270344 | tf_op jit(solution)/shard_map/ppermute | solution.py:47
  10.3 0.5 %collective-permute-start.3 = (bf16[2,2,11264]{2,1,0:T(2,128)(2,1)S(1)}, bf16[2,2,11264]{2,1,0:T(2,128)(2,1)S(1)}, u32[]{:S(2)}, u32[]{:S(2)}) collective-permute-start(bf16[2,2,11264]{2,1,0:T(2,128)(2,1)S(1)} %pad_maximum_fusion), channel_id=1, source_target_pairs={{0,2},{2,0},{4,6},{6,4},{8,10},{10,8},{12,14},{14,12},{1,3},{3,1},... | collective-permute-start | bytes 270344 | tf_op jit(solution)/shard_map/ppermute | solution.py:47
  10.8 0.0 collective-permute-done.1.refs_2_
  10.8 2.0 %collective-permute-start.4 = (bf16[1,2,11264]{2,1,0:T(2,128)(2,1)S(1)}, bf16[1,2,11264]{2,1,0:T(2,128)(2,1)S(1)}, u32[]{:S(2)}, u32[]{:S(2)}) collective-permute-start(bf16[1,2,11264]{2,1,0:T(2,128)(2,1)S(1)} %collective-permute-done.1.refs_2_), channel_id=1, source_target_pairs={{0,4},{2,6},{4,0},{6,2},{8,12},{10,14},{12,8},{14,10},{1,5},{3,7},... | collective-permute-start | bytes 135176 | tf_op jit(solution)/shard_map/ppermute | solution.py:47
  12.8 1.4 %self_influence.1.refs_10_.refs_8_ = f32[8,128]{1,0:T(8,128)S(1)} custom-call(bf16[160,7168]{1,0:T(8,128)(2,1)S(1)} %bitcast.9, bf16[160,4096]{1,0:T(8,128)(2,1)S(1)} %bitcast.15, f32[1,7168]{1,0:T(1,128)S(1)} %copy-done.3, f32[1,4096]{1,0:T(1,128)S(1)} %copy-done.4, s32[1,160]{1,0:T(1,128)S(1)} %copy-done.5), custom_call_target="tpu_custom_call" | custom-call | flops 576716800 | bytes 3700000 | tf_op jit(solution)/shard_map/self_influence/pallas_call | solution.py:238
  14.2 0.7 %collective-permute-done.4.refs_5_ = bf16[1,2,11264]{2,1,0:T(2,128)(2,1)S(1)} collective-permute-done((bf16[1,2,11264]{2,1,0:T(2,128)(2,1)S(1)}, bf16[1,2,11264]{2,1,0:T(2,128)(2,1)S(1)}, u32[]{:S(2)}, u32[]{:S(2)}) %collective-permute-start.4) | collective-permute-done | bytes 45088 | tf_op jit(solution)/shard_map/ppermute | solution.py:47
  14.9 0.0 collective-permute-done.2.refs_3_
  14.9 0.0 collective-permute-done.3.refs_4_
  15.0 0.0 copy-start.6
  15.0 2.6 %rotate.1.refs_0_ = bf16[1,16,1408]{2,1,0:T(8,128)(2,1)S(1)} custom-call(bf16[1,2,11264]{2,1,0:T(2,128)(2,1)S(1)} %bitcast.22, bf16[1,2,11264]{2,1,0:T(2,128)(2,1)S(1)} %collective-permute-done.refs_1_, bf16[1,2,11264]{2,1,0:T(2,128)(2,1)S(1)} %collective-permute-done.1.refs_2_, bf16[2,2,11264]{2,1,0:T(2,128)(2,1)S(1)} %collective-permute-done.2.refs_3_, ...), custom_call_target="tpu_custom_call" | custom-call | flops 272000000 | bytes 17000000 | tf_op jit(solution)/shard_map/rotate/pallas_call | solution.py:241
  17.6 1.9 %collective-permute-start.5 = (bf16[1,16,1408]{2,1,0:T(8,128)(2,1)S(1)}, bf16[1,16,1408]{2,1,0:T(8,128)(2,1)S(1)}, u32[]{:S(2)}, u32[]{:S(2)}) collective-permute-start(bf16[1,16,1408]{2,1,0:T(8,128)(2,1)S(1)} %rotate.1.refs_0_), channel_id=1, source_target_pairs={{0,4},{2,6},{4,0},{6,2},{8,12},{10,14},{12,8},{14,10},{1,5},{3,7},... | collective-permute-start | bytes 135176 | tf_op jit(solution)/shard_map/ppermute | solution.py:47
  19.6 1.4 %collective-permute-start.8 = (bf16[1,16,1408]{2,1,0:T(8,128)(2,1)S(1)}, bf16[1,16,1408]{2,1,0:T(8,128)(2,1)S(1)}, u32[]{:S(2)}, u32[]{:S(2)}) collective-permute-start(bf16[1,16,1408]{2,1,0:T(8,128)(2,1)S(1)} %rotate.1.refs_0_), channel_id=1, source_target_pairs={{0,8},{2,10},{4,12},{6,14},{8,0},{10,2},{12,4},{14,6},{1,9},{3,11}... | collective-permute-start | bytes 135176 | tf_op jit(solution)/shard_map/ppermute | solution.py:47
  21.0 0.7 %collective-permute-done.5.refs_1_ = bf16[1,16,1408]{2,1,0:T(8,128)(2,1)S(1)} collective-permute-done((bf16[1,16,1408]{2,1,0:T(8,128)(2,1)S(1)}, bf16[1,16,1408]{2,1,0:T(8,128)(2,1)S(1)}, u32[]{:S(2)}, u32[]{:S(2)}) %collective-permute-start.5) | collective-permute-done | bytes 45088 | tf_op jit(solution)/shard_map/ppermute | solution.py:47
  21.7 2.1 %collective-permute-start.6 = (bf16[2,16,1408]{2,1,0:T(8,128)(2,1)S(1)}, bf16[2,16,1408]{2,1,0:T(8,128)(2,1)S(1)}, u32[]{:S(2)}, u32[]{:S(2)}) collective-permute-start(bf16[2,16,1408]{2,1,0:T(8,128)(2,1)S(1)} %pad_maximum_fusion.1), channel_id=1, source_target_pairs={{0,10},{2,8},{4,14},{6,12},{8,2},{10,0},{12,6},{14,4},{1,11},{3,9}... | collective-permute-start | bytes 270344 | tf_op jit(solution)/shard_map/ppermute | solution.py:47
  23.8 0.7 %collective-permute-start.7 = (bf16[2,16,1408]{2,1,0:T(8,128)(2,1)S(1)}, bf16[2,16,1408]{2,1,0:T(8,128)(2,1)S(1)}, u32[]{:S(2)}, u32[]{:S(2)}) collective-permute-start(bf16[2,16,1408]{2,1,0:T(8,128)(2,1)S(1)} %pad_maximum_fusion.1), channel_id=1, source_target_pairs={{0,2},{2,0},{4,6},{6,4},{8,10},{10,8},{12,14},{14,12},{1,3},{3,1},... | collective-permute-start | bytes 270344 | tf_op jit(solution)/shard_map/ppermute | solution.py:47
  24.6 1.5 %collective-permute-done.8.refs_2_ = bf16[1,16,1408]{2,1,0:T(8,128)(2,1)S(1)} collective-permute-done((bf16[1,16,1408]{2,1,0:T(8,128)(2,1)S(1)}, bf16[1,16,1408]{2,1,0:T(8,128)(2,1)S(1)}, u32[]{:S(2)}, u32[]{:S(2)}) %collective-permute-start.8) | collective-permute-done | bytes 45088 | tf_op jit(solution)/shard_map/ppermute | solution.py:47
  26.1 0.5 %collective-permute-start.9 = (bf16[1,16,1408]{2,1,0:T(8,128)(2,1)S(1)}, bf16[1,16,1408]{2,1,0:T(8,128)(2,1)S(1)}, u32[]{:S(2)}, u32[]{:S(2)}) collective-permute-start(bf16[1,16,1408]{2,1,0:T(8,128)(2,1)S(1)} %collective-permute-done.8.refs_2_), channel_id=1, source_target_pairs={{0,4},{2,6},{4,0},{6,2},{8,12},{10,14},{12,8},{14,10},{1,5},{3,7},... | collective-permute-start | bytes 135176 | tf_op jit(solution)/shard_map/ppermute | solution.py:47
  26.6 0.5 %early_grams.1 = (f32[2,16,160]{2,1,0:T(8,128)S(1)}, f32[16,128]{1,0:T(8,128)S(1)}) custom-call(bf16[1,16,1408]{2,1,0:T(8,128)(2,1)S(1)} %rotate.1.refs_0_, bf16[1,16,1408]{2,1,0:T(8,128)(2,1)S(1)} %collective-permute-done.5.refs_1_, bf16[1,16,1408]{2,1,0:T(8,128)(2,1)S(1)} %collective-permute-done.8.refs_2_, bf16[160,7168]{1,0:T(8,128)(2,1)S(1)} %bitcast.10, ...), custom_call_target="tpu_custom_call" | custom-call | flops 500000000 | tf_op jit(solution)/shard_map/early_grams/pallas_call | solution.py:251
  27.1 3.0 %collective-permute-done.9.refs_2_ = bf16[1,16,1408]{2,1,0:T(8,128)(2,1)S(1)} collective-permute-done((bf16[1,16,1408]{2,1,0:T(8,128)(2,1)S(1)}, bf16[1,16,1408]{2,1,0:T(8,128)(2,1)S(1)}, u32[]{:S(2)}, u32[]{:S(2)}) %collective-permute-start.9) | collective-permute-done | bytes 45088 | tf_op jit(solution)/shard_map/ppermute | solution.py:47
  30.1 0.0 collective-permute-done.7.refs_1_
  30.1 0.8 %scores.1.mine = f32[8,128]{1,0:T(8,128)S(1)} custom-call(bf16[2,16,1408]{2,1,0:T(8,128)(2,1)S(1)} %collective-permute-done.6.refs_0_, bf16[2,16,1408]{2,1,0:T(8,128)(2,1)S(1)} %collective-permute-done.7.refs_1_, bf16[1,16,1408]{2,1,0:T(8,128)(2,1)S(1)} %collective-permute-done.9.refs_2_, bf16[160,7168]{1,0:T(8,128)(2,1)S(1)} %bitcast.11, ...), custom_call_target="tpu_custom_call" | custom-call | tf_op jit(solution)/shard_map/scores/pallas_call | solution.py:260
  30.9 0.0 collective-permute-start.10
  31.0 1.2 %collective-permute-done.10.other = f32[8,128]{1,0:T(8,128)S(1)} collective-permute-done((f32[8,128]{1,0:T(8,128)S(1)}, f32[8,128]{1,0:T(8,128)S(1)}, u32[]{:S(2)}, u32[]{:S(2)}) %collective-permute-start.10) | collective-permute-done | bytes 4128 | tf_op jit(solution)/shard_map/ppermute | solution.py:192
  32.1 0.6 %finish.1 = f32[2,4]{1,0:T(2,128)} custom-call(f32[8,128]{1,0:T(8,128)S(1)} %scores.1.mine, f32[8,128]{1,0:T(8,128)S(1)} %collective-permute-done.10.other), custom_call_target="tpu_custom_call" | custom-call | tf_op jit(solution)/shard_map/finish/pallas_call | solution.py:263
  (21 shorter events, 0.1 us)
Async XLA Ops:
  0.0 15.0 %slice-start = ((s8[12845056]{0:T(1024)(128)(4,1)}), s8[4194304]{0:T(1024)(128)(4,1)S(1)}, s32[]{:S(2)}) async-start(s8[12845056]{0:T(1024)(128)(4,1)} %bitcast.12), calls=%async_computation | async-start | bytes 8388608
  0.0 12.8 %copy-start = (bf16[1,160,7168]{2,1,0:T(8,128)(2,1)S(1)}, bf16[1,160,7168]{2,1,0:T(8,128)(2,1)}, u32[]{:S(2)}) copy-start(bf16[1,160,7168]{2,1,0:T(8,128)(2,1)} %param.12) | copy-start | bytes 6881284
  0.0 12.8 %copy-start.1 = (bf16[1,160,4096]{2,1,0:T(8,128)(2,1)S(1)}, bf16[1,160,4096]{2,1,0:T(8,128)(2,1)}, u32[]{:S(2)}) copy-start(bf16[1,160,4096]{2,1,0:T(8,128)(2,1)} %param.13) | copy-start | bytes 3932164
  0.0 12.8 %copy-start.3 = (f32[1,7168]{1,0:T(1,128)S(1)}, f32[1,7168]{1,0:T(1,128)}, u32[]{:S(2)}) copy-start(f32[1,7168]{1,0:T(1,128)} %refs_8_.1) | copy-start | bytes 86020
  0.0 12.8 %copy-start.4 = (f32[1,4096]{1,0:T(1,128)S(1)}, f32[1,4096]{1,0:T(1,128)}, u32[]{:S(2)}) copy-start(f32[1,4096]{1,0:T(1,128)} %refs_9_.1) | copy-start | bytes 49156
  0.0 12.8 %copy-start.5 = (s32[1,160]{1,0:T(1,128)S(1)}, s32[1,160]{1,0:T(1,128)}, u32[]{:S(2)}) copy-start(s32[1,160]{1,0:T(1,128)} %refs_7_.1) | copy-start | bytes 1924
  0.0 14.9 %slice-start.1 = ((s8[12845056]{0:T(1024)(128)(4,1)}), s8[4194304]{0:T(1024)(128)(4,1)S(1)}, s32[]{:S(2)}) async-start(s8[12845056]{0:T(1024)(128)(4,1)} %bitcast.12), calls=%async_computation.1 | async-start | bytes 8388608
  0.0 14.9 %slice-start.2 = ((s8[12845056]{0:T(1024)(128)(4,1)}), s8[4194304]{0:T(1024)(128)(4,1)S(1)}, s32[]{:S(2)}) async-start(s8[12845056]{0:T(1024)(128)(4,1)} %bitcast.12), calls=%async_computation.2 | async-start | bytes 8388608
  0.0 14.9 %slice-start.3 = ((s8[12845056]{0:T(1024)(128)(4,1)}), s8[262144]{0:T(1024)(128)(4,1)S(1)}, s32[]{:S(2)}) async-start(s8[12845056]{0:T(1024)(128)(4,1)} %bitcast.12), calls=%async_computation.3 | async-start | bytes 524288
  0.1 14.9 %copy-start.2 = (bf16[1,4096,512]{2,1,0:T(8,128)(2,1)S(1)}, bf16[1,4096,512]{2,1,0:T(8,128)(2,1)}, u32[]{:S(2)}) copy-start(bf16[1,4096,512]{2,1,0:T(8,128)(2,1)} %param.15) | copy-start | bytes 12582916
  1.0 5.7 %collective-permute-start = (bf16[1,2,11264]{2,1,0:T(2,128)(2,1)S(1)}, bf16[1,2,11264]{2,1,0:T(2,128)(2,1)S(1)}, u32[]{:S(2)}, u32[]{:S(2)}) collective-permute-start(bf16[1,2,11264]{2,1,0:T(2,128)(2,1)S(1)} %bitcast.19), channel_id=1, source_target_pairs={{0,4},{2,6},{4,0},{6,2},{8,12},{10,14},{12,8},{14,10},{1,5},{3,7},... | collective-permute-start | bytes 135176 | tf_op jit(solution)/shard_map/ppermute | solution.py:47
  4.1 6.7 %collective-permute-start.1 = (bf16[1,2,11264]{2,1,0:T(2,128)(2,1)S(1)}, bf16[1,2,11264]{2,1,0:T(2,128)(2,1)S(1)}, u32[]{:S(2)}, u32[]{:S(2)}) collective-permute-start(bf16[1,2,11264]{2,1,0:T(2,128)(2,1)S(1)} %bitcast.20), channel_id=1, source_target_pairs={{0,8},{2,10},{4,12},{6,14},{8,0},{10,2},{12,4},{14,6},{1,9},{3,11}... | collective-permute-start | bytes 135176 | tf_op jit(solution)/shard_map/ppermute | solution.py:47
  6.8 8.1 %collective-permute-start.2 = (bf16[2,2,11264]{2,1,0:T(2,128)(2,1)S(1)}, bf16[2,2,11264]{2,1,0:T(2,128)(2,1)S(1)}, u32[]{:S(2)}, u32[]{:S(2)}) collective-permute-start(bf16[2,2,11264]{2,1,0:T(2,128)(2,1)S(1)} %pad_maximum_fusion), channel_id=1, source_target_pairs={{0,10},{2,8},{4,14},{6,12},{8,2},{10,0},{12,6},{14,4},{1,11},{3,9}... | collective-permute-start | bytes 270344 | tf_op jit(solution)/shard_map/ppermute | solution.py:47
  10.3 4.7 %collective-permute-start.3 = (bf16[2,2,11264]{2,1,0:T(2,128)(2,1)S(1)}, bf16[2,2,11264]{2,1,0:T(2,128)(2,1)S(1)}, u32[]{:S(2)}, u32[]{:S(2)}) collective-permute-start(bf16[2,2,11264]{2,1,0:T(2,128)(2,1)S(1)} %pad_maximum_fusion), channel_id=1, source_target_pairs={{0,2},{2,0},{4,6},{6,4},{8,10},{10,8},{12,14},{14,12},{1,3},{3,1},... | collective-permute-start | bytes 270344 | tf_op jit(solution)/shard_map/ppermute | solution.py:47
  10.8 4.1 %collective-permute-start.4 = (bf16[1,2,11264]{2,1,0:T(2,128)(2,1)S(1)}, bf16[1,2,11264]{2,1,0:T(2,128)(2,1)S(1)}, u32[]{:S(2)}, u32[]{:S(2)}) collective-permute-start(bf16[1,2,11264]{2,1,0:T(2,128)(2,1)S(1)} %collective-permute-done.1.refs_2_), channel_id=1, source_target_pairs={{0,4},{2,6},{4,0},{6,2},{8,12},{10,14},{12,8},{14,10},{1,5},{3,7},... | collective-permute-start | bytes 135176 | tf_op jit(solution)/shard_map/ppermute | solution.py:47
  15.0 11.6 %copy-start.6 = (s32[16]{0:T(128)S(1)}, s32[16]{0:T(128)}, u32[]{:S(2)}) copy-start(s32[16]{0:T(128)} %param.18) | copy-start | bytes 196
  17.6 4.1 %collective-permute-start.5 = (bf16[1,16,1408]{2,1,0:T(8,128)(2,1)S(1)}, bf16[1,16,1408]{2,1,0:T(8,128)(2,1)S(1)}, u32[]{:S(2)}, u32[]{:S(2)}) collective-permute-start(bf16[1,16,1408]{2,1,0:T(8,128)(2,1)S(1)} %rotate.1.refs_0_), channel_id=1, source_target_pairs={{0,4},{2,6},{4,0},{6,2},{8,12},{10,14},{12,8},{14,10},{1,5},{3,7},... | collective-permute-start | bytes 135176 | tf_op jit(solution)/shard_map/ppermute | solution.py:47
  19.6 6.5 %collective-permute-start.8 = (bf16[1,16,1408]{2,1,0:T(8,128)(2,1)S(1)}, bf16[1,16,1408]{2,1,0:T(8,128)(2,1)S(1)}, u32[]{:S(2)}, u32[]{:S(2)}) collective-permute-start(bf16[1,16,1408]{2,1,0:T(8,128)(2,1)S(1)} %rotate.1.refs_0_), channel_id=1, source_target_pairs={{0,8},{2,10},{4,12},{6,14},{8,0},{10,2},{12,4},{14,6},{1,9},{3,11}... | collective-permute-start | bytes 135176 | tf_op jit(solution)/shard_map/ppermute | solution.py:47
  21.7 8.4 %collective-permute-start.6 = (bf16[2,16,1408]{2,1,0:T(8,128)(2,1)S(1)}, bf16[2,16,1408]{2,1,0:T(8,128)(2,1)S(1)}, u32[]{:S(2)}, u32[]{:S(2)}) collective-permute-start(bf16[2,16,1408]{2,1,0:T(8,128)(2,1)S(1)} %pad_maximum_fusion.1), channel_id=1, source_target_pairs={{0,10},{2,8},{4,14},{6,12},{8,2},{10,0},{12,6},{14,4},{1,11},{3,9}... | collective-permute-start | bytes 270344 | tf_op jit(solution)/shard_map/ppermute | solution.py:47
  23.8 6.3 %collective-permute-start.7 = (bf16[2,16,1408]{2,1,0:T(8,128)(2,1)S(1)}, bf16[2,16,1408]{2,1,0:T(8,128)(2,1)S(1)}, u32[]{:S(2)}, u32[]{:S(2)}) collective-permute-start(bf16[2,16,1408]{2,1,0:T(8,128)(2,1)S(1)} %pad_maximum_fusion.1), channel_id=1, source_target_pairs={{0,2},{2,0},{4,6},{6,4},{8,10},{10,8},{12,14},{14,12},{1,3},{3,1},... | collective-permute-start | bytes 270344 | tf_op jit(solution)/shard_map/ppermute | solution.py:47
  26.1 4.0 %collective-permute-start.9 = (bf16[1,16,1408]{2,1,0:T(8,128)(2,1)S(1)}, bf16[1,16,1408]{2,1,0:T(8,128)(2,1)S(1)}, u32[]{:S(2)}, u32[]{:S(2)}) collective-permute-start(bf16[1,16,1408]{2,1,0:T(8,128)(2,1)S(1)} %collective-permute-done.8.refs_2_), channel_id=1, source_target_pairs={{0,4},{2,6},{4,0},{6,2},{8,12},{10,14},{12,8},{14,10},{1,5},{3,7},... | collective-permute-start | bytes 135176 | tf_op jit(solution)/shard_map/ppermute | solution.py:47
  30.9 1.2 %collective-permute-start.10 = (f32[8,128]{1,0:T(8,128)S(1)}, f32[8,128]{1,0:T(8,128)S(1)}, u32[]{:S(2)}, u32[]{:S(2)}) collective-permute-start(f32[8,128]{1,0:T(8,128)S(1)} %scores.1.mine), channel_id=1, source_target_pairs={{0,1},{1,0},{2,3},{3,2},{4,5},{5,4},{6,7},{7,6},{8,9},{9,8},{10,11... | collective-permute-start | bytes 12296 | tf_op jit(solution)/shard_map/ppermute | solution.py:192

commit v3 on v2

--- a/solution.py
+++ b/solution.py
@@ -13,7 +13,7 @@
 LANES = 128
 MIB = 2**20
 X, Z, FAR = 1, 2, 4
-PLAN = [(Z, (0,)), (FAR, (0,)), (X ^ FAR, (0, Z)), (X, (0, Z)), (Z, (FAR,))]
+PLAN = [(X, (0,)), (FAR, (0,)), (Z ^ FAR, (0, X)), (Z, (0, X)), (X, (FAR,))]
 BY_LANES = (((1,), (1,)), ((), ()))
 
 
@@ -93,28 +93,15 @@
     hid_block = basis_h.shape[1]
     inp_block = basis_i.shape[1]
     me = lax.axis_index("ex")
-    own_tokens = parts[0].shape[1]
-    rows = tokens.shape[0]
-    column = lax.broadcasted_iota(jnp.int32, (rows, rows), 1)
-    device_of = jnp.zeros((rows, rows), jnp.int32)
-    at = 0
     for part, of_part in zip(parts, masks):
         for i, mask in enumerate(of_part):
-            tokens[pl.ds(at, own_tokens), :] = part[i].astype(jnp.float32)
-            device_of = jnp.where(column // own_tokens == at // own_tokens, me ^ mask, device_of)
-            at += own_tokens
-    token = lax.broadcasted_iota(jnp.int32, (rows, rows), 0)
-    order = (token == device_of * own_tokens + column % own_tokens).astype(jnp.bfloat16)
+            tokens[me ^ mask] = part[i]
 
     def rotate(lanes, basis, eig, block, to):
-        product = jnp.dot(
-            tokens[:, lanes].astype(jnp.bfloat16), basis[...], preferred_element_type=jnp.float32
-        )
+        in_order = jnp.concatenate([tokens[k, :, lanes] for k in range(tokens.shape[0])], axis=0)
+        product = jnp.dot(in_order, basis[...], preferred_element_type=jnp.float32)
         at = pl.ds(pl.multiple_of(me * block, LANES), block)
-        rotated = (product * (1.0 / (eig[:, at] + DAMP))).astype(jnp.bfloat16)
-        out[0, :, to] = jnp.dot(order, rotated, preferred_element_type=jnp.float32).astype(
-            jnp.bfloat16
-        )
+        out[0, :, to] = (product * (1.0 / (eig[:, at] + DAMP))).astype(jnp.bfloat16)
 
     rotate(slice(0, width_h), basis_h, eig_h, hid_block, slice(0, hid_block))
     rotate(slice(width_h, None), basis_i, eig_i, inp_block, slice(hid_block, None))
@@ -244,7 +231,7 @@
         jax.ShapeDtypeStruct((1, tokens, hid_block + inp_block), jnp.bfloat16),
         flops=2 * 16 * 8_500_000,
         moved=17_000_000,
-        scratch_shapes=[pltpu.VMEM((tokens, width), jnp.float32)],
+        scratch_shapes=[pltpu.VMEM((shards, own_tokens, width), jnp.bfloat16)],
     )(*everyone, basis_h, basis_i, eig_h, eig_i, own_self)
     parts, masks = gather(rotated[0], shards)
     first = 3

time: 33 us -> 31.7 us (0.961)
  starting transfers between devices: 18.5 us -> 15.7 us
  waiting for transfers between devices: 7.05 us -> 8.81 us
    ppermute x10, starting transfers between devices: 18.5 us -> 15.7 us  [gather(): lax.ppermute(joined[sent], 'ex', [(i, i ^ mask) for i in range(shards)])]
    ppermute x10, waiting for transfers between devices: 5.89 us -> 7.65 us  [gather(): lax.ppermute(joined[sent], 'ex', [(i, i ^ mask) for i in range(shards)])]
  transfers between devices with their start and end apart: 11 -> 11, of which waited for: 5 -> 7; matrix products, arithmetic and copies ran while one was open for 0% -> 0% of each run, Pallas kernels for 6% -> 6%
where the time goes in v3:
time: 31.7 us; the launch traced here: 31.5 us
  starting transfers between devices  15.7 us (50%)
  waiting for transfers between devices  8.81 us (28%)
  Pallas kernels  6.64 us (21%)
    ppermute x10, starting transfers between devices, gather(): lax.ppermute(joined[sent], 'ex', [(i, i ^ mask) for i in range(shards)])  15.7 us
    ppermute x10, waiting for transfers between devices, gather(): lax.ppermute(joined[sent], 'ex', [(i, i ^ mask) for i in range(shards)])  7.65 us
    pallas_call x1, Pallas kernels, body(): call(functools.partial(rotate_kernel, masks), 'rotate', jax.ShapeDtypeStr...  2.35 us
    pallas_call x1, Pallas kernels, body(): call(self_kernel, 'self_influence', small, flops=2 * 160 * 160 * 11264, m...  1.41 us
    ppermute x1, waiting for transfers between devices, layer_swap(): return lax.ppermute(x, 'layer', [(0, 1), (1, 0)])  1.16 us
    pallas_call x1, Pallas kernels, body(): call(join_kernel, 'join', pltpu.VMEM((own_tokens, width), jnp.bfloat16),...  0.92 us
    pallas_call x1, Pallas kernels, body(): call(functools.partial(late_kernel, masks[first:]), 'scores', small)  0.83 us
    pallas_call x1, Pallas kernels, body(): call(finish_kernel, 'finish', jax.ShapeDtypeStruct((E_DEV, QUERIES // 2),...  0.65 us
  transfers between devices with their start and end apart: 11, of which 7 were waited for; matrix products, arithmetic and copies ran while one was open for 0% of the time, Pallas kernels for 6%

profile of v3, /device:TPU:0, one launch (start us, length us, event | category | flops | bytes accessed | tf_op | source)
XLA Modules:
  0.0 31.5 jit_solution(9137289872173163875)
XLA Ops:
  0.0 0.0 slice-start.1
  0.0 0.0 slice-start.2
  0.0 0.0 slice-start.3
  0.1 0.9 %join.1 = bf16[2,11264]{1,0:T(2,128)(2,1)S(1)} custom-call(bf16[2,7168]{1,0:T(2,128)(2,1)} %bitcast.24, bf16[2,4096]{1,0:T(2,128)(2,1)} %bitcast.25), custom_call_target="tpu_custom_call" | custom-call | flops 20000000000 | tf_op jit(solution)/shard_map/join/pallas_call | solution.py:214
  1.0 3.0 %collective-permute-start = (bf16[1,2,11264]{2,1,0:T(2,128)(2,1)S(1)}, bf16[1,2,11264]{2,1,0:T(2,128)(2,1)S(1)}, u32[]{:S(2)}, u32[]{:S(2)}) collective-permute-start(bf16[1,2,11264]{2,1,0:T(2,128)(2,1)S(1)} %bitcast.19), channel_id=1, source_target_pairs={{0,2},{2,0},{4,6},{6,4},{8,10},{10,8},{12,14},{14,12},{1,3},{3,1},... | collective-permute-start | bytes 135176 | tf_op jit(solution)/shard_map/ppermute | solution.py:47
  4.0 2.6 %collective-permute-start.1 = (bf16[1,2,11264]{2,1,0:T(2,128)(2,1)S(1)}, bf16[1,2,11264]{2,1,0:T(2,128)(2,1)S(1)}, u32[]{:S(2)}, u32[]{:S(2)}) collective-permute-start(bf16[1,2,11264]{2,1,0:T(2,128)(2,1)S(1)} %bitcast.20), channel_id=1, source_target_pairs={{0,8},{2,10},{4,12},{6,14},{8,0},{10,2},{12,4},{14,6},{1,9},{3,11}... | collective-permute-start | bytes 135176 | tf_op jit(solution)/shard_map/ppermute | solution.py:47
  6.6 0.0 collective-permute-done.refs_1_
  6.6 0.1 pad_maximum_fusion
  6.7 3.6 %collective-permute-start.2 = (bf16[2,2,11264]{2,1,0:T(2,128)(2,1)S(1)}, bf16[2,2,11264]{2,1,0:T(2,128)(2,1)S(1)}, u32[]{:S(2)}, u32[]{:S(2)}) collective-permute-start(bf16[2,2,11264]{2,1,0:T(2,128)(2,1)S(1)} %pad_maximum_fusion), channel_id=1, source_target_pairs={{0,12},{2,14},{4,8},{6,10},{8,4},{10,6},{12,0},{14,2},{1,13},{3,15... | collective-permute-start | bytes 270344 | tf_op jit(solution)/shard_map/ppermute | solution.py:47
  10.4 0.0 collective-permute-start.3
  10.4 1.5 %collective-permute-start.4 = (bf16[1,2,11264]{2,1,0:T(2,128)(2,1)S(1)}, bf16[1,2,11264]{2,1,0:T(2,128)(2,1)S(1)}, u32[]{:S(2)}, u32[]{:S(2)}) collective-permute-start(bf16[1,2,11264]{2,1,0:T(2,128)(2,1)S(1)} %collective-permute-done.1.refs_2_), channel_id=1, source_target_pairs={{0,2},{2,0},{4,6},{6,4},{8,10},{10,8},{12,14},{14,12},{1,3},{3,1},... | collective-permute-start | bytes 135176 | tf_op jit(solution)/shard_map/ppermute | solution.py:47
  11.9 1.4 %self_influence.1.refs_10_.refs_8_ = f32[8,128]{1,0:T(8,128)S(1)} custom-call(bf16[160,7168]{1,0:T(8,128)(2,1)S(1)} %bitcast.9, bf16[160,4096]{1,0:T(8,128)(2,1)S(1)} %bitcast.15, f32[1,7168]{1,0:T(1,128)S(1)} %copy-done.3, f32[1,4096]{1,0:T(1,128)S(1)} %copy-done.4, s32[1,160]{1,0:T(1,128)S(1)} %copy-done.5), custom_call_target="tpu_custom_call" | custom-call | flops 576716800 | bytes 3700000 | tf_op jit(solution)/shard_map/self_influence/pallas_call | solution.py:225
  13.3 1.1 %collective-permute-done.4.refs_5_ = bf16[1,2,11264]{2,1,0:T(2,128)(2,1)S(1)} collective-permute-done((bf16[1,2,11264]{2,1,0:T(2,128)(2,1)S(1)}, bf16[1,2,11264]{2,1,0:T(2,128)(2,1)S(1)}, u32[]{:S(2)}, u32[]{:S(2)}) %collective-permute-start.4) | collective-permute-done | bytes 45088 | tf_op jit(solution)/shard_map/ppermute | solution.py:47
  14.4 0.0 collective-permute-done.2.refs_3_
  14.4 0.5 %collective-permute-done.3.refs_4_ = bf16[2,2,11264]{2,1,0:T(2,128)(2,1)S(1)} collective-permute-done((bf16[2,2,11264]{2,1,0:T(2,128)(2,1)S(1)}, bf16[2,2,11264]{2,1,0:T(2,128)(2,1)S(1)}, u32[]{:S(2)}, u32[]{:S(2)}) %collective-permute-start.3) | collective-permute-done | bytes 90144 | tf_op jit(solution)/shard_map/ppermute | solution.py:47
  14.9 0.0 copy-start.6
  14.9 2.3 %rotate.1.refs_0_ = bf16[1,16,1408]{2,1,0:T(8,128)(2,1)S(1)} custom-call(bf16[1,2,11264]{2,1,0:T(2,128)(2,1)S(1)} %bitcast.22, bf16[1,2,11264]{2,1,0:T(2,128)(2,1)S(1)} %collective-permute-done.refs_1_, bf16[1,2,11264]{2,1,0:T(2,128)(2,1)S(1)} %collective-permute-done.1.refs_2_, bf16[2,2,11264]{2,1,0:T(2,128)(2,1)S(1)} %collective-permute-done.2.refs_3_, ...), custom_call_target="tpu_custom_call" | custom-call | flops 272000000 | bytes 17000000 | tf_op jit(solution)/shard_map/rotate/pallas_call | solution.py:228
  17.3 1.5 %collective-permute-start.5 = (bf16[1,16,1408]{2,1,0:T(8,128)(2,1)S(1)}, bf16[1,16,1408]{2,1,0:T(8,128)(2,1)S(1)}, u32[]{:S(2)}, u32[]{:S(2)}) collective-permute-start(bf16[1,16,1408]{2,1,0:T(8,128)(2,1)S(1)} %rotate.1.refs_0_), channel_id=1, source_target_pairs={{0,2},{2,0},{4,6},{6,4},{8,10},{10,8},{12,14},{14,12},{1,3},{3,1},... | collective-permute-start | bytes 135176 | tf_op jit(solution)/shard_map/ppermute | solution.py:47
  18.8 0.3 %collective-permute-start.8 = (bf16[1,16,1408]{2,1,0:T(8,128)(2,1)S(1)}, bf16[1,16,1408]{2,1,0:T(8,128)(2,1)S(1)}, u32[]{:S(2)}, u32[]{:S(2)}) collective-permute-start(bf16[1,16,1408]{2,1,0:T(8,128)(2,1)S(1)} %rotate.1.refs_0_), channel_id=1, source_target_pairs={{0,8},{2,10},{4,12},{6,14},{8,0},{10,2},{12,4},{14,6},{1,9},{3,11}... | collective-permute-start | bytes 135176 | tf_op jit(solution)/shard_map/ppermute | solution.py:47
  19.1 2.2 %collective-permute-done.5.refs_1_ = bf16[1,16,1408]{2,1,0:T(8,128)(2,1)S(1)} collective-permute-done((bf16[1,16,1408]{2,1,0:T(8,128)(2,1)S(1)}, bf16[1,16,1408]{2,1,0:T(8,128)(2,1)S(1)}, u32[]{:S(2)}, u32[]{:S(2)}) %collective-permute-start.5) | collective-permute-done | bytes 45088 | tf_op jit(solution)/shard_map/ppermute | solution.py:47
  21.4 2.7 %collective-permute-start.6 = (bf16[2,16,1408]{2,1,0:T(8,128)(2,1)S(1)}, bf16[2,16,1408]{2,1,0:T(8,128)(2,1)S(1)}, u32[]{:S(2)}, u32[]{:S(2)}) collective-permute-start(bf16[2,16,1408]{2,1,0:T(8,128)(2,1)S(1)} %pad_maximum_fusion.1), channel_id=1, source_target_pairs={{0,12},{2,14},{4,8},{6,10},{8,4},{10,6},{12,0},{14,2},{1,13},{3,15... | collective-permute-start | bytes 270344 | tf_op jit(solution)/shard_map/ppermute | solution.py:47
  24.1 0.0 collective-permute-start.7
  24.1 0.2 collective-permute-done.8.refs_2_
  24.3 0.5 %collective-permute-start.9 = (bf16[1,16,1408]{2,1,0:T(8,128)(2,1)S(1)}, bf16[1,16,1408]{2,1,0:T(8,128)(2,1)S(1)}, u32[]{:S(2)}, u32[]{:S(2)}) collective-permute-start(bf16[1,16,1408]{2,1,0:T(8,128)(2,1)S(1)} %collective-permute-done.8.refs_2_), channel_id=1, source_target_pairs={{0,2},{2,0},{4,6},{6,4},{8,10},{10,8},{12,14},{14,12},{1,3},{3,1},... | collective-permute-start | bytes 135176 | tf_op jit(solution)/shard_map/ppermute | solution.py:47
  24.7 0.5 %early_grams.1 = (f32[2,16,160]{2,1,0:T(8,128)S(1)}, f32[16,128]{1,0:T(8,128)S(1)}) custom-call(bf16[1,16,1408]{2,1,0:T(8,128)(2,1)S(1)} %rotate.1.refs_0_, bf16[1,16,1408]{2,1,0:T(8,128)(2,1)S(1)} %collective-permute-done.5.refs_1_, bf16[1,16,1408]{2,1,0:T(8,128)(2,1)S(1)} %collective-permute-done.8.refs_2_, bf16[160,7168]{1,0:T(8,128)(2,1)S(1)} %bitcast.10, ...), custom_call_target="tpu_custom_call" | custom-call | flops 500000000 | tf_op jit(solution)/shard_map/early_grams/pallas_call | solution.py:238
  25.2 3.1 %collective-permute-done.9.refs_2_ = bf16[1,16,1408]{2,1,0:T(8,128)(2,1)S(1)} collective-permute-done((bf16[1,16,1408]{2,1,0:T(8,128)(2,1)S(1)}, bf16[1,16,1408]{2,1,0:T(8,128)(2,1)S(1)}, u32[]{:S(2)}, u32[]{:S(2)}) %collective-permute-start.9) | collective-permute-done | bytes 45088 | tf_op jit(solution)/shard_map/ppermute | solution.py:47
  28.3 0.0 collective-permute-done.6.refs_0_
  28.3 0.5 %collective-permute-done.7.refs_1_ = bf16[2,16,1408]{2,1,0:T(8,128)(2,1)S(1)} collective-permute-done((bf16[2,16,1408]{2,1,0:T(8,128)(2,1)S(1)}, bf16[2,16,1408]{2,1,0:T(8,128)(2,1)S(1)}, u32[]{:S(2)}, u32[]{:S(2)}) %collective-permute-start.7) | collective-permute-done | bytes 90144 | tf_op jit(solution)/shard_map/ppermute | solution.py:47
  28.8 0.8 %scores.1.mine = f32[8,128]{1,0:T(8,128)S(1)} custom-call(bf16[2,16,1408]{2,1,0:T(8,128)(2,1)S(1)} %collective-permute-done.6.refs_0_, bf16[2,16,1408]{2,1,0:T(8,128)(2,1)S(1)} %collective-permute-done.7.refs_1_, bf16[1,16,1408]{2,1,0:T(8,128)(2,1)S(1)} %collective-permute-done.9.refs_2_, bf16[160,7168]{1,0:T(8,128)(2,1)S(1)} %bitcast.11, ...), custom_call_target="tpu_custom_call" | custom-call | tf_op jit(solution)/shard_map/scores/pallas_call | solution.py:247
  29.7 0.0 collective-permute-start.10
  29.7 1.2 %collective-permute-done.10.other = f32[8,128]{1,0:T(8,128)S(1)} collective-permute-done((f32[8,128]{1,0:T(8,128)S(1)}, f32[8,128]{1,0:T(8,128)S(1)}, u32[]{:S(2)}, u32[]{:S(2)}) %collective-permute-start.10) | collective-permute-done | bytes 4128 | tf_op jit(solution)/shard_map/ppermute | solution.py:179
  30.8 0.6 %finish.1 = f32[2,4]{1,0:T(2,128)} custom-call(f32[8,128]{1,0:T(8,128)S(1)} %scores.1.mine, f32[8,128]{1,0:T(8,128)S(1)} %collective-permute-done.10.other), custom_call_target="tpu_custom_call" | custom-call | tf_op jit(solution)/shard_map/finish/pallas_call | solution.py:250
  (21 shorter events, 0.1 us)
Async XLA Ops:
  0.0 14.9 %slice-start = ((s8[12845056]{0:T(1024)(128)(4,1)}), s8[4194304]{0:T(1024)(128)(4,1)S(1)}, s32[]{:S(2)}) async-start(s8[12845056]{0:T(1024)(128)(4,1)} %bitcast.12), calls=%async_computation | async-start | bytes 8388608
  0.0 11.9 %copy-start = (bf16[1,160,7168]{2,1,0:T(8,128)(2,1)S(1)}, bf16[1,160,7168]{2,1,0:T(8,128)(2,1)}, u32[]{:S(2)}) copy-start(bf16[1,160,7168]{2,1,0:T(8,128)(2,1)} %param.12) | copy-start | bytes 6881284
  0.0 11.9 %copy-start.1 = (bf16[1,160,4096]{2,1,0:T(8,128)(2,1)S(1)}, bf16[1,160,4096]{2,1,0:T(8,128)(2,1)}, u32[]{:S(2)}) copy-start(bf16[1,160,4096]{2,1,0:T(8,128)(2,1)} %param.13) | copy-start | bytes 3932164
  0.0 11.9 %copy-start.3 = (f32[1,7168]{1,0:T(1,128)S(1)}, f32[1,7168]{1,0:T(1,128)}, u32[]{:S(2)}) copy-start(f32[1,7168]{1,0:T(1,128)} %refs_8_.1) | copy-start | bytes 86020
  0.0 11.9 %copy-start.4 = (f32[1,4096]{1,0:T(1,128)S(1)}, f32[1,4096]{1,0:T(1,128)}, u32[]{:S(2)}) copy-start(f32[1,4096]{1,0:T(1,128)} %refs_9_.1) | copy-start | bytes 49156
  0.0 11.9 %copy-start.5 = (s32[1,160]{1,0:T(1,128)S(1)}, s32[1,160]{1,0:T(1,128)}, u32[]{:S(2)}) copy-start(s32[1,160]{1,0:T(1,128)} %refs_7_.1) | copy-start | bytes 1924
  0.0 14.9 %slice-start.1 = ((s8[12845056]{0:T(1024)(128)(4,1)}), s8[4194304]{0:T(1024)(128)(4,1)S(1)}, s32[]{:S(2)}) async-start(s8[12845056]{0:T(1024)(128)(4,1)} %bitcast.12), calls=%async_computation.1 | async-start | bytes 8388608
  0.0 14.9 %slice-start.2 = ((s8[12845056]{0:T(1024)(128)(4,1)}), s8[4194304]{0:T(1024)(128)(4,1)S(1)}, s32[]{:S(2)}) async-start(s8[12845056]{0:T(1024)(128)(4,1)} %bitcast.12), calls=%async_computation.2 | async-start | bytes 8388608
  0.0 14.9 %slice-start.3 = ((s8[12845056]{0:T(1024)(128)(4,1)}), s8[262144]{0:T(1024)(128)(4,1)S(1)}, s32[]{:S(2)}) async-start(s8[12845056]{0:T(1024)(128)(4,1)} %bitcast.12), calls=%async_computation.3 | async-start | bytes 524288
  0.1 14.9 %copy-start.2 = (bf16[1,4096,512]{2,1,0:T(8,128)(2,1)S(1)}, bf16[1,4096,512]{2,1,0:T(8,128)(2,1)}, u32[]{:S(2)}) copy-start(bf16[1,4096,512]{2,1,0:T(8,128)(2,1)} %param.15) | copy-start | bytes 12582916
  1.0 5.6 %collective-permute-start = (bf16[1,2,11264]{2,1,0:T(2,128)(2,1)S(1)}, bf16[1,2,11264]{2,1,0:T(2,128)(2,1)S(1)}, u32[]{:S(2)}, u32[]{:S(2)}) collective-permute-start(bf16[1,2,11264]{2,1,0:T(2,128)(2,1)S(1)} %bitcast.19), channel_id=1, source_target_pairs={{0,2},{2,0},{4,6},{6,4},{8,10},{10,8},{12,14},{14,12},{1,3},{3,1},... | collective-permute-start | bytes 135176 | tf_op jit(solution)/shard_map/ppermute | solution.py:47
  4.0 6.4 %collective-permute-start.1 = (bf16[1,2,11264]{2,1,0:T(2,128)(2,1)S(1)}, bf16[1,2,11264]{2,1,0:T(2,128)(2,1)S(1)}, u32[]{:S(2)}, u32[]{:S(2)}) collective-permute-start(bf16[1,2,11264]{2,1,0:T(2,128)(2,1)S(1)} %bitcast.20), channel_id=1, source_target_pairs={{0,8},{2,10},{4,12},{6,14},{8,0},{10,2},{12,4},{14,6},{1,9},{3,11}... | collective-permute-start | bytes 135176 | tf_op jit(solution)/shard_map/ppermute | solution.py:47
  6.7 7.7 %collective-permute-start.2 = (bf16[2,2,11264]{2,1,0:T(2,128)(2,1)S(1)}, bf16[2,2,11264]{2,1,0:T(2,128)(2,1)S(1)}, u32[]{:S(2)}, u32[]{:S(2)}) collective-permute-start(bf16[2,2,11264]{2,1,0:T(2,128)(2,1)S(1)} %pad_maximum_fusion), channel_id=1, source_target_pairs={{0,12},{2,14},{4,8},{6,10},{8,4},{10,6},{12,0},{14,2},{1,13},{3,15... | collective-permute-start | bytes 270344 | tf_op jit(solution)/shard_map/ppermute | solution.py:47
  10.4 4.5 %collective-permute-start.3 = (bf16[2,2,11264]{2,1,0:T(2,128)(2,1)S(1)}, bf16[2,2,11264]{2,1,0:T(2,128)(2,1)S(1)}, u32[]{:S(2)}, u32[]{:S(2)}) collective-permute-start(bf16[2,2,11264]{2,1,0:T(2,128)(2,1)S(1)} %pad_maximum_fusion), channel_id=1, source_target_pairs={{0,4},{2,6},{4,0},{6,2},{8,12},{10,14},{12,8},{14,10},{1,5},{3,7},... | collective-permute-start | bytes 270344 | tf_op jit(solution)/shard_map/ppermute | solution.py:47
  10.4 4.0 %collective-permute-start.4 = (bf16[1,2,11264]{2,1,0:T(2,128)(2,1)S(1)}, bf16[1,2,11264]{2,1,0:T(2,128)(2,1)S(1)}, u32[]{:S(2)}, u32[]{:S(2)}) collective-permute-start(bf16[1,2,11264]{2,1,0:T(2,128)(2,1)S(1)} %collective-permute-done.1.refs_2_), channel_id=1, source_target_pairs={{0,2},{2,0},{4,6},{6,4},{8,10},{10,8},{12,14},{14,12},{1,3},{3,1},... | collective-permute-start | bytes 135176 | tf_op jit(solution)/shard_map/ppermute | solution.py:47
  14.9 9.8 %copy-start.6 = (s32[16]{0:T(128)S(1)}, s32[16]{0:T(128)}, u32[]{:S(2)}) copy-start(s32[16]{0:T(128)} %param.18) | copy-start | bytes 196
  17.3 4.1 %collective-permute-start.5 = (bf16[1,16,1408]{2,1,0:T(8,128)(2,1)S(1)}, bf16[1,16,1408]{2,1,0:T(8,128)(2,1)S(1)}, u32[]{:S(2)}, u32[]{:S(2)}) collective-permute-start(bf16[1,16,1408]{2,1,0:T(8,128)(2,1)S(1)} %rotate.1.refs_0_), channel_id=1, source_target_pairs={{0,2},{2,0},{4,6},{6,4},{8,10},{10,8},{12,14},{14,12},{1,3},{3,1},... | collective-permute-start | bytes 135176 | tf_op jit(solution)/shard_map/ppermute | solution.py:47
  18.8 5.5 %collective-permute-start.8 = (bf16[1,16,1408]{2,1,0:T(8,128)(2,1)S(1)}, bf16[1,16,1408]{2,1,0:T(8,128)(2,1)S(1)}, u32[]{:S(2)}, u32[]{:S(2)}) collective-permute-start(bf16[1,16,1408]{2,1,0:T(8,128)(2,1)S(1)} %rotate.1.refs_0_), channel_id=1, source_target_pairs={{0,8},{2,10},{4,12},{6,14},{8,0},{10,2},{12,4},{14,6},{1,9},{3,11}... | collective-permute-start | bytes 135176 | tf_op jit(solution)/shard_map/ppermute | solution.py:47
  21.4 7.0 %collective-permute-start.6 = (bf16[2,16,1408]{2,1,0:T(8,128)(2,1)S(1)}, bf16[2,16,1408]{2,1,0:T(8,128)(2,1)S(1)}, u32[]{:S(2)}, u32[]{:S(2)}) collective-permute-start(bf16[2,16,1408]{2,1,0:T(8,128)(2,1)S(1)} %pad_maximum_fusion.1), channel_id=1, source_target_pairs={{0,12},{2,14},{4,8},{6,10},{8,4},{10,6},{12,0},{14,2},{1,13},{3,15... | collective-permute-start | bytes 270344 | tf_op jit(solution)/shard_map/ppermute | solution.py:47
  24.1 4.8 %collective-permute-start.7 = (bf16[2,16,1408]{2,1,0:T(8,128)(2,1)S(1)}, bf16[2,16,1408]{2,1,0:T(8,128)(2,1)S(1)}, u32[]{:S(2)}, u32[]{:S(2)}) collective-permute-start(bf16[2,16,1408]{2,1,0:T(8,128)(2,1)S(1)} %pad_maximum_fusion.1), channel_id=1, source_target_pairs={{0,4},{2,6},{4,0},{6,2},{8,12},{10,14},{12,8},{14,10},{1,5},{3,7},... | collective-permute-start | bytes 270344 | tf_op jit(solution)/shard_map/ppermute | solution.py:47
  24.3 4.0 %collective-permute-start.9 = (bf16[1,16,1408]{2,1,0:T(8,128)(2,1)S(1)}, bf16[1,16,1408]{2,1,0:T(8,128)(2,1)S(1)}, u32[]{:S(2)}, u32[]{:S(2)}) collective-permute-start(bf16[1,16,1408]{2,1,0:T(8,128)(2,1)S(1)} %collective-permute-done.8.refs_2_), channel_id=1, source_target_pairs={{0,2},{2,0},{4,6},{6,4},{8,10},{10,8},{12,14},{14,12},{1,3},{3,1},... | collective-permute-start | bytes 135176 | tf_op jit(solution)/shard_map/ppermute | solution.py:47
  29.7 1.2 %collective-permute-start.10 = (f32[8,128]{1,0:T(8,128)S(1)}, f32[8,128]{1,0:T(8,128)S(1)}, u32[]{:S(2)}, u32[]{:S(2)}) collective-permute-start(f32[8,128]{1,0:T(8,128)S(1)} %scores.1.mine), channel_id=1, source_target_pairs={{0,1},{1,0},{2,3},{3,2},{4,5},{5,4},{6,7},{7,6},{8,9},{9,8},{10,11... | collective-permute-start | bytes 12296 | tf_op jit(solution)/shard_map/ppermute | solution.py:179

commit v4 on v3

--- a/solution.py
+++ b/solution.py
@@ -139,6 +139,12 @@
     own_id = jnp.sum(own_id.astype(jnp.float32), axis=1, keepdims=True)
     query = lax.broadcasted_iota(jnp.int32, query_hot.shape, 1).astype(jnp.float32)
     query_hot[...] = (own_id == query).astype(jnp.float32)
+
+
+def more_kernel(masks, *refs):
+    parts = refs[:-4]
+    train_h, train_i, grams, out = refs[-4:]
+    out[0], out[1] = add_grams((grams[0], grams[1]), masks, parts, train_h, train_i)
 
 
 def late_kernel(masks, *refs):
@@ -234,18 +240,19 @@
         scratch_shapes=[pltpu.VMEM((shards, own_tokens, width), jnp.bfloat16)],
     )(*everyone, basis_h, basis_i, eig_h, eig_i, own_self)
     parts, masks = gather(rotated[0], shards)
-    first = 3
+    gram_shape = jax.ShapeDtypeStruct((2, tokens, train_h.shape[0]), jnp.float32)
+    first, last = 3, 4
     grams, query_hot = call(
         functools.partial(early_kernel, masks[:first]),
         "early_grams",
-        (
-            jax.ShapeDtypeStruct((2, tokens, train_h.shape[0]), jnp.float32),
-            jax.ShapeDtypeStruct((tokens, LANES), jnp.float32),
-        ),
+        (gram_shape, jax.ShapeDtypeStruct((tokens, LANES), jnp.float32)),
         flops=500_000_000,
     )(*parts[:first], train_h, train_i, query_ids)
-    mine = call(functools.partial(late_kernel, masks[first:]), "scores", small)(
-        *parts[first:], train_h, train_i, grams, query_hot, example_ids, own_self
+    grams = call(functools.partial(more_kernel, masks[first:last]), "more_grams", gram_shape, flops=300_000_000)(
+        *parts[first:last], train_h, train_i, grams
+    )
+    mine = call(functools.partial(late_kernel, masks[last:]), "scores", small)(
+        *parts[last:], train_h, train_i, grams, query_hot, example_ids, own_self
     )
     return call(
         finish_kernel,

time: 31.7 us -> 31.4 us (level)
  waiting for transfers between devices: 8.81 us -> 8.47 us
    ppermute x10, waiting for transfers between devices: 7.65 us -> 7.3 us  [gather(): lax.ppermute(joined[sent], 'ex', [(i, i ^ mask) for i in range(shards)])]
    pallas_call x2 -> x3, Pallas kernels: 1.32 us -> 1.4 us  [the longest x1 0.57 us: body(): call(functools.partial(late_kernel, masks[last:]), 'scores', small)]
  transfers between devices with their start and end apart: 11 -> 11, of which waited for: 7 -> 8; matrix products, arithmetic and copies ran while one was open for 0% -> 0% of each run, Pallas kernels for 6% -> 7%
where the time goes in v4:
time: 31.4 us; the launch traced here: 31.2 us
  starting transfers between devices  15.7 us (50%)
  waiting for transfers between devices  8.47 us (27%)
  Pallas kernels  6.73 us (21%)
    ppermute x10, starting transfers between devices, gather(): lax.ppermute(joined[sent], 'ex', [(i, i ^ mask) for i in range(shards)])  15.7 us
    ppermute x10, waiting for transfers between devices, gather(): lax.ppermute(joined[sent], 'ex', [(i, i ^ mask) for i in range(shards)])  7.3 us
    pallas_call x1, Pallas kernels, body(): call(functools.partial(rotate_kernel, masks), 'rotate', jax.ShapeDtypeStr...  2.35 us
    pallas_call x1, Pallas kernels, body(): call(self_kernel, 'self_influence', small, flops=2 * 160 * 160 * 11264, m...  1.41 us
    ppermute x1, waiting for transfers between devices, layer_swap(): return lax.ppermute(x, 'layer', [(0, 1), (1, 0)])  1.16 us
    pallas_call x1, Pallas kernels, body(): call(join_kernel, 'join', pltpu.VMEM((own_tokens, width), jnp.bfloat16),...  0.92 us
    pallas_call x1, Pallas kernels, body(): call(finish_kernel, 'finish', jax.ShapeDtypeStruct((E_DEV, QUERIES // 2),...  0.65 us
  transfers between devices with their start and end apart: 11, of which 8 were waited for; matrix products, arithmetic and copies ran while one was open for 0% of the time, Pallas kernels for 7%

profile of v4, /device:TPU:0, one launch (start us, length us, event | category | flops | bytes accessed | tf_op | source)
XLA Modules:
  0.0 31.2 jit_solution(2999889736770281330)
XLA Ops:
  0.0 0.0 slice-start.1
  0.0 0.0 slice-start.2
  0.0 0.0 slice-start.3
  0.1 0.9 %join.1 = bf16[2,11264]{1,0:T(2,128)(2,1)S(1)} custom-call(bf16[2,7168]{1,0:T(2,128)(2,1)} %bitcast.26, bf16[2,4096]{1,0:T(2,128)(2,1)} %bitcast.27), custom_call_target="tpu_custom_call" | custom-call | flops 20000000000 | tf_op jit(solution)/shard_map/join/pallas_call | solution.py:220
  1.0 3.0 %collective-permute-start = (bf16[1,2,11264]{2,1,0:T(2,128)(2,1)S(1)}, bf16[1,2,11264]{2,1,0:T(2,128)(2,1)S(1)}, u32[]{:S(2)}, u32[]{:S(2)}) collective-permute-start(bf16[1,2,11264]{2,1,0:T(2,128)(2,1)S(1)} %bitcast.21), channel_id=1, source_target_pairs={{0,2},{2,0},{4,6},{6,4},{8,10},{10,8},{12,14},{14,12},{1,3},{3,1},... | collective-permute-start | bytes 135176 | tf_op jit(solution)/shard_map/ppermute | solution.py:47
  4.0 2.6 %collective-permute-start.1 = (bf16[1,2,11264]{2,1,0:T(2,128)(2,1)S(1)}, bf16[1,2,11264]{2,1,0:T(2,128)(2,1)S(1)}, u32[]{:S(2)}, u32[]{:S(2)}) collective-permute-start(bf16[1,2,11264]{2,1,0:T(2,128)(2,1)S(1)} %bitcast.22), channel_id=1, source_target_pairs={{0,8},{2,10},{4,12},{6,14},{8,0},{10,2},{12,4},{14,6},{1,9},{3,11}... | collective-permute-start | bytes 135176 | tf_op jit(solution)/shard_map/ppermute | solution.py:47
  6.6 0.1 pad_maximum_fusion
  6.7 3.6 %collective-permute-start.2 = (bf16[2,2,11264]{2,1,0:T(2,128)(2,1)S(1)}, bf16[2,2,11264]{2,1,0:T(2,128)(2,1)S(1)}, u32[]{:S(2)}, u32[]{:S(2)}) collective-permute-start(bf16[2,2,11264]{2,1,0:T(2,128)(2,1)S(1)} %pad_maximum_fusion), channel_id=1, source_target_pairs={{0,12},{2,14},{4,8},{6,10},{8,4},{10,6},{12,0},{14,2},{1,13},{3,15... | collective-permute-start | bytes 270344 | tf_op jit(solution)/shard_map/ppermute | solution.py:47
  10.4 0.0 collective-permute-start.3
  10.4 0.0 collective-permute-done.1.refs_2_
  10.4 1.5 %collective-permute-start.4 = (bf16[1,2,11264]{2,1,0:T(2,128)(2,1)S(1)}, bf16[1,2,11264]{2,1,0:T(2,128)(2,1)S(1)}, u32[]{:S(2)}, u32[]{:S(2)}) collective-permute-start(bf16[1,2,11264]{2,1,0:T(2,128)(2,1)S(1)} %collective-permute-done.1.refs_2_), channel_id=1, source_target_pairs={{0,2},{2,0},{4,6},{6,4},{8,10},{10,8},{12,14},{14,12},{1,3},{3,1},... | collective-permute-start | bytes 135176 | tf_op jit(solution)/shard_map/ppermute | solution.py:47
  11.9 1.4 %self_influence.1.refs_10_.refs_7_ = f32[8,128]{1,0:T(8,128)S(1)} custom-call(bf16[160,7168]{1,0:T(8,128)(2,1)S(1)} %bitcast.9, bf16[160,4096]{1,0:T(8,128)(2,1)S(1)} %bitcast.13, f32[1,7168]{1,0:T(1,128)S(1)} %copy-done.3, f32[1,4096]{1,0:T(1,128)S(1)} %copy-done.4, s32[1,160]{1,0:T(1,128)S(1)} %copy-done.5), custom_call_target="tpu_custom_call" | custom-call | flops 576716800 | bytes 3700000 | tf_op jit(solution)/shard_map/self_influence/pallas_call | solution.py:231
  13.3 1.1 %collective-permute-done.4.refs_5_ = bf16[1,2,11264]{2,1,0:T(2,128)(2,1)S(1)} collective-permute-done((bf16[1,2,11264]{2,1,0:T(2,128)(2,1)S(1)}, bf16[1,2,11264]{2,1,0:T(2,128)(2,1)S(1)}, u32[]{:S(2)}, u32[]{:S(2)}) %collective-permute-start.4) | collective-permute-done | bytes 45088 | tf_op jit(solution)/shard_map/ppermute | solution.py:47
  14.4 0.5 %collective-permute-done.3.refs_4_ = bf16[2,2,11264]{2,1,0:T(2,128)(2,1)S(1)} collective-permute-done((bf16[2,2,11264]{2,1,0:T(2,128)(2,1)S(1)}, bf16[2,2,11264]{2,1,0:T(2,128)(2,1)S(1)}, u32[]{:S(2)}, u32[]{:S(2)}) %collective-permute-start.3) | collective-permute-done | bytes 90144 | tf_op jit(solution)/shard_map/ppermute | solution.py:47
  14.9 0.0 copy-start.6
  14.9 2.4 %rotate.1.refs_0_ = bf16[1,16,1408]{2,1,0:T(8,128)(2,1)S(1)} custom-call(bf16[1,2,11264]{2,1,0:T(2,128)(2,1)S(1)} %bitcast.24, bf16[1,2,11264]{2,1,0:T(2,128)(2,1)S(1)} %collective-permute-done.refs_1_, bf16[1,2,11264]{2,1,0:T(2,128)(2,1)S(1)} %collective-permute-done.1.refs_2_, bf16[2,2,11264]{2,1,0:T(2,128)(2,1)S(1)} %collective-permute-done.2.refs_3_, ...), custom_call_target="tpu_custom_call" | custom-call | flops 272000000 | bytes 17000000 | tf_op jit(solution)/shard_map/rotate/pallas_call | solution.py:234
  17.3 1.5 %collective-permute-start.5 = (bf16[1,16,1408]{2,1,0:T(8,128)(2,1)S(1)}, bf16[1,16,1408]{2,1,0:T(8,128)(2,1)S(1)}, u32[]{:S(2)}, u32[]{:S(2)}) collective-permute-start(bf16[1,16,1408]{2,1,0:T(8,128)(2,1)S(1)} %rotate.1.refs_0_), channel_id=1, source_target_pairs={{0,2},{2,0},{4,6},{6,4},{8,10},{10,8},{12,14},{14,12},{1,3},{3,1},... | collective-permute-start | bytes 135176 | tf_op jit(solution)/shard_map/ppermute | solution.py:47
  18.8 0.3 %collective-permute-start.7 = (bf16[1,16,1408]{2,1,0:T(8,128)(2,1)S(1)}, bf16[1,16,1408]{2,1,0:T(8,128)(2,1)S(1)}, u32[]{:S(2)}, u32[]{:S(2)}) collective-permute-start(bf16[1,16,1408]{2,1,0:T(8,128)(2,1)S(1)} %rotate.1.refs_0_), channel_id=1, source_target_pairs={{0,8},{2,10},{4,12},{6,14},{8,0},{10,2},{12,4},{14,6},{1,9},{3,11}... | collective-permute-start | bytes 135176 | tf_op jit(solution)/shard_map/ppermute | solution.py:47
  19.1 2.2 %collective-permute-done.5.refs_1_ = bf16[1,16,1408]{2,1,0:T(8,128)(2,1)S(1)} collective-permute-done((bf16[1,16,1408]{2,1,0:T(8,128)(2,1)S(1)}, bf16[1,16,1408]{2,1,0:T(8,128)(2,1)S(1)}, u32[]{:S(2)}, u32[]{:S(2)}) %collective-permute-start.5) | collective-permute-done | bytes 45088 | tf_op jit(solution)/shard_map/ppermute | solution.py:47
  21.4 2.7 %collective-permute-start.9 = (bf16[2,16,1408]{2,1,0:T(8,128)(2,1)S(1)}, bf16[2,16,1408]{2,1,0:T(8,128)(2,1)S(1)}, u32[]{:S(2)}, u32[]{:S(2)}) collective-permute-start(bf16[2,16,1408]{2,1,0:T(8,128)(2,1)S(1)} %pad_maximum_fusion.1), channel_id=1, source_target_pairs={{0,12},{2,14},{4,8},{6,10},{8,4},{10,6},{12,0},{14,2},{1,13},{3,15... | collective-permute-start | bytes 270344 | tf_op jit(solution)/shard_map/ppermute | solution.py:47
  24.1 0.0 collective-permute-start.6
  24.1 0.2 collective-permute-done.7.refs_2_
  24.3 0.5 %collective-permute-start.8 = (bf16[1,16,1408]{2,1,0:T(8,128)(2,1)S(1)}, bf16[1,16,1408]{2,1,0:T(8,128)(2,1)S(1)}, u32[]{:S(2)}, u32[]{:S(2)}) collective-permute-start(bf16[1,16,1408]{2,1,0:T(8,128)(2,1)S(1)} %collective-permute-done.7.refs_2_), channel_id=1, source_target_pairs={{0,2},{2,0},{4,6},{6,4},{8,10},{10,8},{12,14},{14,12},{1,3},{3,1},... | collective-permute-start | bytes 135176 | tf_op jit(solution)/shard_map/ppermute | solution.py:47
  24.7 0.5 %early_grams.1 = (f32[2,16,160]{2,1,0:T(8,128)S(1)}, f32[16,128]{1,0:T(8,128)S(1)}) custom-call(bf16[1,16,1408]{2,1,0:T(8,128)(2,1)S(1)} %rotate.1.refs_0_, bf16[1,16,1408]{2,1,0:T(8,128)(2,1)S(1)} %collective-permute-done.5.refs_1_, bf16[1,16,1408]{2,1,0:T(8,128)(2,1)S(1)} %collective-permute-done.7.refs_2_, bf16[160,7168]{1,0:T(8,128)(2,1)S(1)} %bitcast.10, ...), custom_call_target="tpu_custom_call" | custom-call | flops 500000000 | tf_op jit(solution)/shard_map/early_grams/pallas_call | solution.py:245
  25.2 2.6 %collective-permute-done.9.refs_0_ = bf16[2,16,1408]{2,1,0:T(8,128)(2,1)S(1)} collective-permute-done((bf16[2,16,1408]{2,1,0:T(8,128)(2,1)S(1)}, bf16[2,16,1408]{2,1,0:T(8,128)(2,1)S(1)}, u32[]{:S(2)}, u32[]{:S(2)}) %collective-permute-start.9) | collective-permute-done | bytes 90144 | tf_op jit(solution)/shard_map/ppermute | solution.py:47
  27.9 0.3 %more_grams.1.refs_4_ = f32[2,16,160]{2,1,0:T(8,128)S(1)} custom-call(bf16[2,16,1408]{2,1,0:T(8,128)(2,1)S(1)} %collective-permute-done.9.refs_0_, bf16[160,7168]{1,0:T(8,128)(2,1)S(1)} %bitcast.11, bf16[160,4096]{1,0:T(8,128)(2,1)S(1)} %bitcast.15, f32[2,16,160]{2,1,0:T(8,128)S(1)} %get-tuple-element.7.refs_3_), custom_call_target="tpu_custom_call" | custom-call | flops 300000000 | tf_op jit(solution)/shard_map/more_grams/pallas_call | solution.py:251
  28.2 0.1 collective-permute-done.8.refs_1_
  28.3 0.5 %collective-permute-done.6.refs_0_ = bf16[2,16,1408]{2,1,0:T(8,128)(2,1)S(1)} collective-permute-done((bf16[2,16,1408]{2,1,0:T(8,128)(2,1)S(1)}, bf16[2,16,1408]{2,1,0:T(8,128)(2,1)S(1)}, u32[]{:S(2)}, u32[]{:S(2)}) %collective-permute-start.6) | collective-permute-done | bytes 90144 | tf_op jit(solution)/shard_map/ppermute | solution.py:47
  28.8 0.6 %scores.1.mine = f32[8,128]{1,0:T(8,128)S(1)} custom-call(bf16[2,16,1408]{2,1,0:T(8,128)(2,1)S(1)} %collective-permute-done.6.refs_0_, bf16[1,16,1408]{2,1,0:T(8,128)(2,1)S(1)} %collective-permute-done.8.refs_1_, bf16[160,7168]{1,0:T(8,128)(2,1)S(1)} %bitcast.12, bf16[160,4096]{1,0:T(8,128)(2,1)S(1)} %bitcast.16, f32[2,16,160]{2,1,0:T(8,128)S(1)} %more_grams.1.refs_4_, ...), custom_call_target="tpu_custom_call" | custom-call | tf_op jit(solution)/shard_map/scores/pallas_call | solution.py:254
  29.4 0.0 collective-permute-start.10
  29.4 1.2 %collective-permute-done.10.other = f32[8,128]{1,0:T(8,128)S(1)} collective-permute-done((f32[8,128]{1,0:T(8,128)S(1)}, f32[8,128]{1,0:T(8,128)S(1)}, u32[]{:S(2)}, u32[]{:S(2)}) %collective-permute-start.10) | collective-permute-done | bytes 4128 | tf_op jit(solution)/shard_map/ppermute | solution.py:185
  30.6 0.6 %finish.1 = f32[2,4]{1,0:T(2,128)} custom-call(f32[8,128]{1,0:T(8,128)S(1)} %scores.1.mine, f32[8,128]{1,0:T(8,128)S(1)} %collective-permute-done.10.other), custom_call_target="tpu_custom_call" | custom-call | tf_op jit(solution)/shard_map/finish/pallas_call | solution.py:257
  (22 shorter events, 0.1 us)
Async XLA Ops:
  0.0 14.9 %slice-start = ((s8[12845056]{0:T(1024)(128)(4,1)}), s8[4194304]{0:T(1024)(128)(4,1)S(1)}, s32[]{:S(2)}) async-start(s8[12845056]{0:T(1024)(128)(4,1)} %bitcast.17), calls=%async_computation | async-start | bytes 8388608
  0.0 11.9 %copy-start = (bf16[1,160,7168]{2,1,0:T(8,128)(2,1)S(1)}, bf16[1,160,7168]{2,1,0:T(8,128)(2,1)}, u32[]{:S(2)}) copy-start(bf16[1,160,7168]{2,1,0:T(8,128)(2,1)} %param.12) | copy-start | bytes 6881284
  0.0 11.9 %copy-start.1 = (bf16[1,160,4096]{2,1,0:T(8,128)(2,1)S(1)}, bf16[1,160,4096]{2,1,0:T(8,128)(2,1)}, u32[]{:S(2)}) copy-start(bf16[1,160,4096]{2,1,0:T(8,128)(2,1)} %param.13) | copy-start | bytes 3932164
  0.0 11.9 %copy-start.3 = (f32[1,7168]{1,0:T(1,128)S(1)}, f32[1,7168]{1,0:T(1,128)}, u32[]{:S(2)}) copy-start(f32[1,7168]{1,0:T(1,128)} %refs_8_.1) | copy-start | bytes 86020
  0.0 11.9 %copy-start.4 = (f32[1,4096]{1,0:T(1,128)S(1)}, f32[1,4096]{1,0:T(1,128)}, u32[]{:S(2)}) copy-start(f32[1,4096]{1,0:T(1,128)} %refs_9_.1) | copy-start | bytes 49156
  0.0 11.9 %copy-start.5 = (s32[1,160]{1,0:T(1,128)S(1)}, s32[1,160]{1,0:T(1,128)}, u32[]{:S(2)}) copy-start(s32[1,160]{1,0:T(1,128)} %refs_6_.1) | copy-start | bytes 1924
  0.0 14.9 %slice-start.1 = ((s8[12845056]{0:T(1024)(128)(4,1)}), s8[4194304]{0:T(1024)(128)(4,1)S(1)}, s32[]{:S(2)}) async-start(s8[12845056]{0:T(1024)(128)(4,1)} %bitcast.17), calls=%async_computation.1 | async-start | bytes 8388608
  0.0 14.9 %slice-start.2 = ((s8[12845056]{0:T(1024)(128)(4,1)}), s8[4194304]{0:T(1024)(128)(4,1)S(1)}, s32[]{:S(2)}) async-start(s8[12845056]{0:T(1024)(128)(4,1)} %bitcast.17), calls=%async_computation.2 | async-start | bytes 8388608
  0.0 14.9 %slice-start.3 = ((s8[12845056]{0:T(1024)(128)(4,1)}), s8[262144]{0:T(1024)(128)(4,1)S(1)}, s32[]{:S(2)}) async-start(s8[12845056]{0:T(1024)(128)(4,1)} %bitcast.17), calls=%async_computation.3 | async-start | bytes 524288
  0.1 14.9 %copy-start.2 = (bf16[1,4096,512]{2,1,0:T(8,128)(2,1)S(1)}, bf16[1,4096,512]{2,1,0:T(8,128)(2,1)}, u32[]{:S(2)}) copy-start(bf16[1,4096,512]{2,1,0:T(8,128)(2,1)} %param.15) | copy-start | bytes 12582916
  1.0 5.6 %collective-permute-start = (bf16[1,2,11264]{2,1,0:T(2,128)(2,1)S(1)}, bf16[1,2,11264]{2,1,0:T(2,128)(2,1)S(1)}, u32[]{:S(2)}, u32[]{:S(2)}) collective-permute-start(bf16[1,2,11264]{2,1,0:T(2,128)(2,1)S(1)} %bitcast.21), channel_id=1, source_target_pairs={{0,2},{2,0},{4,6},{6,4},{8,10},{10,8},{12,14},{14,12},{1,3},{3,1},... | collective-permute-start | bytes 135176 | tf_op jit(solution)/shard_map/ppermute | solution.py:47
  4.0 6.4 %collective-permute-start.1 = (bf16[1,2,11264]{2,1,0:T(2,128)(2,1)S(1)}, bf16[1,2,11264]{2,1,0:T(2,128)(2,1)S(1)}, u32[]{:S(2)}, u32[]{:S(2)}) collective-permute-start(bf16[1,2,11264]{2,1,0:T(2,128)(2,1)S(1)} %bitcast.22), channel_id=1, source_target_pairs={{0,8},{2,10},{4,12},{6,14},{8,0},{10,2},{12,4},{14,6},{1,9},{3,11}... | collective-permute-start | bytes 135176 | tf_op jit(solution)/shard_map/ppermute | solution.py:47
  6.7 7.7 %collective-permute-start.2 = (bf16[2,2,11264]{2,1,0:T(2,128)(2,1)S(1)}, bf16[2,2,11264]{2,1,0:T(2,128)(2,1)S(1)}, u32[]{:S(2)}, u32[]{:S(2)}) collective-permute-start(bf16[2,2,11264]{2,1,0:T(2,128)(2,1)S(1)} %pad_maximum_fusion), channel_id=1, source_target_pairs={{0,12},{2,14},{4,8},{6,10},{8,4},{10,6},{12,0},{14,2},{1,13},{3,15... | collective-permute-start | bytes 270344 | tf_op jit(solution)/shard_map/ppermute | solution.py:47
  10.4 4.5 %collective-permute-start.3 = (bf16[2,2,11264]{2,1,0:T(2,128)(2,1)S(1)}, bf16[2,2,11264]{2,1,0:T(2,128)(2,1)S(1)}, u32[]{:S(2)}, u32[]{:S(2)}) collective-permute-start(bf16[2,2,11264]{2,1,0:T(2,128)(2,1)S(1)} %pad_maximum_fusion), channel_id=1, source_target_pairs={{0,4},{2,6},{4,0},{6,2},{8,12},{10,14},{12,8},{14,10},{1,5},{3,7},... | collective-permute-start | bytes 270344 | tf_op jit(solution)/shard_map/ppermute | solution.py:47
  10.4 4.0 %collective-permute-start.4 = (bf16[1,2,11264]{2,1,0:T(2,128)(2,1)S(1)}, bf16[1,2,11264]{2,1,0:T(2,128)(2,1)S(1)}, u32[]{:S(2)}, u32[]{:S(2)}) collective-permute-start(bf16[1,2,11264]{2,1,0:T(2,128)(2,1)S(1)} %collective-permute-done.1.refs_2_), channel_id=1, source_target_pairs={{0,2},{2,0},{4,6},{6,4},{8,10},{10,8},{12,14},{14,12},{1,3},{3,1},... | collective-permute-start | bytes 135176 | tf_op jit(solution)/shard_map/ppermute | solution.py:47
  14.9 9.8 %copy-start.6 = (s32[16]{0:T(128)S(1)}, s32[16]{0:T(128)}, u32[]{:S(2)}) copy-start(s32[16]{0:T(128)} %param.18) | copy-start | bytes 196
  17.3 4.1 %collective-permute-start.5 = (bf16[1,16,1408]{2,1,0:T(8,128)(2,1)S(1)}, bf16[1,16,1408]{2,1,0:T(8,128)(2,1)S(1)}, u32[]{:S(2)}, u32[]{:S(2)}) collective-permute-start(bf16[1,16,1408]{2,1,0:T(8,128)(2,1)S(1)} %rotate.1.refs_0_), channel_id=1, source_target_pairs={{0,2},{2,0},{4,6},{6,4},{8,10},{10,8},{12,14},{14,12},{1,3},{3,1},... | collective-permute-start | bytes 135176 | tf_op jit(solution)/shard_map/ppermute | solution.py:47
  18.8 5.5 %collective-permute-start.7 = (bf16[1,16,1408]{2,1,0:T(8,128)(2,1)S(1)}, bf16[1,16,1408]{2,1,0:T(8,128)(2,1)S(1)}, u32[]{:S(2)}, u32[]{:S(2)}) collective-permute-start(bf16[1,16,1408]{2,1,0:T(8,128)(2,1)S(1)} %rotate.1.refs_0_), channel_id=1, source_target_pairs={{0,8},{2,10},{4,12},{6,14},{8,0},{10,2},{12,4},{14,6},{1,9},{3,11}... | collective-permute-start | bytes 135176 | tf_op jit(solution)/shard_map/ppermute | solution.py:47
  21.4 6.5 %collective-permute-start.9 = (bf16[2,16,1408]{2,1,0:T(8,128)(2,1)S(1)}, bf16[2,16,1408]{2,1,0:T(8,128)(2,1)S(1)}, u32[]{:S(2)}, u32[]{:S(2)}) collective-permute-start(bf16[2,16,1408]{2,1,0:T(8,128)(2,1)S(1)} %pad_maximum_fusion.1), channel_id=1, source_target_pairs={{0,12},{2,14},{4,8},{6,10},{8,4},{10,6},{12,0},{14,2},{1,13},{3,15... | collective-permute-start | bytes 270344 | tf_op jit(solution)/shard_map/ppermute | solution.py:47
  24.1 4.8 %collective-permute-start.6 = (bf16[2,16,1408]{2,1,0:T(8,128)(2,1)S(1)}, bf16[2,16,1408]{2,1,0:T(8,128)(2,1)S(1)}, u32[]{:S(2)}, u32[]{:S(2)}) collective-permute-start(bf16[2,16,1408]{2,1,0:T(8,128)(2,1)S(1)} %pad_maximum_fusion.1), channel_id=1, source_target_pairs={{0,4},{2,6},{4,0},{6,2},{8,12},{10,14},{12,8},{14,10},{1,5},{3,7},... | collective-permute-start | bytes 270344 | tf_op jit(solution)/shard_map/ppermute | solution.py:47
  24.3 4.0 %collective-permute-start.8 = (bf16[1,16,1408]{2,1,0:T(8,128)(2,1)S(1)}, bf16[1,16,1408]{2,1,0:T(8,128)(2,1)S(1)}, u32[]{:S(2)}, u32[]{:S(2)}) collective-permute-start(bf16[1,16,1408]{2,1,0:T(8,128)(2,1)S(1)} %collective-permute-done.7.refs_2_), channel_id=1, source_target_pairs={{0,2},{2,0},{4,6},{6,4},{8,10},{10,8},{12,14},{14,12},{1,3},{3,1},... | collective-permute-start | bytes 135176 | tf_op jit(solution)/shard_map/ppermute | solution.py:47
  29.4 1.2 %collective-permute-start.10 = (f32[8,128]{1,0:T(8,128)S(1)}, f32[8,128]{1,0:T(8,128)S(1)}, u32[]{:S(2)}, u32[]{:S(2)}) collective-permute-start(f32[8,128]{1,0:T(8,128)S(1)} %scores.1.mine), channel_id=1, source_target_pairs={{0,1},{1,0},{2,3},{3,2},{4,5},{5,4},{6,7},{7,6},{8,9},{9,8},{10,11... | collective-permute-start | bytes 12296 | tf_op jit(solution)/shard_map/ppermute | solution.py:185

commit v5 on v4

--- a/solution.py
+++ b/solution.py
@@ -13,7 +13,8 @@
 LANES = 128
 MIB = 2**20
 X, Z, FAR = 1, 2, 4
-PLAN = [(X, (0,)), (FAR, (0,)), (Z ^ FAR, (0, X)), (Z, (0, X)), (X, (FAR,))]
+QUERY_PLAN = [(FAR, (0,)), (X, (0,)), (Z, (0, X)), (Z ^ FAR, (0, X)), (X, (FAR,))]
+ROTATED_PLAN = [(FAR, (0,)), (X, (0,)), (Z ^ FAR, (0, X)), (Z, (0, X)), (X, (FAR,))]
 BY_LANES = (((1,), (1,)), ((), ()))
 
 
@@ -25,9 +26,9 @@
     return pltpu.with_memory_space_constraint(x, pltpu.HBM)
 
 
-def steps(shards):
+def steps(shards, plan):
     if shards == 8:
-        return PLAN
+        return plan
     plan, known, stride = [], [0], shards
     while stride > 1:
         radix = min(4, stride)
@@ -37,19 +38,29 @@
     return plan
 
 
-def gather(x, shards):
+def gather(x, shards, plan=QUERY_PLAN, by_kernel=False):
     x = x[None]
     parts, masks = [x], [[0]]
     blocks, joined = {0: x}, {(0,): x}
-    for mask, sent in steps(shards):
+    for mask, sent in steps(shards, plan):
         if sent not in joined:
-            joined[sent] = jnp.concatenate([blocks[s] for s in sent], axis=0)
+            if by_kernel and len(sent) == 2:
+                joined[sent] = call(
+                    pair_kernel, "pair", jax.ShapeDtypeStruct((2, *x.shape[1:]), x.dtype)
+                )(*[blocks[s] for s in sent])
+            else:
+                joined[sent] = jnp.concatenate([blocks[s] for s in sent], axis=0)
         part = lax.ppermute(joined[sent], "ex", [(i, i ^ mask) for i in range(shards)])
         parts.append(part)
         masks.append([mask ^ s for s in sent])
         for i, s in enumerate(sent):
             blocks[mask ^ s] = part[i : i + 1]
     return parts, masks
+
+
+def pair_kernel(first, second, out):
+    out[:1] = first[...]
+    out[1:] = second[...]
 
 
 def in_order(parts, masks):
@@ -226,7 +237,7 @@
         out_specs=pl.BlockSpec(memory_space=pltpu.VMEM),
         scratch_shapes=[pltpu.SemaphoreType.DMA((2,))],
     )(hbm(query_out_grads[0]), hbm(query_inputs[0]))
-    everyone, masks = gather(own, shards)
+    everyone, masks = gather(own, shards, by_kernel=True)
     small = jax.ShapeDtypeStruct((8, LANES), jnp.float32)
     own_self = call(
         self_kernel, "self_influence", small, flops=2 * 160 * 160 * 11264, moved=3_700_000
@@ -239,7 +250,7 @@
         moved=17_000_000,
         scratch_shapes=[pltpu.VMEM((shards, own_tokens, width), jnp.bfloat16)],
     )(*everyone, basis_h, basis_i, eig_h, eig_i, own_self)
-    parts, masks = gather(rotated[0], shards)
+    parts, masks = gather(rotated[0], shards, ROTATED_PLAN)
     gram_shape = jax.ShapeDtypeStruct((2, tokens, train_h.shape[0]), jnp.float32)
     first, last = 3, 4
     grams, query_hot = call(

time: 31.4 us -> 31.3 us (level)
  waiting for transfers between devices: 8.47 us -> 6.7 us
  starting transfers between devices: 15.7 us -> 17.4 us
    ppermute x10, waiting for transfers between devices: 7.3 us -> 5.54 us  [gather(): lax.ppermute(joined[sent], 'ex', [(i, i ^ mask) for i in range(shards)])]
    ppermute x10, starting transfers between devices: 15.7 us -> 17.4 us  [gather(): lax.ppermute(joined[sent], 'ex', [(i, i ^ mask) for i in range(shards)])]
  transfers between devices with their start and end apart: 11 -> 11, of which waited for: 8 -> 6; matrix products, arithmetic and copies ran while one was open for 0% -> 0% of each run, Pallas kernels for 7% -> 7%
where the time goes in v5:
time: 31.3 us; the launch traced here: 31.1 us
  starting transfers between devices  17.4 us (56%)
  Pallas kernels  6.74 us (22%)
  waiting for transfers between devices  6.7 us (21%)
    ppermute x10, starting transfers between devices, gather(): lax.ppermute(joined[sent], 'ex', [(i, i ^ mask) for i in range(shards)])  17.4 us
    ppermute x10, waiting for transfers between devices, gather(): lax.ppermute(joined[sent], 'ex', [(i, i ^ mask) for i in range(shards)])  5.54 us
    pallas_call x1, Pallas kernels, body(): call(functools.partial(rotate_kernel, masks), 'rotate', jax.ShapeDtypeStr...  2.35 us
    pallas_call x1, Pallas kernels, body(): call(self_kernel, 'self_influence', small, flops=2 * 160 * 160 * 11264, m...  1.41 us
    ppermute x1, waiting for transfers between devices, layer_swap(): return lax.ppermute(x, 'layer', [(0, 1), (1, 0)])  1.16 us
    pallas_call x1, Pallas kernels, body(): call(join_kernel, 'join', pltpu.VMEM((own_tokens, width), jnp.bfloat16),...  0.92 us
    pallas_call x1, Pallas kernels, body(): call(finish_kernel, 'finish', jax.ShapeDtypeStruct((E_DEV, QUERIES // 2),...  0.65 us
  transfers between devices with their start and end apart: 11, of which 6 were waited for; matrix products, arithmetic and copies ran while one was open for 0% of the time, Pallas kernels for 7%

profile of v5, /device:TPU:0, one launch (start us, length us, event | category | flops | bytes accessed | tf_op | source)
XLA Modules:
  0.0 31.1 jit_solution(2542918483688592431)
XLA Ops:
  0.0 0.0 slice-start.1
  0.0 0.0 slice-start.2
  0.0 0.0 slice-start.3
  0.1 0.9 %join.1 = bf16[2,11264]{1,0:T(2,128)(2,1)S(1)} custom-call(bf16[2,7168]{1,0:T(2,128)(2,1)} %bitcast.26, bf16[2,4096]{1,0:T(2,128)(2,1)} %bitcast.27), custom_call_target="tpu_custom_call" | custom-call | flops 20000000000 | tf_op jit(solution)/shard_map/join/pallas_call | solution.py:231
  1.0 3.0 %collective-permute-start.1 = (bf16[1,2,11264]{2,1,0:T(2,128)(2,1)S(1)}, bf16[1,2,11264]{2,1,0:T(2,128)(2,1)S(1)}, u32[]{:S(2)}, u32[]{:S(2)}) collective-permute-start(bf16[1,2,11264]{2,1,0:T(2,128)(2,1)S(1)} %bitcast.21), channel_id=1, source_target_pairs={{0,2},{2,0},{4,6},{6,4},{8,10},{10,8},{12,14},{14,12},{1,3},{3,1},... | collective-permute-start | bytes 135176 | tf_op jit(solution)/shard_map/ppermute | solution.py:53
  4.0 2.6 %collective-permute-start = (bf16[1,2,11264]{2,1,0:T(2,128)(2,1)S(1)}, bf16[1,2,11264]{2,1,0:T(2,128)(2,1)S(1)}, u32[]{:S(2)}, u32[]{:S(2)}) collective-permute-start(bf16[1,2,11264]{2,1,0:T(2,128)(2,1)S(1)} %bitcast.22), channel_id=1, source_target_pairs={{0,8},{2,10},{4,12},{6,14},{8,0},{10,2},{12,4},{14,6},{1,9},{3,11}... | collective-permute-start | bytes 135176 | tf_op jit(solution)/shard_map/ppermute | solution.py:53
  6.6 1.6 %collective-permute-start.2 = (bf16[2,2,11264]{2,1,0:T(2,128)(2,1)S(1)}, bf16[2,2,11264]{2,1,0:T(2,128)(2,1)S(1)}, u32[]{:S(2)}, u32[]{:S(2)}) collective-permute-start(bf16[2,2,11264]{2,1,0:T(2,128)(2,1)S(1)} %pair.1), channel_id=1, source_target_pairs={{0,4},{2,6},{4,0},{6,2},{8,12},{10,14},{12,8},{14,10},{1,5},{3,7},... | collective-permute-start | bytes 270344 | tf_op jit(solution)/shard_map/ppermute | solution.py:53
  8.3 2.4 %collective-permute-start.3 = (bf16[2,2,11264]{2,1,0:T(2,128)(2,1)S(1)}, bf16[2,2,11264]{2,1,0:T(2,128)(2,1)S(1)}, u32[]{:S(2)}, u32[]{:S(2)}) collective-permute-start(bf16[2,2,11264]{2,1,0:T(2,128)(2,1)S(1)} %pair.1), channel_id=1, source_target_pairs={{0,12},{2,14},{4,8},{6,10},{8,4},{10,6},{12,0},{14,2},{1,13},{3,15... | collective-permute-start | bytes 270344 | tf_op jit(solution)/shard_map/ppermute | solution.py:53
  10.7 0.0 collective-permute-done.refs_1_
  10.7 1.5 %collective-permute-start.4 = (bf16[1,2,11264]{2,1,0:T(2,128)(2,1)S(1)}, bf16[1,2,11264]{2,1,0:T(2,128)(2,1)S(1)}, u32[]{:S(2)}, u32[]{:S(2)}) collective-permute-start(bf16[1,2,11264]{2,1,0:T(2,128)(2,1)S(1)} %collective-permute-done.refs_1_), channel_id=1, source_target_pairs={{0,2},{2,0},{4,6},{6,4},{8,10},{10,8},{12,14},{14,12},{1,3},{3,1},... | collective-permute-start | bytes 135176 | tf_op jit(solution)/shard_map/ppermute | solution.py:53
  12.2 1.4 %self_influence.1.refs_10_.refs_7_ = f32[8,128]{1,0:T(8,128)S(1)} custom-call(bf16[160,7168]{1,0:T(8,128)(2,1)S(1)} %bitcast.9, bf16[160,4096]{1,0:T(8,128)(2,1)S(1)} %bitcast.13, f32[1,7168]{1,0:T(1,128)S(1)} %copy-done.3, f32[1,4096]{1,0:T(1,128)S(1)} %copy-done.4, s32[1,160]{1,0:T(1,128)S(1)} %copy-done.5), custom_call_target="tpu_custom_call" | custom-call | flops 576716800 | bytes 3700000 | tf_op jit(solution)/shard_map/self_influence/pallas_call | solution.py:242
  13.6 1.1 %collective-permute-done.4.refs_5_ = bf16[1,2,11264]{2,1,0:T(2,128)(2,1)S(1)} collective-permute-done((bf16[1,2,11264]{2,1,0:T(2,128)(2,1)S(1)}, bf16[1,2,11264]{2,1,0:T(2,128)(2,1)S(1)}, u32[]{:S(2)}, u32[]{:S(2)}) %collective-permute-start.4) | collective-permute-done | bytes 45088 | tf_op jit(solution)/shard_map/ppermute | solution.py:53
  14.7 0.0 collective-permute-done.2.refs_3_
  14.7 0.0 collective-permute-done.3.refs_4_
  14.8 0.0 copy-start.6
  14.8 2.4 %rotate.1.refs_0_ = bf16[1,16,1408]{2,1,0:T(8,128)(2,1)S(1)} custom-call(bf16[1,2,11264]{2,1,0:T(2,128)(2,1)S(1)} %bitcast.24, bf16[1,2,11264]{2,1,0:T(2,128)(2,1)S(1)} %collective-permute-done.refs_1_, bf16[1,2,11264]{2,1,0:T(2,128)(2,1)S(1)} %collective-permute-done.1.second.refs_2_, bf16[2,2,11264]{2,1,0:T(2,128)(2,1)S(1)} %collective-permute-done.2.refs_3_, ...), custom_call_target="tpu_custom_call" | custom-call | flops 272000000 | bytes 17000000 | tf_op jit(solution)/shard_map/rotate/pallas_call | solution.py:245
  17.2 1.5 %collective-permute-start.5 = (bf16[1,16,1408]{2,1,0:T(8,128)(2,1)S(1)}, bf16[1,16,1408]{2,1,0:T(8,128)(2,1)S(1)}, u32[]{:S(2)}, u32[]{:S(2)}) collective-permute-start(bf16[1,16,1408]{2,1,0:T(8,128)(2,1)S(1)} %rotate.1.refs_0_), channel_id=1, source_target_pairs={{0,2},{2,0},{4,6},{6,4},{8,10},{10,8},{12,14},{14,12},{1,3},{3,1},... | collective-permute-start | bytes 135176 | tf_op jit(solution)/shard_map/ppermute | solution.py:53
  18.7 1.6 %collective-permute-start.7 = (bf16[1,16,1408]{2,1,0:T(8,128)(2,1)S(1)}, bf16[1,16,1408]{2,1,0:T(8,128)(2,1)S(1)}, u32[]{:S(2)}, u32[]{:S(2)}) collective-permute-start(bf16[1,16,1408]{2,1,0:T(8,128)(2,1)S(1)} %rotate.1.refs_0_), channel_id=1, source_target_pairs={{0,8},{2,10},{4,12},{6,14},{8,0},{10,2},{12,4},{14,6},{1,9},{3,11}... | collective-permute-start | bytes 135176 | tf_op jit(solution)/shard_map/ppermute | solution.py:53
  20.2 1.0 %collective-permute-done.5.refs_2_ = bf16[1,16,1408]{2,1,0:T(8,128)(2,1)S(1)} collective-permute-done((bf16[1,16,1408]{2,1,0:T(8,128)(2,1)S(1)}, bf16[1,16,1408]{2,1,0:T(8,128)(2,1)S(1)}, u32[]{:S(2)}, u32[]{:S(2)}) %collective-permute-start.5) | collective-permute-done | bytes 45088 | tf_op jit(solution)/shard_map/ppermute | solution.py:53
  21.2 2.5 %collective-permute-start.9 = (bf16[2,16,1408]{2,1,0:T(8,128)(2,1)S(1)}, bf16[2,16,1408]{2,1,0:T(8,128)(2,1)S(1)}, u32[]{:S(2)}, u32[]{:S(2)}) collective-permute-start(bf16[2,16,1408]{2,1,0:T(8,128)(2,1)S(1)} %pad_maximum_fusion), channel_id=1, source_target_pairs={{0,12},{2,14},{4,8},{6,10},{8,4},{10,6},{12,0},{14,2},{1,13},{3,15... | collective-permute-start | bytes 270344 | tf_op jit(solution)/shard_map/ppermute | solution.py:53
  23.8 0.0 collective-permute-start.6
  23.8 0.9 %collective-permute-done.7.refs_1_ = bf16[1,16,1408]{2,1,0:T(8,128)(2,1)S(1)} collective-permute-done((bf16[1,16,1408]{2,1,0:T(8,128)(2,1)S(1)}, bf16[1,16,1408]{2,1,0:T(8,128)(2,1)S(1)}, u32[]{:S(2)}, u32[]{:S(2)}) %collective-permute-start.7) | collective-permute-done | bytes 45088 | tf_op jit(solution)/shard_map/ppermute | solution.py:53
  24.6 0.7 %collective-permute-start.8 = (bf16[1,16,1408]{2,1,0:T(8,128)(2,1)S(1)}, bf16[1,16,1408]{2,1,0:T(8,128)(2,1)S(1)}, u32[]{:S(2)}, u32[]{:S(2)}) collective-permute-start(bf16[1,16,1408]{2,1,0:T(8,128)(2,1)S(1)} %collective-permute-done.7.refs_1_), channel_id=1, source_target_pairs={{0,2},{2,0},{4,6},{6,4},{8,10},{10,8},{12,14},{14,12},{1,3},{3,1},... | collective-permute-start | bytes 135176 | tf_op jit(solution)/shard_map/ppermute | solution.py:53
  25.3 0.5 %early_grams.1 = (f32[2,16,160]{2,1,0:T(8,128)S(1)}, f32[16,128]{1,0:T(8,128)S(1)}) custom-call(bf16[1,16,1408]{2,1,0:T(8,128)(2,1)S(1)} %rotate.1.refs_0_, bf16[1,16,1408]{2,1,0:T(8,128)(2,1)S(1)} %collective-permute-done.7.refs_1_, bf16[1,16,1408]{2,1,0:T(8,128)(2,1)S(1)} %collective-permute-done.5.refs_2_, bf16[160,7168]{1,0:T(8,128)(2,1)S(1)} %bitcast.10, ...), custom_call_target="tpu_custom_call" | custom-call | flops 500000000 | tf_op jit(solution)/shard_map/early_grams/pallas_call | solution.py:256
  25.8 1.9 %collective-permute-done.9.refs_0_ = bf16[2,16,1408]{2,1,0:T(8,128)(2,1)S(1)} collective-permute-done((bf16[2,16,1408]{2,1,0:T(8,128)(2,1)S(1)}, bf16[2,16,1408]{2,1,0:T(8,128)(2,1)S(1)}, u32[]{:S(2)}, u32[]{:S(2)}) %collective-permute-start.9) | collective-permute-done | bytes 90144 | tf_op jit(solution)/shard_map/ppermute | solution.py:53
  27.7 0.3 %more_grams.1.refs_4_ = f32[2,16,160]{2,1,0:T(8,128)S(1)} custom-call(bf16[2,16,1408]{2,1,0:T(8,128)(2,1)S(1)} %collective-permute-done.9.refs_0_, bf16[160,7168]{1,0:T(8,128)(2,1)S(1)} %bitcast.11, bf16[160,4096]{1,0:T(8,128)(2,1)S(1)} %bitcast.15, f32[2,16,160]{2,1,0:T(8,128)S(1)} %get-tuple-element.7.refs_3_), custom_call_target="tpu_custom_call" | custom-call | flops 300000000 | tf_op jit(solution)/shard_map/more_grams/pallas_call | solution.py:262
  28.0 0.7 %collective-permute-done.8.refs_1_ = bf16[1,16,1408]{2,1,0:T(8,128)(2,1)S(1)} collective-permute-done((bf16[1,16,1408]{2,1,0:T(8,128)(2,1)S(1)}, bf16[1,16,1408]{2,1,0:T(8,128)(2,1)S(1)}, u32[]{:S(2)}, u32[]{:S(2)}) %collective-permute-start.8) | collective-permute-done | bytes 45088 | tf_op jit(solution)/shard_map/ppermute | solution.py:53
  28.7 0.0 collective-permute-done.6.refs_0_
  28.7 0.6 %scores.1.mine = f32[8,128]{1,0:T(8,128)S(1)} custom-call(bf16[2,16,1408]{2,1,0:T(8,128)(2,1)S(1)} %collective-permute-done.6.refs_0_, bf16[1,16,1408]{2,1,0:T(8,128)(2,1)S(1)} %collective-permute-done.8.refs_1_, bf16[160,7168]{1,0:T(8,128)(2,1)S(1)} %bitcast.12, bf16[160,4096]{1,0:T(8,128)(2,1)S(1)} %bitcast.16, f32[2,16,160]{2,1,0:T(8,128)S(1)} %more_grams.1.refs_4_, ...), custom_call_target="tpu_custom_call" | custom-call | tf_op jit(solution)/shard_map/scores/pallas_call | solution.py:265
  29.3 0.0 collective-permute-start.10
  29.3 1.2 %collective-permute-done.10.other = f32[8,128]{1,0:T(8,128)S(1)} collective-permute-done((f32[8,128]{1,0:T(8,128)S(1)}, f32[8,128]{1,0:T(8,128)S(1)}, u32[]{:S(2)}, u32[]{:S(2)}) %collective-permute-start.10) | collective-permute-done | bytes 4128 | tf_op jit(solution)/shard_map/ppermute | solution.py:196
  30.4 0.6 %finish.1 = f32[2,4]{1,0:T(2,128)} custom-call(f32[8,128]{1,0:T(8,128)S(1)} %scores.1.mine, f32[8,128]{1,0:T(8,128)S(1)} %collective-permute-done.10.other), custom_call_target="tpu_custom_call" | custom-call | tf_op jit(solution)/shard_map/finish/pallas_call | solution.py:268
  (22 shorter events, 0.1 us)
Async XLA Ops:
  0.0 14.7 %slice-start = ((s8[12845056]{0:T(1024)(128)(4,1)}), s8[4194304]{0:T(1024)(128)(4,1)S(1)}, s32[]{:S(2)}) async-start(s8[12845056]{0:T(1024)(128)(4,1)} %bitcast.17), calls=%async_computation | async-start | bytes 8388608
  0.0 12.2 %copy-start = (bf16[1,160,7168]{2,1,0:T(8,128)(2,1)S(1)}, bf16[1,160,7168]{2,1,0:T(8,128)(2,1)}, u32[]{:S(2)}) copy-start(bf16[1,160,7168]{2,1,0:T(8,128)(2,1)} %param.12) | copy-start | bytes 6881284
  0.0 12.2 %copy-start.1 = (bf16[1,160,4096]{2,1,0:T(8,128)(2,1)S(1)}, bf16[1,160,4096]{2,1,0:T(8,128)(2,1)}, u32[]{:S(2)}) copy-start(bf16[1,160,4096]{2,1,0:T(8,128)(2,1)} %param.13) | copy-start | bytes 3932164
  0.0 12.2 %copy-start.3 = (f32[1,7168]{1,0:T(1,128)S(1)}, f32[1,7168]{1,0:T(1,128)}, u32[]{:S(2)}) copy-start(f32[1,7168]{1,0:T(1,128)} %refs_8_.1) | copy-start | bytes 86020
  0.0 12.2 %copy-start.4 = (f32[1,4096]{1,0:T(1,128)S(1)}, f32[1,4096]{1,0:T(1,128)}, u32[]{:S(2)}) copy-start(f32[1,4096]{1,0:T(1,128)} %refs_9_.1) | copy-start | bytes 49156
  0.0 12.2 %copy-start.5 = (s32[1,160]{1,0:T(1,128)S(1)}, s32[1,160]{1,0:T(1,128)}, u32[]{:S(2)}) copy-start(s32[1,160]{1,0:T(1,128)} %refs_6_.1) | copy-start | bytes 1924
  0.0 14.7 %slice-start.1 = ((s8[12845056]{0:T(1024)(128)(4,1)}), s8[4194304]{0:T(1024)(128)(4,1)S(1)}, s32[]{:S(2)}) async-start(s8[12845056]{0:T(1024)(128)(4,1)} %bitcast.17), calls=%async_computation.1 | async-start | bytes 8388608
  0.0 14.7 %slice-start.2 = ((s8[12845056]{0:T(1024)(128)(4,1)}), s8[4194304]{0:T(1024)(128)(4,1)S(1)}, s32[]{:S(2)}) async-start(s8[12845056]{0:T(1024)(128)(4,1)} %bitcast.17), calls=%async_computation.2 | async-start | bytes 8388608
  0.0 14.7 %slice-start.3 = ((s8[12845056]{0:T(1024)(128)(4,1)}), s8[262144]{0:T(1024)(128)(4,1)S(1)}, s32[]{:S(2)}) async-start(s8[12845056]{0:T(1024)(128)(4,1)} %bitcast.17), calls=%async_computation.3 | async-start | bytes 524288
  0.1 14.7 %copy-start.2 = (bf16[1,4096,512]{2,1,0:T(8,128)(2,1)S(1)}, bf16[1,4096,512]{2,1,0:T(8,128)(2,1)}, u32[]{:S(2)}) copy-start(bf16[1,4096,512]{2,1,0:T(8,128)(2,1)} %param.15) | copy-start | bytes 12582916
  1.0 5.6 %collective-permute-start.1 = (bf16[1,2,11264]{2,1,0:T(2,128)(2,1)S(1)}, bf16[1,2,11264]{2,1,0:T(2,128)(2,1)S(1)}, u32[]{:S(2)}, u32[]{:S(2)}) collective-permute-start(bf16[1,2,11264]{2,1,0:T(2,128)(2,1)S(1)} %bitcast.21), channel_id=1, source_target_pairs={{0,2},{2,0},{4,6},{6,4},{8,10},{10,8},{12,14},{14,12},{1,3},{3,1},... | collective-permute-start | bytes 135176 | tf_op jit(solution)/shard_map/ppermute | solution.py:53
  4.0 6.7 %collective-permute-start = (bf16[1,2,11264]{2,1,0:T(2,128)(2,1)S(1)}, bf16[1,2,11264]{2,1,0:T(2,128)(2,1)S(1)}, u32[]{:S(2)}, u32[]{:S(2)}) collective-permute-start(bf16[1,2,11264]{2,1,0:T(2,128)(2,1)S(1)} %bitcast.22), channel_id=1, source_target_pairs={{0,8},{2,10},{4,12},{6,14},{8,0},{10,2},{12,4},{14,6},{1,9},{3,11}... | collective-permute-start | bytes 135176 | tf_op jit(solution)/shard_map/ppermute | solution.py:53
  6.6 8.1 %collective-permute-start.2 = (bf16[2,2,11264]{2,1,0:T(2,128)(2,1)S(1)}, bf16[2,2,11264]{2,1,0:T(2,128)(2,1)S(1)}, u32[]{:S(2)}, u32[]{:S(2)}) collective-permute-start(bf16[2,2,11264]{2,1,0:T(2,128)(2,1)S(1)} %pair.1), channel_id=1, source_target_pairs={{0,4},{2,6},{4,0},{6,2},{8,12},{10,14},{12,8},{14,10},{1,5},{3,7},... | collective-permute-start | bytes 270344 | tf_op jit(solution)/shard_map/ppermute | solution.py:53
  8.3 6.5 %collective-permute-start.3 = (bf16[2,2,11264]{2,1,0:T(2,128)(2,1)S(1)}, bf16[2,2,11264]{2,1,0:T(2,128)(2,1)S(1)}, u32[]{:S(2)}, u32[]{:S(2)}) collective-permute-start(bf16[2,2,11264]{2,1,0:T(2,128)(2,1)S(1)} %pair.1), channel_id=1, source_target_pairs={{0,12},{2,14},{4,8},{6,10},{8,4},{10,6},{12,0},{14,2},{1,13},{3,15... | collective-permute-start | bytes 270344 | tf_op jit(solution)/shard_map/ppermute | solution.py:53
  10.7 4.0 %collective-permute-start.4 = (bf16[1,2,11264]{2,1,0:T(2,128)(2,1)S(1)}, bf16[1,2,11264]{2,1,0:T(2,128)(2,1)S(1)}, u32[]{:S(2)}, u32[]{:S(2)}) collective-permute-start(bf16[1,2,11264]{2,1,0:T(2,128)(2,1)S(1)} %collective-permute-done.refs_1_), channel_id=1, source_target_pairs={{0,2},{2,0},{4,6},{6,4},{8,10},{10,8},{12,14},{14,12},{1,3},{3,1},... | collective-permute-start | bytes 135176 | tf_op jit(solution)/shard_map/ppermute | solution.py:53
  14.8 10.5 %copy-start.6 = (s32[16]{0:T(128)S(1)}, s32[16]{0:T(128)}, u32[]{:S(2)}) copy-start(s32[16]{0:T(128)} %param.18) | copy-start | bytes 196
  17.2 4.1 %collective-permute-start.5 = (bf16[1,16,1408]{2,1,0:T(8,128)(2,1)S(1)}, bf16[1,16,1408]{2,1,0:T(8,128)(2,1)S(1)}, u32[]{:S(2)}, u32[]{:S(2)}) collective-permute-start(bf16[1,16,1408]{2,1,0:T(8,128)(2,1)S(1)} %rotate.1.refs_0_), channel_id=1, source_target_pairs={{0,2},{2,0},{4,6},{6,4},{8,10},{10,8},{12,14},{14,12},{1,3},{3,1},... | collective-permute-start | bytes 135176 | tf_op jit(solution)/shard_map/ppermute | solution.py:53
  18.7 6.0 %collective-permute-start.7 = (bf16[1,16,1408]{2,1,0:T(8,128)(2,1)S(1)}, bf16[1,16,1408]{2,1,0:T(8,128)(2,1)S(1)}, u32[]{:S(2)}, u32[]{:S(2)}) collective-permute-start(bf16[1,16,1408]{2,1,0:T(8,128)(2,1)S(1)} %rotate.1.refs_0_), channel_id=1, source_target_pairs={{0,8},{2,10},{4,12},{6,14},{8,0},{10,2},{12,4},{14,6},{1,9},{3,11}... | collective-permute-start | bytes 135176 | tf_op jit(solution)/shard_map/ppermute | solution.py:53
  21.2 6.4 %collective-permute-start.9 = (bf16[2,16,1408]{2,1,0:T(8,128)(2,1)S(1)}, bf16[2,16,1408]{2,1,0:T(8,128)(2,1)S(1)}, u32[]{:S(2)}, u32[]{:S(2)}) collective-permute-start(bf16[2,16,1408]{2,1,0:T(8,128)(2,1)S(1)} %pad_maximum_fusion), channel_id=1, source_target_pairs={{0,12},{2,14},{4,8},{6,10},{8,4},{10,6},{12,0},{14,2},{1,13},{3,15... | collective-permute-start | bytes 270344 | tf_op jit(solution)/shard_map/ppermute | solution.py:53
  23.8 4.9 %collective-permute-start.6 = (bf16[2,16,1408]{2,1,0:T(8,128)(2,1)S(1)}, bf16[2,16,1408]{2,1,0:T(8,128)(2,1)S(1)}, u32[]{:S(2)}, u32[]{:S(2)}) collective-permute-start(bf16[2,16,1408]{2,1,0:T(8,128)(2,1)S(1)} %pad_maximum_fusion), channel_id=1, source_target_pairs={{0,4},{2,6},{4,0},{6,2},{8,12},{10,14},{12,8},{14,10},{1,5},{3,7},... | collective-permute-start | bytes 270344 | tf_op jit(solution)/shard_map/ppermute | solution.py:53
  24.6 4.0 %collective-permute-start.8 = (bf16[1,16,1408]{2,1,0:T(8,128)(2,1)S(1)}, bf16[1,16,1408]{2,1,0:T(8,128)(2,1)S(1)}, u32[]{:S(2)}, u32[]{:S(2)}) collective-permute-start(bf16[1,16,1408]{2,1,0:T(8,128)(2,1)S(1)} %collective-permute-done.7.refs_1_), channel_id=1, source_target_pairs={{0,2},{2,0},{4,6},{6,4},{8,10},{10,8},{12,14},{14,12},{1,3},{3,1},... | collective-permute-start | bytes 135176 | tf_op jit(solution)/shard_map/ppermute | solution.py:53
  29.3 1.2 %collective-permute-start.10 = (f32[8,128]{1,0:T(8,128)S(1)}, f32[8,128]{1,0:T(8,128)S(1)}, u32[]{:S(2)}, u32[]{:S(2)}) collective-permute-start(f32[8,128]{1,0:T(8,128)S(1)} %scores.1.mine), channel_id=1, source_target_pairs={{0,1},{1,0},{2,3},{3,2},{4,5},{5,4},{6,7},{7,6},{8,9},{9,8},{10,11... | collective-permute-start | bytes 12296 | tf_op jit(solution)/shard_map/ppermute | solution.py:196

commit v6 on v5

--- a/solution.py
+++ b/solution.py
@@ -14,7 +14,7 @@
 MIB = 2**20
 X, Z, FAR = 1, 2, 4
 QUERY_PLAN = [(FAR, (0,)), (X, (0,)), (Z, (0, X)), (Z ^ FAR, (0, X)), (X, (FAR,))]
-ROTATED_PLAN = [(FAR, (0,)), (X, (0,)), (Z ^ FAR, (0, X)), (Z, (0, X)), (X, (FAR,))]
+ROTATED_PLAN = [(FAR, (0,)), (X, (0,)), (Z ^ FAR, (0, X)), (X, (FAR,)), (Z, (0, X))]
 BY_LANES = (((1,), (1,)), ((), ()))
 
 

time: 31.3 us -> 31.3 us (level)
  no operation moved by 1% of the time
where the time goes in v6:
time: 31.3 us; the launch traced here: 31.1 us
  starting transfers between devices  17.4 us (56%)
  Pallas kernels  6.74 us (22%)
  waiting for transfers between devices  6.7 us (21%)
    ppermute x10, starting transfers between devices, gather(): lax.ppermute(joined[sent], 'ex', [(i, i ^ mask) for i in range(shards)])  17.4 us
    ppermute x10, waiting for transfers between devices, gather(): lax.ppermute(joined[sent], 'ex', [(i, i ^ mask) for i in range(shards)])  5.54 us
    pallas_call x1, Pallas kernels, body(): call(functools.partial(rotate_kernel, masks), 'rotate', jax.ShapeDtypeStr...  2.35 us
    pallas_call x1, Pallas kernels, body(): call(self_kernel, 'self_influence', small, flops=2 * 160 * 160 * 11264, m...  1.41 us
    ppermute x1, waiting for transfers between devices, layer_swap(): return lax.ppermute(x, 'layer', [(0, 1), (1, 0)])  1.16 us
    pallas_call x1, Pallas kernels, body(): call(join_kernel, 'join', pltpu.VMEM((own_tokens, width), jnp.bfloat16),...  0.92 us
    pallas_call x1, Pallas kernels, body(): call(finish_kernel, 'finish', jax.ShapeDtypeStruct((E_DEV, QUERIES // 2),...  0.65 us
  transfers between devices with their start and end apart: 11, of which 6 were waited for; matrix products, arithmetic and copies ran while one was open for 0% of the time, Pallas kernels for 7%

profile of v6, /device:TPU:0, one launch (start us, length us, event | category | flops | bytes accessed | tf_op | source)
XLA Modules:
  0.0 31.1 jit_solution(4513697851186536764)
XLA Ops:
  0.0 0.0 slice-start.1
  0.0 0.0 slice-start.2
  0.0 0.0 slice-start.3
  0.1 0.9 %join.1 = bf16[2,11264]{1,0:T(2,128)(2,1)S(1)} custom-call(bf16[2,7168]{1,0:T(2,128)(2,1)} %bitcast.26, bf16[2,4096]{1,0:T(2,128)(2,1)} %bitcast.27), custom_call_target="tpu_custom_call" | custom-call | flops 20000000000 | tf_op jit(solution)/shard_map/join/pallas_call | solution.py:231
  1.0 3.0 %collective-permute-start.1 = (bf16[1,2,11264]{2,1,0:T(2,128)(2,1)S(1)}, bf16[1,2,11264]{2,1,0:T(2,128)(2,1)S(1)}, u32[]{:S(2)}, u32[]{:S(2)}) collective-permute-start(bf16[1,2,11264]{2,1,0:T(2,128)(2,1)S(1)} %bitcast.21), channel_id=1, source_target_pairs={{0,2},{2,0},{4,6},{6,4},{8,10},{10,8},{12,14},{14,12},{1,3},{3,1},... | collective-permute-start | bytes 135176 | tf_op jit(solution)/shard_map/ppermute | solution.py:53
  4.0 2.6 %collective-permute-start = (bf16[1,2,11264]{2,1,0:T(2,128)(2,1)S(1)}, bf16[1,2,11264]{2,1,0:T(2,128)(2,1)S(1)}, u32[]{:S(2)}, u32[]{:S(2)}) collective-permute-start(bf16[1,2,11264]{2,1,0:T(2,128)(2,1)S(1)} %bitcast.22), channel_id=1, source_target_pairs={{0,8},{2,10},{4,12},{6,14},{8,0},{10,2},{12,4},{14,6},{1,9},{3,11}... | collective-permute-start | bytes 135176 | tf_op jit(solution)/shard_map/ppermute | solution.py:53
  6.6 0.0 collective-permute-done.1.second.refs_2_
  6.6 1.6 %collective-permute-start.2 = (bf16[2,2,11264]{2,1,0:T(2,128)(2,1)S(1)}, bf16[2,2,11264]{2,1,0:T(2,128)(2,1)S(1)}, u32[]{:S(2)}, u32[]{:S(2)}) collective-permute-start(bf16[2,2,11264]{2,1,0:T(2,128)(2,1)S(1)} %pair.1), channel_id=1, source_target_pairs={{0,4},{2,6},{4,0},{6,2},{8,12},{10,14},{12,8},{14,10},{1,5},{3,7},... | collective-permute-start | bytes 270344 | tf_op jit(solution)/shard_map/ppermute | solution.py:53
  8.3 2.4 %collective-permute-start.3 = (bf16[2,2,11264]{2,1,0:T(2,128)(2,1)S(1)}, bf16[2,2,11264]{2,1,0:T(2,128)(2,1)S(1)}, u32[]{:S(2)}, u32[]{:S(2)}) collective-permute-start(bf16[2,2,11264]{2,1,0:T(2,128)(2,1)S(1)} %pair.1), channel_id=1, source_target_pairs={{0,12},{2,14},{4,8},{6,10},{8,4},{10,6},{12,0},{14,2},{1,13},{3,15... | collective-permute-start | bytes 270344 | tf_op jit(solution)/shard_map/ppermute | solution.py:53
  10.7 0.0 collective-permute-done.refs_1_
  10.7 1.5 %collective-permute-start.4 = (bf16[1,2,11264]{2,1,0:T(2,128)(2,1)S(1)}, bf16[1,2,11264]{2,1,0:T(2,128)(2,1)S(1)}, u32[]{:S(2)}, u32[]{:S(2)}) collective-permute-start(bf16[1,2,11264]{2,1,0:T(2,128)(2,1)S(1)} %collective-permute-done.refs_1_), channel_id=1, source_target_pairs={{0,2},{2,0},{4,6},{6,4},{8,10},{10,8},{12,14},{14,12},{1,3},{3,1},... | collective-permute-start | bytes 135176 | tf_op jit(solution)/shard_map/ppermute | solution.py:53
  12.2 1.4 %self_influence.1.refs_10_.refs_7_ = f32[8,128]{1,0:T(8,128)S(1)} custom-call(bf16[160,7168]{1,0:T(8,128)(2,1)S(1)} %bitcast.9, bf16[160,4096]{1,0:T(8,128)(2,1)S(1)} %bitcast.13, f32[1,7168]{1,0:T(1,128)S(1)} %copy-done.3, f32[1,4096]{1,0:T(1,128)S(1)} %copy-done.4, s32[1,160]{1,0:T(1,128)S(1)} %copy-done.5), custom_call_target="tpu_custom_call" | custom-call | flops 576716800 | bytes 3700000 | tf_op jit(solution)/shard_map/self_influence/pallas_call | solution.py:242
  13.6 1.1 %collective-permute-done.4.refs_5_ = bf16[1,2,11264]{2,1,0:T(2,128)(2,1)S(1)} collective-permute-done((bf16[1,2,11264]{2,1,0:T(2,128)(2,1)S(1)}, bf16[1,2,11264]{2,1,0:T(2,128)(2,1)S(1)}, u32[]{:S(2)}, u32[]{:S(2)}) %collective-permute-start.4) | collective-permute-done | bytes 45088 | tf_op jit(solution)/shard_map/ppermute | solution.py:53
  14.7 0.0 collective-permute-done.3.refs_4_
  14.8 0.0 copy-start.6
  14.8 2.4 %rotate.1.refs_0_ = bf16[1,16,1408]{2,1,0:T(8,128)(2,1)S(1)} custom-call(bf16[1,2,11264]{2,1,0:T(2,128)(2,1)S(1)} %bitcast.24, bf16[1,2,11264]{2,1,0:T(2,128)(2,1)S(1)} %collective-permute-done.refs_1_, bf16[1,2,11264]{2,1,0:T(2,128)(2,1)S(1)} %collective-permute-done.1.second.refs_2_, bf16[2,2,11264]{2,1,0:T(2,128)(2,1)S(1)} %collective-permute-done.2.refs_3_, ...), custom_call_target="tpu_custom_call" | custom-call | flops 272000000 | bytes 17000000 | tf_op jit(solution)/shard_map/rotate/pallas_call | solution.py:245
  17.2 1.5 %collective-permute-start.7 = (bf16[1,16,1408]{2,1,0:T(8,128)(2,1)S(1)}, bf16[1,16,1408]{2,1,0:T(8,128)(2,1)S(1)}, u32[]{:S(2)}, u32[]{:S(2)}) collective-permute-start(bf16[1,16,1408]{2,1,0:T(8,128)(2,1)S(1)} %rotate.1.refs_0_), channel_id=1, source_target_pairs={{0,2},{2,0},{4,6},{6,4},{8,10},{10,8},{12,14},{14,12},{1,3},{3,1},... | collective-permute-start | bytes 135176 | tf_op jit(solution)/shard_map/ppermute | solution.py:53
  18.7 1.6 %collective-permute-start.5 = (bf16[1,16,1408]{2,1,0:T(8,128)(2,1)S(1)}, bf16[1,16,1408]{2,1,0:T(8,128)(2,1)S(1)}, u32[]{:S(2)}, u32[]{:S(2)}) collective-permute-start(bf16[1,16,1408]{2,1,0:T(8,128)(2,1)S(1)} %rotate.1.refs_0_), channel_id=1, source_target_pairs={{0,8},{2,10},{4,12},{6,14},{8,0},{10,2},{12,4},{14,6},{1,9},{3,11}... | collective-permute-start | bytes 135176 | tf_op jit(solution)/shard_map/ppermute | solution.py:53
  20.2 1.0 %collective-permute-done.7.refs_2_ = bf16[1,16,1408]{2,1,0:T(8,128)(2,1)S(1)} collective-permute-done((bf16[1,16,1408]{2,1,0:T(8,128)(2,1)S(1)}, bf16[1,16,1408]{2,1,0:T(8,128)(2,1)S(1)}, u32[]{:S(2)}, u32[]{:S(2)}) %collective-permute-start.7) | collective-permute-done | bytes 45088 | tf_op jit(solution)/shard_map/ppermute | solution.py:53
  21.2 2.5 %collective-permute-start.9 = (bf16[2,16,1408]{2,1,0:T(8,128)(2,1)S(1)}, bf16[2,16,1408]{2,1,0:T(8,128)(2,1)S(1)}, u32[]{:S(2)}, u32[]{:S(2)}) collective-permute-start(bf16[2,16,1408]{2,1,0:T(8,128)(2,1)S(1)} %pad_maximum_fusion), channel_id=1, source_target_pairs={{0,12},{2,14},{4,8},{6,10},{8,4},{10,6},{12,0},{14,2},{1,13},{3,15... | collective-permute-start | bytes 270344 | tf_op jit(solution)/shard_map/ppermute | solution.py:53
  23.8 0.0 collective-permute-start.8
  23.8 0.9 %collective-permute-done.5.refs_1_ = bf16[1,16,1408]{2,1,0:T(8,128)(2,1)S(1)} collective-permute-done((bf16[1,16,1408]{2,1,0:T(8,128)(2,1)S(1)}, bf16[1,16,1408]{2,1,0:T(8,128)(2,1)S(1)}, u32[]{:S(2)}, u32[]{:S(2)}) %collective-permute-start.5) | collective-permute-done | bytes 45088 | tf_op jit(solution)/shard_map/ppermute | solution.py:53
  24.6 0.7 %collective-permute-start.6 = (bf16[1,16,1408]{2,1,0:T(8,128)(2,1)S(1)}, bf16[1,16,1408]{2,1,0:T(8,128)(2,1)S(1)}, u32[]{:S(2)}, u32[]{:S(2)}) collective-permute-start(bf16[1,16,1408]{2,1,0:T(8,128)(2,1)S(1)} %collective-permute-done.5.refs_1_), channel_id=1, source_target_pairs={{0,2},{2,0},{4,6},{6,4},{8,10},{10,8},{12,14},{14,12},{1,3},{3,1},... | collective-permute-start | bytes 135176 | tf_op jit(solution)/shard_map/ppermute | solution.py:53
  25.3 0.5 %early_grams.1 = (f32[2,16,160]{2,1,0:T(8,128)S(1)}, f32[16,128]{1,0:T(8,128)S(1)}) custom-call(bf16[1,16,1408]{2,1,0:T(8,128)(2,1)S(1)} %rotate.1.refs_0_, bf16[1,16,1408]{2,1,0:T(8,128)(2,1)S(1)} %collective-permute-done.5.refs_1_, bf16[1,16,1408]{2,1,0:T(8,128)(2,1)S(1)} %collective-permute-done.7.refs_2_, bf16[160,7168]{1,0:T(8,128)(2,1)S(1)} %bitcast.10, ...), custom_call_target="tpu_custom_call" | custom-call | flops 500000000 | tf_op jit(solution)/shard_map/early_grams/pallas_call | solution.py:256
  25.8 1.9 %collective-permute-done.9.refs_0_ = bf16[2,16,1408]{2,1,0:T(8,128)(2,1)S(1)} collective-permute-done((bf16[2,16,1408]{2,1,0:T(8,128)(2,1)S(1)}, bf16[2,16,1408]{2,1,0:T(8,128)(2,1)S(1)}, u32[]{:S(2)}, u32[]{:S(2)}) %collective-permute-start.9) | collective-permute-done | bytes 90144 | tf_op jit(solution)/shard_map/ppermute | solution.py:53
  27.7 0.3 %more_grams.1.refs_4_ = f32[2,16,160]{2,1,0:T(8,128)S(1)} custom-call(bf16[2,16,1408]{2,1,0:T(8,128)(2,1)S(1)} %collective-permute-done.9.refs_0_, bf16[160,7168]{1,0:T(8,128)(2,1)S(1)} %bitcast.11, bf16[160,4096]{1,0:T(8,128)(2,1)S(1)} %bitcast.15, f32[2,16,160]{2,1,0:T(8,128)S(1)} %get-tuple-element.7.refs_3_), custom_call_target="tpu_custom_call" | custom-call | flops 300000000 | tf_op jit(solution)/shard_map/more_grams/pallas_call | solution.py:262
  28.0 0.7 %collective-permute-done.6.refs_0_ = bf16[1,16,1408]{2,1,0:T(8,128)(2,1)S(1)} collective-permute-done((bf16[1,16,1408]{2,1,0:T(8,128)(2,1)S(1)}, bf16[1,16,1408]{2,1,0:T(8,128)(2,1)S(1)}, u32[]{:S(2)}, u32[]{:S(2)}) %collective-permute-start.6) | collective-permute-done | bytes 45088 | tf_op jit(solution)/shard_map/ppermute | solution.py:53
  28.7 0.0 collective-permute-done.8.refs_1_
  28.7 0.6 %scores.1.mine = f32[8,128]{1,0:T(8,128)S(1)} custom-call(bf16[1,16,1408]{2,1,0:T(8,128)(2,1)S(1)} %collective-permute-done.6.refs_0_, bf16[2,16,1408]{2,1,0:T(8,128)(2,1)S(1)} %collective-permute-done.8.refs_1_, bf16[160,7168]{1,0:T(8,128)(2,1)S(1)} %bitcast.12, bf16[160,4096]{1,0:T(8,128)(2,1)S(1)} %bitcast.16, f32[2,16,160]{2,1,0:T(8,128)S(1)} %more_grams.1.refs_4_, ...), custom_call_target="tpu_custom_call" | custom-call | tf_op jit(solution)/shard_map/scores/pallas_call | solution.py:265
  29.3 0.0 collective-permute-start.10
  29.3 1.2 %collective-permute-done.10.other = f32[8,128]{1,0:T(8,128)S(1)} collective-permute-done((f32[8,128]{1,0:T(8,128)S(1)}, f32[8,128]{1,0:T(8,128)S(1)}, u32[]{:S(2)}, u32[]{:S(2)}) %collective-permute-start.10) | collective-permute-done | bytes 4128 | tf_op jit(solution)/shard_map/ppermute | solution.py:196
  30.4 0.6 %finish.1 = f32[2,4]{1,0:T(2,128)} custom-call(f32[8,128]{1,0:T(8,128)S(1)} %scores.1.mine, f32[8,128]{1,0:T(8,128)S(1)} %collective-permute-done.10.other), custom_call_target="tpu_custom_call" | custom-call | tf_op jit(solution)/shard_map/finish/pallas_call | solution.py:268
  (22 shorter events, 0.1 us)
Async XLA Ops:
  0.0 14.7 %slice-start = ((s8[12845056]{0:T(1024)(128)(4,1)}), s8[4194304]{0:T(1024)(128)(4,1)S(1)}, s32[]{:S(2)}) async-start(s8[12845056]{0:T(1024)(128)(4,1)} %bitcast.17), calls=%async_computation | async-start | bytes 8388608
  0.0 12.2 %copy-start = (bf16[1,160,7168]{2,1,0:T(8,128)(2,1)S(1)}, bf16[1,160,7168]{2,1,0:T(8,128)(2,1)}, u32[]{:S(2)}) copy-start(bf16[1,160,7168]{2,1,0:T(8,128)(2,1)} %param.12) | copy-start | bytes 6881284
  0.0 12.2 %copy-start.1 = (bf16[1,160,4096]{2,1,0:T(8,128)(2,1)S(1)}, bf16[1,160,4096]{2,1,0:T(8,128)(2,1)}, u32[]{:S(2)}) copy-start(bf16[1,160,4096]{2,1,0:T(8,128)(2,1)} %param.13) | copy-start | bytes 3932164
  0.0 12.2 %copy-start.3 = (f32[1,7168]{1,0:T(1,128)S(1)}, f32[1,7168]{1,0:T(1,128)}, u32[]{:S(2)}) copy-start(f32[1,7168]{1,0:T(1,128)} %refs_8_.1) | copy-start | bytes 86020
  0.0 12.2 %copy-start.4 = (f32[1,4096]{1,0:T(1,128)S(1)}, f32[1,4096]{1,0:T(1,128)}, u32[]{:S(2)}) copy-start(f32[1,4096]{1,0:T(1,128)} %refs_9_.1) | copy-start | bytes 49156
  0.0 12.2 %copy-start.5 = (s32[1,160]{1,0:T(1,128)S(1)}, s32[1,160]{1,0:T(1,128)}, u32[]{:S(2)}) copy-start(s32[1,160]{1,0:T(1,128)} %refs_6_.1) | copy-start | bytes 1924
  0.0 14.7 %slice-start.1 = ((s8[12845056]{0:T(1024)(128)(4,1)}), s8[4194304]{0:T(1024)(128)(4,1)S(1)}, s32[]{:S(2)}) async-start(s8[12845056]{0:T(1024)(128)(4,1)} %bitcast.17), calls=%async_computation.1 | async-start | bytes 8388608
  0.0 14.7 %slice-start.2 = ((s8[12845056]{0:T(1024)(128)(4,1)}), s8[4194304]{0:T(1024)(128)(4,1)S(1)}, s32[]{:S(2)}) async-start(s8[12845056]{0:T(1024)(128)(4,1)} %bitcast.17), calls=%async_computation.2 | async-start | bytes 8388608
  0.0 14.7 %slice-start.3 = ((s8[12845056]{0:T(1024)(128)(4,1)}), s8[262144]{0:T(1024)(128)(4,1)S(1)}, s32[]{:S(2)}) async-start(s8[12845056]{0:T(1024)(128)(4,1)} %bitcast.17), calls=%async_computation.3 | async-start | bytes 524288
  0.1 14.7 %copy-start.2 = (bf16[1,4096,512]{2,1,0:T(8,128)(2,1)S(1)}, bf16[1,4096,512]{2,1,0:T(8,128)(2,1)}, u32[]{:S(2)}) copy-start(bf16[1,4096,512]{2,1,0:T(8,128)(2,1)} %param.15) | copy-start | bytes 12582916
  1.0 5.6 %collective-permute-start.1 = (bf16[1,2,11264]{2,1,0:T(2,128)(2,1)S(1)}, bf16[1,2,11264]{2,1,0:T(2,128)(2,1)S(1)}, u32[]{:S(2)}, u32[]{:S(2)}) collective-permute-start(bf16[1,2,11264]{2,1,0:T(2,128)(2,1)S(1)} %bitcast.21), channel_id=1, source_target_pairs={{0,2},{2,0},{4,6},{6,4},{8,10},{10,8},{12,14},{14,12},{1,3},{3,1},... | collective-permute-start | bytes 135176 | tf_op jit(solution)/shard_map/ppermute | solution.py:53
  4.0 6.7 %collective-permute-start = (bf16[1,2,11264]{2,1,0:T(2,128)(2,1)S(1)}, bf16[1,2,11264]{2,1,0:T(2,128)(2,1)S(1)}, u32[]{:S(2)}, u32[]{:S(2)}) collective-permute-start(bf16[1,2,11264]{2,1,0:T(2,128)(2,1)S(1)} %bitcast.22), channel_id=1, source_target_pairs={{0,8},{2,10},{4,12},{6,14},{8,0},{10,2},{12,4},{14,6},{1,9},{3,11}... | collective-permute-start | bytes 135176 | tf_op jit(solution)/shard_map/ppermute | solution.py:53
  6.6 8.1 %collective-permute-start.2 = (bf16[2,2,11264]{2,1,0:T(2,128)(2,1)S(1)}, bf16[2,2,11264]{2,1,0:T(2,128)(2,1)S(1)}, u32[]{:S(2)}, u32[]{:S(2)}) collective-permute-start(bf16[2,2,11264]{2,1,0:T(2,128)(2,1)S(1)} %pair.1), channel_id=1, source_target_pairs={{0,4},{2,6},{4,0},{6,2},{8,12},{10,14},{12,8},{14,10},{1,5},{3,7},... | collective-permute-start | bytes 270344 | tf_op jit(solution)/shard_map/ppermute | solution.py:53
  8.3 6.5 %collective-permute-start.3 = (bf16[2,2,11264]{2,1,0:T(2,128)(2,1)S(1)}, bf16[2,2,11264]{2,1,0:T(2,128)(2,1)S(1)}, u32[]{:S(2)}, u32[]{:S(2)}) collective-permute-start(bf16[2,2,11264]{2,1,0:T(2,128)(2,1)S(1)} %pair.1), channel_id=1, source_target_pairs={{0,12},{2,14},{4,8},{6,10},{8,4},{10,6},{12,0},{14,2},{1,13},{3,15... | collective-permute-start | bytes 270344 | tf_op jit(solution)/shard_map/ppermute | solution.py:53
  10.7 4.0 %collective-permute-start.4 = (bf16[1,2,11264]{2,1,0:T(2,128)(2,1)S(1)}, bf16[1,2,11264]{2,1,0:T(2,128)(2,1)S(1)}, u32[]{:S(2)}, u32[]{:S(2)}) collective-permute-start(bf16[1,2,11264]{2,1,0:T(2,128)(2,1)S(1)} %collective-permute-done.refs_1_), channel_id=1, source_target_pairs={{0,2},{2,0},{4,6},{6,4},{8,10},{10,8},{12,14},{14,12},{1,3},{3,1},... | collective-permute-start | bytes 135176 | tf_op jit(solution)/shard_map/ppermute | solution.py:53
  14.8 10.5 %copy-start.6 = (s32[16]{0:T(128)S(1)}, s32[16]{0:T(128)}, u32[]{:S(2)}) copy-start(s32[16]{0:T(128)} %param.18) | copy-start | bytes 196
  17.2 4.1 %collective-permute-start.7 = (bf16[1,16,1408]{2,1,0:T(8,128)(2,1)S(1)}, bf16[1,16,1408]{2,1,0:T(8,128)(2,1)S(1)}, u32[]{:S(2)}, u32[]{:S(2)}) collective-permute-start(bf16[1,16,1408]{2,1,0:T(8,128)(2,1)S(1)} %rotate.1.refs_0_), channel_id=1, source_target_pairs={{0,2},{2,0},{4,6},{6,4},{8,10},{10,8},{12,14},{14,12},{1,3},{3,1},... | collective-permute-start | bytes 135176 | tf_op jit(solution)/shard_map/ppermute | solution.py:53
  18.7 6.0 %collective-permute-start.5 = (bf16[1,16,1408]{2,1,0:T(8,128)(2,1)S(1)}, bf16[1,16,1408]{2,1,0:T(8,128)(2,1)S(1)}, u32[]{:S(2)}, u32[]{:S(2)}) collective-permute-start(bf16[1,16,1408]{2,1,0:T(8,128)(2,1)S(1)} %rotate.1.refs_0_), channel_id=1, source_target_pairs={{0,8},{2,10},{4,12},{6,14},{8,0},{10,2},{12,4},{14,6},{1,9},{3,11}... | collective-permute-start | bytes 135176 | tf_op jit(solution)/shard_map/ppermute | solution.py:53
  21.2 6.4 %collective-permute-start.9 = (bf16[2,16,1408]{2,1,0:T(8,128)(2,1)S(1)}, bf16[2,16,1408]{2,1,0:T(8,128)(2,1)S(1)}, u32[]{:S(2)}, u32[]{:S(2)}) collective-permute-start(bf16[2,16,1408]{2,1,0:T(8,128)(2,1)S(1)} %pad_maximum_fusion), channel_id=1, source_target_pairs={{0,12},{2,14},{4,8},{6,10},{8,4},{10,6},{12,0},{14,2},{1,13},{3,15... | collective-permute-start | bytes 270344 | tf_op jit(solution)/shard_map/ppermute | solution.py:53
  23.8 4.9 %collective-permute-start.8 = (bf16[2,16,1408]{2,1,0:T(8,128)(2,1)S(1)}, bf16[2,16,1408]{2,1,0:T(8,128)(2,1)S(1)}, u32[]{:S(2)}, u32[]{:S(2)}) collective-permute-start(bf16[2,16,1408]{2,1,0:T(8,128)(2,1)S(1)} %pad_maximum_fusion), channel_id=1, source_target_pairs={{0,4},{2,6},{4,0},{6,2},{8,12},{10,14},{12,8},{14,10},{1,5},{3,7},... | collective-permute-start | bytes 270344 | tf_op jit(solution)/shard_map/ppermute | solution.py:53
  24.6 4.0 %collective-permute-start.6 = (bf16[1,16,1408]{2,1,0:T(8,128)(2,1)S(1)}, bf16[1,16,1408]{2,1,0:T(8,128)(2,1)S(1)}, u32[]{:S(2)}, u32[]{:S(2)}) collective-permute-start(bf16[1,16,1408]{2,1,0:T(8,128)(2,1)S(1)} %collective-permute-done.5.refs_1_), channel_id=1, source_target_pairs={{0,2},{2,0},{4,6},{6,4},{8,10},{10,8},{12,14},{14,12},{1,3},{3,1},... | collective-permute-start | bytes 135176 | tf_op jit(solution)/shard_map/ppermute | solution.py:53
  29.3 1.2 %collective-permute-start.10 = (f32[8,128]{1,0:T(8,128)S(1)}, f32[8,128]{1,0:T(8,128)S(1)}, u32[]{:S(2)}, u32[]{:S(2)}) collective-permute-start(f32[8,128]{1,0:T(8,128)S(1)} %scores.1.mine), channel_id=1, source_target_pairs={{0,1},{1,0},{2,3},{3,2},{4,5},{5,4},{6,7},{7,6},{8,9},{9,8},{10,11... | collective-permute-start | bytes 12296 | tf_op jit(solution)/shard_map/ppermute | solution.py:196

commit v7 on v6

--- a/solution.py
+++ b/solution.py
@@ -252,7 +252,7 @@
     )(*everyone, basis_h, basis_i, eig_h, eig_i, own_self)
     parts, masks = gather(rotated[0], shards, ROTATED_PLAN)
     gram_shape = jax.ShapeDtypeStruct((2, tokens, train_h.shape[0]), jnp.float32)
-    first, last = 3, 4
+    first, last = 3, 5
     grams, query_hot = call(
         functools.partial(early_kernel, masks[:first]),
         "early_grams",

time: 31.3 us -> 31.7 us (1.013)
  waiting for transfers between devices: 6.7 us -> 7.04 us
    ppermute x10, waiting for transfers between devices: 5.54 us -> 5.88 us  [gather(): lax.ppermute(joined[sent], 'ex', [(i, i ^ mask) for i in range(shards)])]
  transfers between devices with their start and end apart: 11 -> 11, of which waited for: 6 -> 5; matrix products, arithmetic and copies ran while one was open for 0% -> 0% of each run, Pallas kernels for 7% -> 8%
where the time goes in v7:
time: 31.7 us; the launch traced here: 31.5 us
  starting transfers between devices  17.5 us (55%)
  waiting for transfers between devices  7.04 us (22%)
  Pallas kernels  6.76 us (21%)
    ppermute x10, starting transfers between devices, gather(): lax.ppermute(joined[sent], 'ex', [(i, i ^ mask) for i in range(shards)])  17.4 us
    ppermute x10, waiting for transfers between devices, gather(): lax.ppermute(joined[sent], 'ex', [(i, i ^ mask) for i in range(shards)])  5.88 us
    pallas_call x1, Pallas kernels, body(): call(functools.partial(rotate_kernel, masks), 'rotate', jax.ShapeDtypeStr...  2.35 us
    pallas_call x1, Pallas kernels, body(): call(self_kernel, 'self_influence', small, flops=2 * 160 * 160 * 11264, m...  1.41 us
    ppermute x1, waiting for transfers between devices, layer_swap(): return lax.ppermute(x, 'layer', [(0, 1), (1, 0)])  1.16 us
    pallas_call x1, Pallas kernels, body(): call(join_kernel, 'join', pltpu.VMEM((own_tokens, width), jnp.bfloat16),...  0.92 us
    pallas_call x1, Pallas kernels, body(): call(finish_kernel, 'finish', jax.ShapeDtypeStruct((E_DEV, QUERIES // 2),...  0.65 us
  transfers between devices with their start and end apart: 11, of which 5 were waited for; matrix products, arithmetic and copies ran while one was open for 0% of the time, Pallas kernels for 8%

profile of v7, /device:TPU:0, one launch (start us, length us, event | category | flops | bytes accessed | tf_op | source)
XLA Modules:
  0.0 31.5 jit_solution(8581602779630681133)
XLA Ops:
  0.0 0.0 slice-start.1
  0.0 0.0 slice-start.2
  0.0 0.0 slice-start.3
  0.1 0.9 %join.1 = bf16[2,11264]{1,0:T(2,128)(2,1)S(1)} custom-call(bf16[2,7168]{1,0:T(2,128)(2,1)} %bitcast.26, bf16[2,4096]{1,0:T(2,128)(2,1)} %bitcast.27), custom_call_target="tpu_custom_call" | custom-call | flops 20000000000 | tf_op jit(solution)/shard_map/join/pallas_call | solution.py:231
  1.0 3.0 %collective-permute-start.1 = (bf16[1,2,11264]{2,1,0:T(2,128)(2,1)S(1)}, bf16[1,2,11264]{2,1,0:T(2,128)(2,1)S(1)}, u32[]{:S(2)}, u32[]{:S(2)}) collective-permute-start(bf16[1,2,11264]{2,1,0:T(2,128)(2,1)S(1)} %bitcast.21), channel_id=1, source_target_pairs={{0,2},{2,0},{4,6},{6,4},{8,10},{10,8},{12,14},{14,12},{1,3},{3,1},... | collective-permute-start | bytes 135176 | tf_op jit(solution)/shard_map/ppermute | solution.py:53
  4.0 2.6 %collective-permute-start = (bf16[1,2,11264]{2,1,0:T(2,128)(2,1)S(1)}, bf16[1,2,11264]{2,1,0:T(2,128)(2,1)S(1)}, u32[]{:S(2)}, u32[]{:S(2)}) collective-permute-start(bf16[1,2,11264]{2,1,0:T(2,128)(2,1)S(1)} %bitcast.22), channel_id=1, source_target_pairs={{0,8},{2,10},{4,12},{6,14},{8,0},{10,2},{12,4},{14,6},{1,9},{3,11}... | collective-permute-start | bytes 135176 | tf_op jit(solution)/shard_map/ppermute | solution.py:53
  6.6 0.0 collective-permute-done.1.second.refs_2_
  6.6 1.6 %collective-permute-start.2 = (bf16[2,2,11264]{2,1,0:T(2,128)(2,1)S(1)}, bf16[2,2,11264]{2,1,0:T(2,128)(2,1)S(1)}, u32[]{:S(2)}, u32[]{:S(2)}) collective-permute-start(bf16[2,2,11264]{2,1,0:T(2,128)(2,1)S(1)} %pair.1), channel_id=1, source_target_pairs={{0,4},{2,6},{4,0},{6,2},{8,12},{10,14},{12,8},{14,10},{1,5},{3,7},... | collective-permute-start | bytes 270344 | tf_op jit(solution)/shard_map/ppermute | solution.py:53
  8.3 2.4 %collective-permute-start.3 = (bf16[2,2,11264]{2,1,0:T(2,128)(2,1)S(1)}, bf16[2,2,11264]{2,1,0:T(2,128)(2,1)S(1)}, u32[]{:S(2)}, u32[]{:S(2)}) collective-permute-start(bf16[2,2,11264]{2,1,0:T(2,128)(2,1)S(1)} %pair.1), channel_id=1, source_target_pairs={{0,12},{2,14},{4,8},{6,10},{8,4},{10,6},{12,0},{14,2},{1,13},{3,15... | collective-permute-start | bytes 270344 | tf_op jit(solution)/shard_map/ppermute | solution.py:53
  10.7 0.0 collective-permute-done.refs_1_
  10.7 1.5 %collective-permute-start.4 = (bf16[1,2,11264]{2,1,0:T(2,128)(2,1)S(1)}, bf16[1,2,11264]{2,1,0:T(2,128)(2,1)S(1)}, u32[]{:S(2)}, u32[]{:S(2)}) collective-permute-start(bf16[1,2,11264]{2,1,0:T(2,128)(2,1)S(1)} %collective-permute-done.refs_1_), channel_id=1, source_target_pairs={{0,2},{2,0},{4,6},{6,4},{8,10},{10,8},{12,14},{14,12},{1,3},{3,1},... | collective-permute-start | bytes 135176 | tf_op jit(solution)/shard_map/ppermute | solution.py:53
  12.2 1.4 %self_influence.1.refs_10_.refs_6_ = f32[8,128]{1,0:T(8,128)S(1)} custom-call(bf16[160,7168]{1,0:T(8,128)(2,1)S(1)} %bitcast.9, bf16[160,4096]{1,0:T(8,128)(2,1)S(1)} %bitcast.13, f32[1,7168]{1,0:T(1,128)S(1)} %copy-done.3, f32[1,4096]{1,0:T(1,128)S(1)} %copy-done.4, s32[1,160]{1,0:T(1,128)S(1)} %copy-done.5), custom_call_target="tpu_custom_call" | custom-call | flops 576716800 | bytes 3700000 | tf_op jit(solution)/shard_map/self_influence/pallas_call | solution.py:242
  13.6 1.1 %collective-permute-done.4.refs_5_ = bf16[1,2,11264]{2,1,0:T(2,128)(2,1)S(1)} collective-permute-done((bf16[1,2,11264]{2,1,0:T(2,128)(2,1)S(1)}, bf16[1,2,11264]{2,1,0:T(2,128)(2,1)S(1)}, u32[]{:S(2)}, u32[]{:S(2)}) %collective-permute-start.4) | collective-permute-done | bytes 45088 | tf_op jit(solution)/shard_map/ppermute | solution.py:53
  14.7 0.0 collective-permute-done.2.refs_3_
  14.7 0.0 collective-permute-done.3.refs_4_
  14.8 0.0 copy-start.6
  14.8 2.4 %rotate.1.refs_0_ = bf16[1,16,1408]{2,1,0:T(8,128)(2,1)S(1)} custom-call(bf16[1,2,11264]{2,1,0:T(2,128)(2,1)S(1)} %bitcast.24, bf16[1,2,11264]{2,1,0:T(2,128)(2,1)S(1)} %collective-permute-done.refs_1_, bf16[1,2,11264]{2,1,0:T(2,128)(2,1)S(1)} %collective-permute-done.1.second.refs_2_, bf16[2,2,11264]{2,1,0:T(2,128)(2,1)S(1)} %collective-permute-done.2.refs_3_, ...), custom_call_target="tpu_custom_call" | custom-call | flops 272000000 | bytes 17000000 | tf_op jit(solution)/shard_map/rotate/pallas_call | solution.py:245
  17.2 1.5 %collective-permute-start.5 = (bf16[1,16,1408]{2,1,0:T(8,128)(2,1)S(1)}, bf16[1,16,1408]{2,1,0:T(8,128)(2,1)S(1)}, u32[]{:S(2)}, u32[]{:S(2)}) collective-permute-start(bf16[1,16,1408]{2,1,0:T(8,128)(2,1)S(1)} %rotate.1.refs_0_), channel_id=1, source_target_pairs={{0,2},{2,0},{4,6},{6,4},{8,10},{10,8},{12,14},{14,12},{1,3},{3,1},... | collective-permute-start | bytes 135176 | tf_op jit(solution)/shard_map/ppermute | solution.py:53
  18.7 1.6 %collective-permute-start.8 = (bf16[1,16,1408]{2,1,0:T(8,128)(2,1)S(1)}, bf16[1,16,1408]{2,1,0:T(8,128)(2,1)S(1)}, u32[]{:S(2)}, u32[]{:S(2)}) collective-permute-start(bf16[1,16,1408]{2,1,0:T(8,128)(2,1)S(1)} %rotate.1.refs_0_), channel_id=1, source_target_pairs={{0,8},{2,10},{4,12},{6,14},{8,0},{10,2},{12,4},{14,6},{1,9},{3,11}... | collective-permute-start | bytes 135176 | tf_op jit(solution)/shard_map/ppermute | solution.py:53
  20.2 1.0 %collective-permute-done.5.refs_2_ = bf16[1,16,1408]{2,1,0:T(8,128)(2,1)S(1)} collective-permute-done((bf16[1,16,1408]{2,1,0:T(8,128)(2,1)S(1)}, bf16[1,16,1408]{2,1,0:T(8,128)(2,1)S(1)}, u32[]{:S(2)}, u32[]{:S(2)}) %collective-permute-start.5) | collective-permute-done | bytes 45088 | tf_op jit(solution)/shard_map/ppermute | solution.py:53
  21.2 2.5 %collective-permute-start.7 = (bf16[2,16,1408]{2,1,0:T(8,128)(2,1)S(1)}, bf16[2,16,1408]{2,1,0:T(8,128)(2,1)S(1)}, u32[]{:S(2)}, u32[]{:S(2)}) collective-permute-start(bf16[2,16,1408]{2,1,0:T(8,128)(2,1)S(1)} %pad_maximum_fusion), channel_id=1, source_target_pairs={{0,12},{2,14},{4,8},{6,10},{8,4},{10,6},{12,0},{14,2},{1,13},{3,15... | collective-permute-start | bytes 270344 | tf_op jit(solution)/shard_map/ppermute | solution.py:53
  23.8 0.0 collective-permute-start.6
  23.8 0.9 %collective-permute-done.8.refs_1_ = bf16[1,16,1408]{2,1,0:T(8,128)(2,1)S(1)} collective-permute-done((bf16[1,16,1408]{2,1,0:T(8,128)(2,1)S(1)}, bf16[1,16,1408]{2,1,0:T(8,128)(2,1)S(1)}, u32[]{:S(2)}, u32[]{:S(2)}) %collective-permute-start.8) | collective-permute-done | bytes 45088 | tf_op jit(solution)/shard_map/ppermute | solution.py:53
  24.6 0.7 %collective-permute-start.9 = (bf16[1,16,1408]{2,1,0:T(8,128)(2,1)S(1)}, bf16[1,16,1408]{2,1,0:T(8,128)(2,1)S(1)}, u32[]{:S(2)}, u32[]{:S(2)}) collective-permute-start(bf16[1,16,1408]{2,1,0:T(8,128)(2,1)S(1)} %collective-permute-done.8.refs_1_), channel_id=1, source_target_pairs={{0,2},{2,0},{4,6},{6,4},{8,10},{10,8},{12,14},{14,12},{1,3},{3,1},... | collective-permute-start | bytes 135176 | tf_op jit(solution)/shard_map/ppermute | solution.py:53
  25.3 0.5 %early_grams.1 = (f32[2,16,160]{2,1,0:T(8,128)S(1)}, f32[16,128]{1,0:T(8,128)S(1)}) custom-call(bf16[1,16,1408]{2,1,0:T(8,128)(2,1)S(1)} %rotate.1.refs_0_, bf16[1,16,1408]{2,1,0:T(8,128)(2,1)S(1)} %collective-permute-done.8.refs_1_, bf16[1,16,1408]{2,1,0:T(8,128)(2,1)S(1)} %collective-permute-done.5.refs_2_, bf16[160,7168]{1,0:T(8,128)(2,1)S(1)} %bitcast.10, ...), custom_call_target="tpu_custom_call" | custom-call | flops 500000000 | tf_op jit(solution)/shard_map/early_grams/pallas_call | solution.py:256
  25.8 2.9 %collective-permute-done.9.refs_1_ = bf16[1,16,1408]{2,1,0:T(8,128)(2,1)S(1)} collective-permute-done((bf16[1,16,1408]{2,1,0:T(8,128)(2,1)S(1)}, bf16[1,16,1408]{2,1,0:T(8,128)(2,1)S(1)}, u32[]{:S(2)}, u32[]{:S(2)}) %collective-permute-start.9) | collective-permute-done | bytes 45088 | tf_op jit(solution)/shard_map/ppermute | solution.py:53
  28.7 0.0 collective-permute-done.7.refs_0_
  28.7 0.5 %more_grams.1.refs_3_ = f32[2,16,160]{2,1,0:T(8,128)S(1)} custom-call(bf16[2,16,1408]{2,1,0:T(8,128)(2,1)S(1)} %collective-permute-done.7.refs_0_, bf16[1,16,1408]{2,1,0:T(8,128)(2,1)S(1)} %collective-permute-done.9.refs_1_, bf16[160,7168]{1,0:T(8,128)(2,1)S(1)} %bitcast.11, bf16[160,4096]{1,0:T(8,128)(2,1)S(1)} %bitcast.15, ...), custom_call_target="tpu_custom_call" | custom-call | flops 300000000 | tf_op jit(solution)/shard_map/more_grams/pallas_call | solution.py:262
  29.2 0.5 %scores.1.mine = f32[8,128]{1,0:T(8,128)S(1)} custom-call(bf16[2,16,1408]{2,1,0:T(8,128)(2,1)S(1)} %collective-permute-done.6.refs_0_, bf16[160,7168]{1,0:T(8,128)(2,1)S(1)} %bitcast.12, bf16[160,4096]{1,0:T(8,128)(2,1)S(1)} %bitcast.16, f32[2,16,160]{2,1,0:T(8,128)S(1)} %more_grams.1.refs_3_, f32[16,128]{1,0:T(8,128)S(1)} %get-tuple-element.8.refs_4_, ...), custom_call_target="tpu_custom_call" | custom-call | tf_op jit(solution)/shard_map/scores/pallas_call | solution.py:265
  29.6 0.0 collective-permute-start.10
  29.7 1.2 %collective-permute-done.10.other = f32[8,128]{1,0:T(8,128)S(1)} collective-permute-done((f32[8,128]{1,0:T(8,128)S(1)}, f32[8,128]{1,0:T(8,128)S(1)}, u32[]{:S(2)}, u32[]{:S(2)}) %collective-permute-start.10) | collective-permute-done | bytes 4128 | tf_op jit(solution)/shard_map/ppermute | solution.py:196
  30.8 0.6 %finish.1 = f32[2,4]{1,0:T(2,128)} custom-call(f32[8,128]{1,0:T(8,128)S(1)} %scores.1.mine, f32[8,128]{1,0:T(8,128)S(1)} %collective-permute-done.10.other), custom_call_target="tpu_custom_call" | custom-call | tf_op jit(solution)/shard_map/finish/pallas_call | solution.py:268
  (22 shorter events, 0.1 us)
Async XLA Ops:
  0.0 14.7 %slice-start = ((s8[12845056]{0:T(1024)(128)(4,1)}), s8[4194304]{0:T(1024)(128)(4,1)S(1)}, s32[]{:S(2)}) async-start(s8[12845056]{0:T(1024)(128)(4,1)} %bitcast.17), calls=%async_computation | async-start | bytes 8388608
  0.0 12.2 %copy-start = (bf16[1,160,7168]{2,1,0:T(8,128)(2,1)S(1)}, bf16[1,160,7168]{2,1,0:T(8,128)(2,1)}, u32[]{:S(2)}) copy-start(bf16[1,160,7168]{2,1,0:T(8,128)(2,1)} %param.12) | copy-start | bytes 6881284
  0.0 12.2 %copy-start.1 = (bf16[1,160,4096]{2,1,0:T(8,128)(2,1)S(1)}, bf16[1,160,4096]{2,1,0:T(8,128)(2,1)}, u32[]{:S(2)}) copy-start(bf16[1,160,4096]{2,1,0:T(8,128)(2,1)} %param.13) | copy-start | bytes 3932164
  0.0 12.2 %copy-start.3 = (f32[1,7168]{1,0:T(1,128)S(1)}, f32[1,7168]{1,0:T(1,128)}, u32[]{:S(2)}) copy-start(f32[1,7168]{1,0:T(1,128)} %refs_8_.1) | copy-start | bytes 86020
  0.0 12.2 %copy-start.4 = (f32[1,4096]{1,0:T(1,128)S(1)}, f32[1,4096]{1,0:T(1,128)}, u32[]{:S(2)}) copy-start(f32[1,4096]{1,0:T(1,128)} %refs_9_.1) | copy-start | bytes 49156
  0.0 12.2 %copy-start.5 = (s32[1,160]{1,0:T(1,128)S(1)}, s32[1,160]{1,0:T(1,128)}, u32[]{:S(2)}) copy-start(s32[1,160]{1,0:T(1,128)} %refs_5_.1) | copy-start | bytes 1924
  0.0 14.7 %slice-start.1 = ((s8[12845056]{0:T(1024)(128)(4,1)}), s8[4194304]{0:T(1024)(128)(4,1)S(1)}, s32[]{:S(2)}) async-start(s8[12845056]{0:T(1024)(128)(4,1)} %bitcast.17), calls=%async_computation.1 | async-start | bytes 8388608
  0.0 14.7 %slice-start.2 = ((s8[12845056]{0:T(1024)(128)(4,1)}), s8[4194304]{0:T(1024)(128)(4,1)S(1)}, s32[]{:S(2)}) async-start(s8[12845056]{0:T(1024)(128)(4,1)} %bitcast.17), calls=%async_computation.2 | async-start | bytes 8388608
  0.0 14.7 %slice-start.3 = ((s8[12845056]{0:T(1024)(128)(4,1)}), s8[262144]{0:T(1024)(128)(4,1)S(1)}, s32[]{:S(2)}) async-start(s8[12845056]{0:T(1024)(128)(4,1)} %bitcast.17), calls=%async_computation.3 | async-start | bytes 524288
  0.1 14.7 %copy-start.2 = (bf16[1,4096,512]{2,1,0:T(8,128)(2,1)S(1)}, bf16[1,4096,512]{2,1,0:T(8,128)(2,1)}, u32[]{:S(2)}) copy-start(bf16[1,4096,512]{2,1,0:T(8,128)(2,1)} %param.15) | copy-start | bytes 12582916
  1.0 5.6 %collective-permute-start.1 = (bf16[1,2,11264]{2,1,0:T(2,128)(2,1)S(1)}, bf16[1,2,11264]{2,1,0:T(2,128)(2,1)S(1)}, u32[]{:S(2)}, u32[]{:S(2)}) collective-permute-start(bf16[1,2,11264]{2,1,0:T(2,128)(2,1)S(1)} %bitcast.21), channel_id=1, source_target_pairs={{0,2},{2,0},{4,6},{6,4},{8,10},{10,8},{12,14},{14,12},{1,3},{3,1},... | collective-permute-start | bytes 135176 | tf_op jit(solution)/shard_map/ppermute | solution.py:53
  4.0 6.7 %collective-permute-start = (bf16[1,2,11264]{2,1,0:T(2,128)(2,1)S(1)}, bf16[1,2,11264]{2,1,0:T(2,128)(2,1)S(1)}, u32[]{:S(2)}, u32[]{:S(2)}) collective-permute-start(bf16[1,2,11264]{2,1,0:T(2,128)(2,1)S(1)} %bitcast.22), channel_id=1, source_target_pairs={{0,8},{2,10},{4,12},{6,14},{8,0},{10,2},{12,4},{14,6},{1,9},{3,11}... | collective-permute-start | bytes 135176 | tf_op jit(solution)/shard_map/ppermute | solution.py:53
  6.6 8.1 %collective-permute-start.2 = (bf16[2,2,11264]{2,1,0:T(2,128)(2,1)S(1)}, bf16[2,2,11264]{2,1,0:T(2,128)(2,1)S(1)}, u32[]{:S(2)}, u32[]{:S(2)}) collective-permute-start(bf16[2,2,11264]{2,1,0:T(2,128)(2,1)S(1)} %pair.1), channel_id=1, source_target_pairs={{0,4},{2,6},{4,0},{6,2},{8,12},{10,14},{12,8},{14,10},{1,5},{3,7},... | collective-permute-start | bytes 270344 | tf_op jit(solution)/shard_map/ppermute | solution.py:53
  8.3 6.5 %collective-permute-start.3 = (bf16[2,2,11264]{2,1,0:T(2,128)(2,1)S(1)}, bf16[2,2,11264]{2,1,0:T(2,128)(2,1)S(1)}, u32[]{:S(2)}, u32[]{:S(2)}) collective-permute-start(bf16[2,2,11264]{2,1,0:T(2,128)(2,1)S(1)} %pair.1), channel_id=1, source_target_pairs={{0,12},{2,14},{4,8},{6,10},{8,4},{10,6},{12,0},{14,2},{1,13},{3,15... | collective-permute-start | bytes 270344 | tf_op jit(solution)/shard_map/ppermute | solution.py:53
  10.7 4.0 %collective-permute-start.4 = (bf16[1,2,11264]{2,1,0:T(2,128)(2,1)S(1)}, bf16[1,2,11264]{2,1,0:T(2,128)(2,1)S(1)}, u32[]{:S(2)}, u32[]{:S(2)}) collective-permute-start(bf16[1,2,11264]{2,1,0:T(2,128)(2,1)S(1)} %collective-permute-done.refs_1_), channel_id=1, source_target_pairs={{0,2},{2,0},{4,6},{6,4},{8,10},{10,8},{12,14},{14,12},{1,3},{3,1},... | collective-permute-start | bytes 135176 | tf_op jit(solution)/shard_map/ppermute | solution.py:53
  14.8 10.5 %copy-start.6 = (s32[16]{0:T(128)S(1)}, s32[16]{0:T(128)}, u32[]{:S(2)}) copy-start(s32[16]{0:T(128)} %param.18) | copy-start | bytes 196
  17.2 4.1 %collective-permute-start.5 = (bf16[1,16,1408]{2,1,0:T(8,128)(2,1)S(1)}, bf16[1,16,1408]{2,1,0:T(8,128)(2,1)S(1)}, u32[]{:S(2)}, u32[]{:S(2)}) collective-permute-start(bf16[1,16,1408]{2,1,0:T(8,128)(2,1)S(1)} %rotate.1.refs_0_), channel_id=1, source_target_pairs={{0,2},{2,0},{4,6},{6,4},{8,10},{10,8},{12,14},{14,12},{1,3},{3,1},... | collective-permute-start | bytes 135176 | tf_op jit(solution)/shard_map/ppermute | solution.py:53
  18.7 6.0 %collective-permute-start.8 = (bf16[1,16,1408]{2,1,0:T(8,128)(2,1)S(1)}, bf16[1,16,1408]{2,1,0:T(8,128)(2,1)S(1)}, u32[]{:S(2)}, u32[]{:S(2)}) collective-permute-start(bf16[1,16,1408]{2,1,0:T(8,128)(2,1)S(1)} %rotate.1.refs_0_), channel_id=1, source_target_pairs={{0,8},{2,10},{4,12},{6,14},{8,0},{10,2},{12,4},{14,6},{1,9},{3,11}... | collective-permute-start | bytes 135176 | tf_op jit(solution)/shard_map/ppermute | solution.py:53
  21.2 7.4 %collective-permute-start.7 = (bf16[2,16,1408]{2,1,0:T(8,128)(2,1)S(1)}, bf16[2,16,1408]{2,1,0:T(8,128)(2,1)S(1)}, u32[]{:S(2)}, u32[]{:S(2)}) collective-permute-start(bf16[2,16,1408]{2,1,0:T(8,128)(2,1)S(1)} %pad_maximum_fusion), channel_id=1, source_target_pairs={{0,12},{2,14},{4,8},{6,10},{8,4},{10,6},{12,0},{14,2},{1,13},{3,15... | collective-permute-start | bytes 270344 | tf_op jit(solution)/shard_map/ppermute | solution.py:53
  23.8 5.4 %collective-permute-start.6 = (bf16[2,16,1408]{2,1,0:T(8,128)(2,1)S(1)}, bf16[2,16,1408]{2,1,0:T(8,128)(2,1)S(1)}, u32[]{:S(2)}, u32[]{:S(2)}) collective-permute-start(bf16[2,16,1408]{2,1,0:T(8,128)(2,1)S(1)} %pad_maximum_fusion), channel_id=1, source_target_pairs={{0,4},{2,6},{4,0},{6,2},{8,12},{10,14},{12,8},{14,10},{1,5},{3,7},... | collective-permute-start | bytes 270344 | tf_op jit(solution)/shard_map/ppermute | solution.py:53
  24.6 4.0 %collective-permute-start.9 = (bf16[1,16,1408]{2,1,0:T(8,128)(2,1)S(1)}, bf16[1,16,1408]{2,1,0:T(8,128)(2,1)S(1)}, u32[]{:S(2)}, u32[]{:S(2)}) collective-permute-start(bf16[1,16,1408]{2,1,0:T(8,128)(2,1)S(1)} %collective-permute-done.8.refs_1_), channel_id=1, source_target_pairs={{0,2},{2,0},{4,6},{6,4},{8,10},{10,8},{12,14},{14,12},{1,3},{3,1},... | collective-permute-start | bytes 135176 | tf_op jit(solution)/shard_map/ppermute | solution.py:53
  29.6 1.2 %collective-permute-start.10 = (f32[8,128]{1,0:T(8,128)S(1)}, f32[8,128]{1,0:T(8,128)S(1)}, u32[]{:S(2)}, u32[]{:S(2)}) collective-permute-start(f32[8,128]{1,0:T(8,128)S(1)} %scores.1.mine), channel_id=1, source_target_pairs={{0,1},{1,0},{2,3},{3,2},{4,5},{5,4},{6,7},{7,6},{8,9},{9,8},{10,11... | collective-permute-start | bytes 12296 | tf_op jit(solution)/shard_map/ppermute | solution.py:196

commit v8 on v5

--- a/solution.py
+++ b/solution.py
@@ -70,16 +70,8 @@
     return jnp.concatenate(parts, axis=0)[table[device]]
 
 
-def join_kernel(hidden, inputs, out, sems):
-    width_h = hidden.shape[1]
-    copies = [
-        pltpu.make_async_copy(hidden, out.at[:, :width_h], sems.at[0]),
-        pltpu.make_async_copy(inputs, out.at[:, width_h:], sems.at[1]),
-    ]
-    for copy in copies:
-        copy.start()
-    for copy in copies:
-        copy.wait()
+def hand_on_kernel(block, out):
+    out[...] = block[...]
 
 
 def self_kernel(train_h, train_i, eig_h, eig_i, ids, out):
@@ -228,15 +220,13 @@
     own_tokens = query_inputs.shape[1]
     width = query_out_grads.shape[2] + query_inputs.shape[2]
     tokens = own_tokens * shards
+    own = jnp.concatenate([query_out_grads[0], query_inputs[0]], axis=1)
     own = call(
-        join_kernel,
-        "join",
-        pltpu.VMEM((own_tokens, width), jnp.bfloat16),
-        flops=20_000_000_000,
-        in_specs=[pl.BlockSpec(memory_space=pl.ANY)] * 2,
-        out_specs=pl.BlockSpec(memory_space=pltpu.VMEM),
-        scratch_shapes=[pltpu.SemaphoreType.DMA((2,))],
-    )(hbm(query_out_grads[0]), hbm(query_inputs[0]))
+        hand_on_kernel,
+        "hand_on",
+        jax.ShapeDtypeStruct((own_tokens, width), jnp.bfloat16),
+        flops=8_000_000_000,
+    )(own)
     everyone, masks = gather(own, shards, by_kernel=True)
     small = jax.ShapeDtypeStruct((8, LANES), jnp.float32)
     own_self = call(

time: 31.3 us -> 31.3 us (level)
  other arithmetic: 0.01 us -> 0.97 us
  Pallas kernels: 6.74 us -> 5.82 us
    concatenate x0 -> x1, other arithmetic: none -> 0.96 us  [body(): own = jnp.concatenate([query_out_grads[0], query_inputs[0]], axis=1)]
    pallas_call x1, Pallas kernels: 0.92 us -> 0.01 us  [body(): call(hand_on_kernel, 'hand_on', jax.ShapeDtypeStruct((own_tokens, width),...]
where the time goes in v8:
time: 31.3 us; the launch traced here: 31.2 us
  starting transfers between devices  17.4 us (56%)
  waiting for transfers between devices  6.7 us (21%)
  Pallas kernels  5.82 us (19%)
  other arithmetic  0.97 us (3%)
    ppermute x10, starting transfers between devices, gather(): lax.ppermute(joined[sent], 'ex', [(i, i ^ mask) for i in range(shards)])  17.4 us
    ppermute x10, waiting for transfers between devices, gather(): lax.ppermute(joined[sent], 'ex', [(i, i ^ mask) for i in range(shards)])  5.54 us
    pallas_call x1, Pallas kernels, body(): call(functools.partial(rotate_kernel, masks), 'rotate', jax.ShapeDtypeStr...  2.35 us
    pallas_call x1, Pallas kernels, body(): call(self_kernel, 'self_influence', small, flops=2 * 160 * 160 * 11264, m...  1.41 us
    ppermute x1, waiting for transfers between devices, layer_swap(): return lax.ppermute(x, 'layer', [(0, 1), (1, 0)])  1.16 us
    concatenate x1, other arithmetic, body(): own = jnp.concatenate([query_out_grads[0], query_inputs[0]], axis=1)  0.96 us
    pallas_call x1, Pallas kernels, body(): call(finish_kernel, 'finish', jax.ShapeDtypeStruct((E_DEV, QUERIES // 2),...  0.65 us
  transfers between devices with their start and end apart: 11, of which 6 were waited for; matrix products, arithmetic and copies ran while one was open for 0% of the time, Pallas kernels for 7%

profile of v8, /device:TPU:0, one launch (start us, length us, event | category | flops | bytes accessed | tf_op | source)
XLA Modules:
  0.0 31.2 jit_solution(11838947794002735392)
XLA Ops:
  0.0 1.0 %pad_maximum_fusion.1.block = bf16[2,11264]{1,0:T(2,128)(2,1)S(1)} fusion(bf16[2,4096]{1,0:T(2,128)(2,1)} %bitcast.27, bf16[2,7168]{1,0:T(2,128)(2,1)} %bitcast.26), kind=kLoop, calls=%fused_computation.1 | loop fusion | flops 90112 | bytes 90112 | tf_op jit(solution)/shard_map/concatenate | solution.py:223
  1.0 0.0 copy-start
  1.0 0.0 copy-start.1
  1.0 0.0 copy-start.3
  1.0 0.0 copy-start.4
  1.0 0.0 copy-start.5
  1.0 0.0 slice-start.1
  1.0 0.0 slice-start.2
  1.1 0.0 copy-start.2
  1.1 3.0 %collective-permute-start.1 = (bf16[1,2,11264]{2,1,0:T(2,128)(2,1)S(1)}, bf16[1,2,11264]{2,1,0:T(2,128)(2,1)S(1)}, u32[]{:S(2)}, u32[]{:S(2)}) collective-permute-start(bf16[1,2,11264]{2,1,0:T(2,128)(2,1)S(1)} %bitcast.21), channel_id=1, source_target_pairs={{0,2},{2,0},{4,6},{6,4},{8,10},{10,8},{12,14},{14,12},{1,3},{3,1},... | collective-permute-start | bytes 135176 | tf_op jit(solution)/shard_map/ppermute | solution.py:53
  4.1 2.6 %collective-permute-start = (bf16[1,2,11264]{2,1,0:T(2,128)(2,1)S(1)}, bf16[1,2,11264]{2,1,0:T(2,128)(2,1)S(1)}, u32[]{:S(2)}, u32[]{:S(2)}) collective-permute-start(bf16[1,2,11264]{2,1,0:T(2,128)(2,1)S(1)} %bitcast.22), channel_id=1, source_target_pairs={{0,8},{2,10},{4,12},{6,14},{8,0},{10,2},{12,4},{14,6},{1,9},{3,11}... | collective-permute-start | bytes 135176 | tf_op jit(solution)/shard_map/ppermute | solution.py:53
  6.7 1.6 %collective-permute-start.2 = (bf16[2,2,11264]{2,1,0:T(2,128)(2,1)S(1)}, bf16[2,2,11264]{2,1,0:T(2,128)(2,1)S(1)}, u32[]{:S(2)}, u32[]{:S(2)}) collective-permute-start(bf16[2,2,11264]{2,1,0:T(2,128)(2,1)S(1)} %pair.1), channel_id=1, source_target_pairs={{0,4},{2,6},{4,0},{6,2},{8,12},{10,14},{12,8},{14,10},{1,5},{3,7},... | collective-permute-start | bytes 270344 | tf_op jit(solution)/shard_map/ppermute | solution.py:53
  8.3 2.4 %collective-permute-start.3 = (bf16[2,2,11264]{2,1,0:T(2,128)(2,1)S(1)}, bf16[2,2,11264]{2,1,0:T(2,128)(2,1)S(1)}, u32[]{:S(2)}, u32[]{:S(2)}) collective-permute-start(bf16[2,2,11264]{2,1,0:T(2,128)(2,1)S(1)} %pair.1), channel_id=1, source_target_pairs={{0,12},{2,14},{4,8},{6,10},{8,4},{10,6},{12,0},{14,2},{1,13},{3,15... | collective-permute-start | bytes 270344 | tf_op jit(solution)/shard_map/ppermute | solution.py:53
  10.8 1.5 %collective-permute-start.4 = (bf16[1,2,11264]{2,1,0:T(2,128)(2,1)S(1)}, bf16[1,2,11264]{2,1,0:T(2,128)(2,1)S(1)}, u32[]{:S(2)}, u32[]{:S(2)}) collective-permute-start(bf16[1,2,11264]{2,1,0:T(2,128)(2,1)S(1)} %collective-permute-done.refs_1_), channel_id=1, source_target_pairs={{0,2},{2,0},{4,6},{6,4},{8,10},{10,8},{12,14},{14,12},{1,3},{3,1},... | collective-permute-start | bytes 135176 | tf_op jit(solution)/shard_map/ppermute | solution.py:53
  12.3 1.4 %self_influence.1.refs_10_.refs_7_ = f32[8,128]{1,0:T(8,128)S(1)} custom-call(bf16[160,7168]{1,0:T(8,128)(2,1)S(1)} %bitcast.9, bf16[160,4096]{1,0:T(8,128)(2,1)S(1)} %bitcast.13, f32[1,7168]{1,0:T(1,128)S(1)} %copy-done.3, f32[1,4096]{1,0:T(1,128)S(1)} %copy-done.4, s32[1,160]{1,0:T(1,128)S(1)} %copy-done.5), custom_call_target="tpu_custom_call" | custom-call | flops 576716800 | bytes 3700000 | tf_op jit(solution)/shard_map/self_influence/pallas_call | solution.py:232
  13.7 1.1 %collective-permute-done.4.refs_5_ = bf16[1,2,11264]{2,1,0:T(2,128)(2,1)S(1)} collective-permute-done((bf16[1,2,11264]{2,1,0:T(2,128)(2,1)S(1)}, bf16[1,2,11264]{2,1,0:T(2,128)(2,1)S(1)}, u32[]{:S(2)}, u32[]{:S(2)}) %collective-permute-start.4) | collective-permute-done | bytes 45088 | tf_op jit(solution)/shard_map/ppermute | solution.py:53
  14.9 0.0 copy-start.6
  14.9 2.4 %rotate.1.refs_0_ = bf16[1,16,1408]{2,1,0:T(8,128)(2,1)S(1)} custom-call(bf16[1,2,11264]{2,1,0:T(2,128)(2,1)S(1)} %bitcast.24, bf16[1,2,11264]{2,1,0:T(2,128)(2,1)S(1)} %collective-permute-done.refs_1_, bf16[1,2,11264]{2,1,0:T(2,128)(2,1)S(1)} %collective-permute-done.1.second.refs_2_, bf16[2,2,11264]{2,1,0:T(2,128)(2,1)S(1)} %collective-permute-done.2.refs_3_, ...), custom_call_target="tpu_custom_call" | custom-call | flops 272000000 | bytes 17000000 | tf_op jit(solution)/shard_map/rotate/pallas_call | solution.py:235
  17.2 1.5 %collective-permute-start.5 = (bf16[1,16,1408]{2,1,0:T(8,128)(2,1)S(1)}, bf16[1,16,1408]{2,1,0:T(8,128)(2,1)S(1)}, u32[]{:S(2)}, u32[]{:S(2)}) collective-permute-start(bf16[1,16,1408]{2,1,0:T(8,128)(2,1)S(1)} %rotate.1.refs_0_), channel_id=1, source_target_pairs={{0,2},{2,0},{4,6},{6,4},{8,10},{10,8},{12,14},{14,12},{1,3},{3,1},... | collective-permute-start | bytes 135176 | tf_op jit(solution)/shard_map/ppermute | solution.py:53
  18.7 1.6 %collective-permute-start.7 = (bf16[1,16,1408]{2,1,0:T(8,128)(2,1)S(1)}, bf16[1,16,1408]{2,1,0:T(8,128)(2,1)S(1)}, u32[]{:S(2)}, u32[]{:S(2)}) collective-permute-start(bf16[1,16,1408]{2,1,0:T(8,128)(2,1)S(1)} %rotate.1.refs_0_), channel_id=1, source_target_pairs={{0,8},{2,10},{4,12},{6,14},{8,0},{10,2},{12,4},{14,6},{1,9},{3,11}... | collective-permute-start | bytes 135176 | tf_op jit(solution)/shard_map/ppermute | solution.py:53
  20.3 1.0 %collective-permute-done.5.refs_2_ = bf16[1,16,1408]{2,1,0:T(8,128)(2,1)S(1)} collective-permute-done((bf16[1,16,1408]{2,1,0:T(8,128)(2,1)S(1)}, bf16[1,16,1408]{2,1,0:T(8,128)(2,1)S(1)}, u32[]{:S(2)}, u32[]{:S(2)}) %collective-permute-start.5) | collective-permute-done | bytes 45088 | tf_op jit(solution)/shard_map/ppermute | solution.py:53
  21.3 2.5 %collective-permute-start.9 = (bf16[2,16,1408]{2,1,0:T(8,128)(2,1)S(1)}, bf16[2,16,1408]{2,1,0:T(8,128)(2,1)S(1)}, u32[]{:S(2)}, u32[]{:S(2)}) collective-permute-start(bf16[2,16,1408]{2,1,0:T(8,128)(2,1)S(1)} %pad_maximum_fusion), channel_id=1, source_target_pairs={{0,12},{2,14},{4,8},{6,10},{8,4},{10,6},{12,0},{14,2},{1,13},{3,15... | collective-permute-start | bytes 270344 | tf_op jit(solution)/shard_map/ppermute | solution.py:53
  23.8 0.9 %collective-permute-done.7.refs_1_ = bf16[1,16,1408]{2,1,0:T(8,128)(2,1)S(1)} collective-permute-done((bf16[1,16,1408]{2,1,0:T(8,128)(2,1)S(1)}, bf16[1,16,1408]{2,1,0:T(8,128)(2,1)S(1)}, u32[]{:S(2)}, u32[]{:S(2)}) %collective-permute-start.7) | collective-permute-done | bytes 45088 | tf_op jit(solution)/shard_map/ppermute | solution.py:53
  24.7 0.7 %collective-permute-start.8 = (bf16[1,16,1408]{2,1,0:T(8,128)(2,1)S(1)}, bf16[1,16,1408]{2,1,0:T(8,128)(2,1)S(1)}, u32[]{:S(2)}, u32[]{:S(2)}) collective-permute-start(bf16[1,16,1408]{2,1,0:T(8,128)(2,1)S(1)} %collective-permute-done.7.refs_1_), channel_id=1, source_target_pairs={{0,2},{2,0},{4,6},{6,4},{8,10},{10,8},{12,14},{14,12},{1,3},{3,1},... | collective-permute-start | bytes 135176 | tf_op jit(solution)/shard_map/ppermute | solution.py:53
  25.4 0.5 %early_grams.1 = (f32[2,16,160]{2,1,0:T(8,128)S(1)}, f32[16,128]{1,0:T(8,128)S(1)}) custom-call(bf16[1,16,1408]{2,1,0:T(8,128)(2,1)S(1)} %rotate.1.refs_0_, bf16[1,16,1408]{2,1,0:T(8,128)(2,1)S(1)} %collective-permute-done.7.refs_1_, bf16[1,16,1408]{2,1,0:T(8,128)(2,1)S(1)} %collective-permute-done.5.refs_2_, bf16[160,7168]{1,0:T(8,128)(2,1)S(1)} %bitcast.10, ...), custom_call_target="tpu_custom_call" | custom-call | flops 500000000 | tf_op jit(solution)/shard_map/early_grams/pallas_call | solution.py:246
  25.9 1.9 %collective-permute-done.9.refs_0_ = bf16[2,16,1408]{2,1,0:T(8,128)(2,1)S(1)} collective-permute-done((bf16[2,16,1408]{2,1,0:T(8,128)(2,1)S(1)}, bf16[2,16,1408]{2,1,0:T(8,128)(2,1)S(1)}, u32[]{:S(2)}, u32[]{:S(2)}) %collective-permute-start.9) | collective-permute-done | bytes 90144 | tf_op jit(solution)/shard_map/ppermute | solution.py:53
  27.7 0.3 %more_grams.1.refs_4_ = f32[2,16,160]{2,1,0:T(8,128)S(1)} custom-call(bf16[2,16,1408]{2,1,0:T(8,128)(2,1)S(1)} %collective-permute-done.9.refs_0_, bf16[160,7168]{1,0:T(8,128)(2,1)S(1)} %bitcast.11, bf16[160,4096]{1,0:T(8,128)(2,1)S(1)} %bitcast.15, f32[2,16,160]{2,1,0:T(8,128)S(1)} %get-tuple-element.7.refs_3_), custom_call_target="tpu_custom_call" | custom-call | flops 300000000 | tf_op jit(solution)/shard_map/more_grams/pallas_call | solution.py:252
  28.1 0.7 %collective-permute-done.8.refs_1_ = bf16[1,16,1408]{2,1,0:T(8,128)(2,1)S(1)} collective-permute-done((bf16[1,16,1408]{2,1,0:T(8,128)(2,1)S(1)}, bf16[1,16,1408]{2,1,0:T(8,128)(2,1)S(1)}, u32[]{:S(2)}, u32[]{:S(2)}) %collective-permute-start.8) | collective-permute-done | bytes 45088 | tf_op jit(solution)/shard_map/ppermute | solution.py:53
  28.8 0.6 %scores.1.mine = f32[8,128]{1,0:T(8,128)S(1)} custom-call(bf16[2,16,1408]{2,1,0:T(8,128)(2,1)S(1)} %collective-permute-done.6.refs_0_, bf16[1,16,1408]{2,1,0:T(8,128)(2,1)S(1)} %collective-permute-done.8.refs_1_, bf16[160,7168]{1,0:T(8,128)(2,1)S(1)} %bitcast.12, bf16[160,4096]{1,0:T(8,128)(2,1)S(1)} %bitcast.16, f32[2,16,160]{2,1,0:T(8,128)S(1)} %more_grams.1.refs_4_, ...), custom_call_target="tpu_custom_call" | custom-call | tf_op jit(solution)/shard_map/scores/pallas_call | solution.py:255
  29.3 0.0 collective-permute-start.10
  29.4 1.2 %collective-permute-done.10.other = f32[8,128]{1,0:T(8,128)S(1)} collective-permute-done((f32[8,128]{1,0:T(8,128)S(1)}, f32[8,128]{1,0:T(8,128)S(1)}, u32[]{:S(2)}, u32[]{:S(2)}) %collective-permute-start.10) | collective-permute-done | bytes 4128 | tf_op jit(solution)/shard_map/ppermute | solution.py:188
  30.5 0.6 %finish.1 = f32[2,4]{1,0:T(2,128)} custom-call(f32[8,128]{1,0:T(8,128)S(1)} %scores.1.mine, f32[8,128]{1,0:T(8,128)S(1)} %collective-permute-done.10.other), custom_call_target="tpu_custom_call" | custom-call | tf_op jit(solution)/shard_map/finish/pallas_call | solution.py:258
  (23 shorter events, 0.1 us)
Async XLA Ops:
  0.0 14.8 %slice-start = ((s8[12845056]{0:T(1024)(128)(4,1)}), s8[4194304]{0:T(1024)(128)(4,1)S(1)}, s32[]{:S(2)}) async-start(s8[12845056]{0:T(1024)(128)(4,1)} %bitcast.17), calls=%async_computation | async-start | bytes 8388608
  1.0 11.3 %copy-start = (bf16[1,160,7168]{2,1,0:T(8,128)(2,1)S(1)}, bf16[1,160,7168]{2,1,0:T(8,128)(2,1)}, u32[]{:S(2)}) copy-start(bf16[1,160,7168]{2,1,0:T(8,128)(2,1)} %param.12) | copy-start | bytes 6881284
  1.0 11.3 %copy-start.1 = (bf16[1,160,4096]{2,1,0:T(8,128)(2,1)S(1)}, bf16[1,160,4096]{2,1,0:T(8,128)(2,1)}, u32[]{:S(2)}) copy-start(bf16[1,160,4096]{2,1,0:T(8,128)(2,1)} %param.13) | copy-start | bytes 3932164
  1.0 11.3 %copy-start.3 = (f32[1,7168]{1,0:T(1,128)S(1)}, f32[1,7168]{1,0:T(1,128)}, u32[]{:S(2)}) copy-start(f32[1,7168]{1,0:T(1,128)} %refs_8_.1) | copy-start | bytes 86020
  1.0 11.3 %copy-start.4 = (f32[1,4096]{1,0:T(1,128)S(1)}, f32[1,4096]{1,0:T(1,128)}, u32[]{:S(2)}) copy-start(f32[1,4096]{1,0:T(1,128)} %refs_9_.1) | copy-start | bytes 49156
  1.0 11.3 %copy-start.5 = (s32[1,160]{1,0:T(1,128)S(1)}, s32[1,160]{1,0:T(1,128)}, u32[]{:S(2)}) copy-start(s32[1,160]{1,0:T(1,128)} %refs_6_.1) | copy-start | bytes 1924
  1.0 13.8 %slice-start.1 = ((s8[12845056]{0:T(1024)(128)(4,1)}), s8[4194304]{0:T(1024)(128)(4,1)S(1)}, s32[]{:S(2)}) async-start(s8[12845056]{0:T(1024)(128)(4,1)} %bitcast.17), calls=%async_computation.1 | async-start | bytes 8388608
  1.0 13.8 %slice-start.2 = ((s8[12845056]{0:T(1024)(128)(4,1)}), s8[4194304]{0:T(1024)(128)(4,1)S(1)}, s32[]{:S(2)}) async-start(s8[12845056]{0:T(1024)(128)(4,1)} %bitcast.17), calls=%async_computation.2 | async-start | bytes 8388608
  1.0 13.8 %slice-start.3 = ((s8[12845056]{0:T(1024)(128)(4,1)}), s8[262144]{0:T(1024)(128)(4,1)S(1)}, s32[]{:S(2)}) async-start(s8[12845056]{0:T(1024)(128)(4,1)} %bitcast.17), calls=%async_computation.3 | async-start | bytes 524288
  1.1 13.8 %copy-start.2 = (bf16[1,4096,512]{2,1,0:T(8,128)(2,1)S(1)}, bf16[1,4096,512]{2,1,0:T(8,128)(2,1)}, u32[]{:S(2)}) copy-start(bf16[1,4096,512]{2,1,0:T(8,128)(2,1)} %param.15) | copy-start | bytes 12582916
  1.1 5.6 %collective-permute-start.1 = (bf16[1,2,11264]{2,1,0:T(2,128)(2,1)S(1)}, bf16[1,2,11264]{2,1,0:T(2,128)(2,1)S(1)}, u32[]{:S(2)}, u32[]{:S(2)}) collective-permute-start(bf16[1,2,11264]{2,1,0:T(2,128)(2,1)S(1)} %bitcast.21), channel_id=1, source_target_pairs={{0,2},{2,0},{4,6},{6,4},{8,10},{10,8},{12,14},{14,12},{1,3},{3,1},... | collective-permute-start | bytes 135176 | tf_op jit(solution)/shard_map/ppermute | solution.py:53
  4.1 6.7 %collective-permute-start = (bf16[1,2,11264]{2,1,0:T(2,128)(2,1)S(1)}, bf16[1,2,11264]{2,1,0:T(2,128)(2,1)S(1)}, u32[]{:S(2)}, u32[]{:S(2)}) collective-permute-start(bf16[1,2,11264]{2,1,0:T(2,128)(2,1)S(1)} %bitcast.22), channel_id=1, source_target_pairs={{0,8},{2,10},{4,12},{6,14},{8,0},{10,2},{12,4},{14,6},{1,9},{3,11}... | collective-permute-start | bytes 135176 | tf_op jit(solution)/shard_map/ppermute | solution.py:53
  6.7 8.1 %collective-permute-start.2 = (bf16[2,2,11264]{2,1,0:T(2,128)(2,1)S(1)}, bf16[2,2,11264]{2,1,0:T(2,128)(2,1)S(1)}, u32[]{:S(2)}, u32[]{:S(2)}) collective-permute-start(bf16[2,2,11264]{2,1,0:T(2,128)(2,1)S(1)} %pair.1), channel_id=1, source_target_pairs={{0,4},{2,6},{4,0},{6,2},{8,12},{10,14},{12,8},{14,10},{1,5},{3,7},... | collective-permute-start | bytes 270344 | tf_op jit(solution)/shard_map/ppermute | solution.py:53
  8.3 6.5 %collective-permute-start.3 = (bf16[2,2,11264]{2,1,0:T(2,128)(2,1)S(1)}, bf16[2,2,11264]{2,1,0:T(2,128)(2,1)S(1)}, u32[]{:S(2)}, u32[]{:S(2)}) collective-permute-start(bf16[2,2,11264]{2,1,0:T(2,128)(2,1)S(1)} %pair.1), channel_id=1, source_target_pairs={{0,12},{2,14},{4,8},{6,10},{8,4},{10,6},{12,0},{14,2},{1,13},{3,15... | collective-permute-start | bytes 270344 | tf_op jit(solution)/shard_map/ppermute | solution.py:53
  10.8 4.0 %collective-permute-start.4 = (bf16[1,2,11264]{2,1,0:T(2,128)(2,1)S(1)}, bf16[1,2,11264]{2,1,0:T(2,128)(2,1)S(1)}, u32[]{:S(2)}, u32[]{:S(2)}) collective-permute-start(bf16[1,2,11264]{2,1,0:T(2,128)(2,1)S(1)} %collective-permute-done.refs_1_), channel_id=1, source_target_pairs={{0,2},{2,0},{4,6},{6,4},{8,10},{10,8},{12,14},{14,12},{1,3},{3,1},... | collective-permute-start | bytes 135176 | tf_op jit(solution)/shard_map/ppermute | solution.py:53
  14.9 10.5 %copy-start.6 = (s32[16]{0:T(128)S(1)}, s32[16]{0:T(128)}, u32[]{:S(2)}) copy-start(s32[16]{0:T(128)} %param.18) | copy-start | bytes 196
  17.2 4.1 %collective-permute-start.5 = (bf16[1,16,1408]{2,1,0:T(8,128)(2,1)S(1)}, bf16[1,16,1408]{2,1,0:T(8,128)(2,1)S(1)}, u32[]{:S(2)}, u32[]{:S(2)}) collective-permute-start(bf16[1,16,1408]{2,1,0:T(8,128)(2,1)S(1)} %rotate.1.refs_0_), channel_id=1, source_target_pairs={{0,2},{2,0},{4,6},{6,4},{8,10},{10,8},{12,14},{14,12},{1,3},{3,1},... | collective-permute-start | bytes 135176 | tf_op jit(solution)/shard_map/ppermute | solution.py:53
  18.7 6.0 %collective-permute-start.7 = (bf16[1,16,1408]{2,1,0:T(8,128)(2,1)S(1)}, bf16[1,16,1408]{2,1,0:T(8,128)(2,1)S(1)}, u32[]{:S(2)}, u32[]{:S(2)}) collective-permute-start(bf16[1,16,1408]{2,1,0:T(8,128)(2,1)S(1)} %rotate.1.refs_0_), channel_id=1, source_target_pairs={{0,8},{2,10},{4,12},{6,14},{8,0},{10,2},{12,4},{14,6},{1,9},{3,11}... | collective-permute-start | bytes 135176 | tf_op jit(solution)/shard_map/ppermute | solution.py:53
  21.3 6.4 %collective-permute-start.9 = (bf16[2,16,1408]{2,1,0:T(8,128)(2,1)S(1)}, bf16[2,16,1408]{2,1,0:T(8,128)(2,1)S(1)}, u32[]{:S(2)}, u32[]{:S(2)}) collective-permute-start(bf16[2,16,1408]{2,1,0:T(8,128)(2,1)S(1)} %pad_maximum_fusion), channel_id=1, source_target_pairs={{0,12},{2,14},{4,8},{6,10},{8,4},{10,6},{12,0},{14,2},{1,13},{3,15... | collective-permute-start | bytes 270344 | tf_op jit(solution)/shard_map/ppermute | solution.py:53
  23.8 4.9 %collective-permute-start.6 = (bf16[2,16,1408]{2,1,0:T(8,128)(2,1)S(1)}, bf16[2,16,1408]{2,1,0:T(8,128)(2,1)S(1)}, u32[]{:S(2)}, u32[]{:S(2)}) collective-permute-start(bf16[2,16,1408]{2,1,0:T(8,128)(2,1)S(1)} %pad_maximum_fusion), channel_id=1, source_target_pairs={{0,4},{2,6},{4,0},{6,2},{8,12},{10,14},{12,8},{14,10},{1,5},{3,7},... | collective-permute-start | bytes 270344 | tf_op jit(solution)/shard_map/ppermute | solution.py:53
  24.7 4.0 %collective-permute-start.8 = (bf16[1,16,1408]{2,1,0:T(8,128)(2,1)S(1)}, bf16[1,16,1408]{2,1,0:T(8,128)(2,1)S(1)}, u32[]{:S(2)}, u32[]{:S(2)}) collective-permute-start(bf16[1,16,1408]{2,1,0:T(8,128)(2,1)S(1)} %collective-permute-done.7.refs_1_), channel_id=1, source_target_pairs={{0,2},{2,0},{4,6},{6,4},{8,10},{10,8},{12,14},{14,12},{1,3},{3,1},... | collective-permute-start | bytes 135176 | tf_op jit(solution)/shard_map/ppermute | solution.py:53
  29.3 1.2 %collective-permute-start.10 = (f32[8,128]{1,0:T(8,128)S(1)}, f32[8,128]{1,0:T(8,128)S(1)}, u32[]{:S(2)}, u32[]{:S(2)}) collective-permute-start(f32[8,128]{1,0:T(8,128)S(1)} %scores.1.mine), channel_id=1, source_target_pairs={{0,1},{1,0},{2,3},{3,2},{4,5},{5,4},{6,7},{7,6},{8,9},{9,8},{10,11... | collective-permute-start | bytes 12296 | tf_op jit(solution)/shard_map/ppermute | solution.py:188
